TPU v7x, 32 devices: a whole 2x2x4 slice. The times are simulated.
32 devices in a mesh: fsdp: 8 (over y, x, core), dp: 4 (over z).
Axes of the slice: x: 2, y: 2, z: 4, core: 2. Of those that a mesh axis runs over, the one named last changes fastest.
Arguments:
- candidate_layer_inputs: bfloat16 [128, 32, 8192], P(('dp', 'fsdp')), parts along dimension 0, may hold values from -8 to 8
- candidate_loss_cotangent: bfloat16 [128, 32, 1024], P(('dp', 'fsdp')), parts along dimension 0, may hold values from -8 to 8
- candidate_live_lengths: int32 [128], P(('dp', 'fsdp')), parts along dimension 0, may hold values from 4 to 32, as said below
- probe_layer_inputs: bfloat16 [128, 32, 8192], P(('dp', 'fsdp')), parts along dimension 0, may hold values from -8 to 8
- probe_loss_cotangent: bfloat16 [128, 32, 1024], P(('dp', 'fsdp')), parts along dimension 0, may hold values from -8 to 8
- probe_live_lengths: int32 [128], P(('dp', 'fsdp')), parts along dimension 0, may hold values from 4 to 32, as said below
- adapter_down_matrix: bfloat16 [8192, 128], P('fsdp'), may hold values from -0.0625 to 0.0625
- adapter_up_matrix: bfloat16 [1024, 128], P('fsdp'), may hold values from -0.5 to 0.5
- input_side_sketch: bfloat16 [8192, 256], P('fsdp'), may hold values from -0.0625 to 0.0625
- output_side_sketch: bfloat16 [1024, 256], P('fsdp'), may hold values from -0.1875 to 0.1875
- rank_sketch_down: bfloat16 [128, 16], replicated, may hold values from -0.5 to 0.5
- rank_sketch_up: bfloat16 [128, 16], replicated, may hold values from -0.5 to 0.5
Outputs:
- scores: float32 [128, 32], P(('dp', 'fsdp')), parts along dimension 0
- features: bfloat16 [128, 8192], P(('dp', 'fsdp')), parts along dimension 0
There are 4 independent parts, one for each index of `dp`. A program takes and returns all parts, laid end to end along the dimension named above; an argument that names none is the same for every part. Nothing has to cross between parts.
Inputs may be any that keep to these rules, and one draw needn't show every extreme that they name: `candidate_live_lengths`: the live positions of an example are its first that many; some example has exactly 32 live positions and some exactly 4. `probe_live_lengths`: the live positions of an example are its first that many; some example has exactly 32 live positions and some exactly 4.
All inputs are finite; a program needn't handle non-finite values.
Results may differ from a plain program's by a relative error of at most 0.0056.
Values may be sent and summed in bfloat16 or wider, within the bound.
No kernel may reach another device: no remote copies, remote signals or barrier semaphores. Data moves between devices by JAX's collectives and lax.ppermute only.
A program may use at most 64 MiB of HBM per device.

v0:
```python
import jax
import jax.numpy as jnp
from jax import lax
from jax.sharding import PartitionSpec as P

eps_mean = 1e-06


def live_cotangent(loss_cotangent, example_lengths):
    positions = lax.broadcasted_iota(jnp.int32, loss_cotangent.shape[:2], 1)
    live_mask = (positions < example_lengths[:, None]).astype(loss_cotangent.dtype)
    return loss_cotangent * live_mask[:, :, None]


def compute_sketch_features(
    down_total_acc,
    inward_total_acc,
    loss_cotangent,
    example_lengths,
    up_full,
    outward_full,
    rank_sketch_down,
    rank_sketch_up,
):
    examples = loss_cotangent.shape[0]
    seq_len = loss_cotangent.shape[1]
    kv_width = loss_cotangent.shape[2]
    masked_values = live_cotangent(loss_cotangent, example_lengths).reshape(
        examples * seq_len, kv_width
    )
    gradient_rowset = jnp.dot(masked_values, up_full, preferred_element_type=jnp.float32).astype(
        jnp.bfloat16
    )
    outward = jnp.dot(masked_values, outward_full, preferred_element_type=jnp.float32).astype(
        jnp.bfloat16
    )
    down_round = down_total_acc.astype(jnp.bfloat16)
    inward_round = inward_total_acc.astype(jnp.bfloat16)
    left_small = jnp.dot(
        gradient_rowset, rank_sketch_down, preferred_element_type=jnp.float32
    ).astype(jnp.bfloat16)
    right_small = jnp.dot(down_round, rank_sketch_up, preferred_element_type=jnp.float32).astype(
        jnp.bfloat16
    )
    small_cols = rank_sketch_down.shape[1]
    large_cols = inward_round.shape[1]
    grad_left = jnp.einsum(
        "esk,esp->ekp",
        left_small.reshape(examples, seq_len, small_cols),
        inward_round.reshape(examples, seq_len, large_cols),
        preferred_element_type=jnp.float32,
    )
    grad_right = jnp.einsum(
        "esk,esp->ekp",
        right_small.reshape(examples, seq_len, small_cols),
        outward.reshape(examples, seq_len, large_cols),
        preferred_element_type=jnp.float32,
    )
    joined = jnp.concatenate([grad_left, grad_right], axis=1).reshape(
        examples, 2 * small_cols * large_cols
    )
    inv_rms = lax.rsqrt(jnp.mean(joined * joined, axis=1, keepdims=True) + eps_mean)
    return (joined * inv_rms).astype(jnp.bfloat16)


def body(
    candidate_layer_inputs,
    candidate_loss_cotangent,
    candidate_live_lengths,
    probe_layer_inputs,
    probe_loss_cotangent,
    probe_live_lengths,
    adapter_down_matrix,
    adapter_up_matrix,
    input_side_sketch,
    output_side_sketch,
    rank_sketch_down,
    rank_sketch_up,
):
    model_width = candidate_layer_inputs.shape[2]
    train_flat = candidate_layer_inputs.reshape(-1, model_width)
    probe_flat = probe_layer_inputs.reshape(-1, model_width)
    up_full, outward_full = (
        lax.all_gather(adapter_up_matrix, "fsdp", axis=0, tiled=True),
        lax.all_gather(output_side_sketch, "fsdp", axis=0, tiled=True),
    )

    def combine_couple(shard_rows):
        return (
            jnp.dot(train_flat, shard_rows, preferred_element_type=jnp.float32),
            jnp.dot(probe_flat, shard_rows, preferred_element_type=jnp.float32),
        )

    candidate_down_gradient, probe_down_gradient = combine_couple(
        lax.all_gather(adapter_down_matrix, "fsdp", axis=0, tiled=True)
    )
    train_in, probe_in = combine_couple(
        lax.all_gather(input_side_sketch, "fsdp", axis=0, tiled=True)
    )
    probe_normed = compute_sketch_features(
        probe_down_gradient,
        probe_in,
        probe_loss_cotangent,
        probe_live_lengths,
        up_full,
        outward_full,
        rank_sketch_down,
        rank_sketch_up,
    )
    train_normed = compute_sketch_features(
        candidate_down_gradient,
        train_in,
        candidate_loss_cotangent,
        candidate_live_lengths,
        up_full,
        outward_full,
        rank_sketch_down,
        rank_sketch_up,
    )
    feat_count = train_normed.shape[1]
    scores = (
        jnp.dot(
            train_normed,
            lax.all_gather(probe_normed, "fsdp", axis=0, tiled=True).T,
            preferred_element_type=jnp.float32,
        )
        / feat_count
    )
    return (scores, train_normed)


def solution(mesh):
    in_specs = (
        P(("dp", "fsdp"), None, None),
        P(("dp", "fsdp"), None, None),
        P(("dp", "fsdp")),
        P(("dp", "fsdp"), None, None),
        P(("dp", "fsdp"), None, None),
        P(("dp", "fsdp")),
        P("fsdp", None),
        P("fsdp", None),
        P("fsdp", None),
        P("fsdp", None),
        P(),
        P(),
    )
    out_specs = (P(("dp", "fsdp"), None), P(("dp", "fsdp"), None))
    return jax.shard_map(body, mesh=mesh, in_specs=in_specs, out_specs=out_specs, check_vma=False)
```

profile of v0, /device:TPU:0, one launch (start us, length us, event | category | flops | bytes accessed | tf_op | source)
XLA Modules:
  0.0 102.3 jit_solution(4229393782945602550)
XLA Ops:
  7.3 0.7 all-gather.6.cloned.1.call-update
  8.0 0.7 all-gather.4.cloned.1.call-update
  8.7 11.0 %all_gather.15 = bf16[1024,128]{1,0:T(8,128)(2,1)S(1)} all-gather(bf16[128,128]{1,0:T(8,128)(2,1)} %param.19), channel_id=1, replica_groups=mesh['fsdp'=8,'dp'=4] {'fsdp'}, dimensions={0}, use_global_device_ids=true | all-gather | bytes 294912 | tf_op jit(solution)/shard_map/all_gather | solution.py:84
  19.7 0.7 fusion.19
  20.4 1.0 %broadcast_multiply_fusion.1 = bf16[4,32,1024]{2,1,0:T(8,128)(2,1)S(1)} fusion(bf16[4,32,1024]{2,1,0:T(8,128)(2,1)} %param.13, bf16[4,32]{1,0:T(4,128)(2,1)S(1)} %fusion.19), kind=kLoop, calls=%fused_computation.24 | loop fusion | flops 131072 | bytes 524544 | tf_op jit(solution)/shard_map/mul | solution.py:12
  21.5 1.0 fusion.7
  22.7 0.1 broadcast_multiply_fusion
  22.8 0.3 fusion.6
  23.2 9.6 %all_gather.18 = bf16[1024,256]{1,0:T(8,128)(2,1)S(1)} all-gather(bf16[128,256]{1,0:T(8,128)(2,1)S(1)} %copy-done.4), channel_id=1, replica_groups=mesh['fsdp'=8,'dp'=4] {'fsdp'}, dimensions={0}, use_global_device_ids=true | all-gather | bytes 589824 | tf_op jit(solution)/shard_map/all_gather | solution.py:85
  32.8 0.2 convolution_convert_fusion
  33.1 0.2 convolution_convert_fusion.2
  33.3 7.3 %all-gather.6.cloned.1.call-done = bf16[8192,128]{1,0:T(8,128)(2,1)} async-done(((bf16[1024,128]{1,0:T(8,128)(2,1)}), bf16[8192,128]{1,0:T(8,128)(2,1)}) %all-gather.6.cloned.1.call-update) | async-done | bytes 2097168 | tf_op jit(solution)/shard_map/all_gather | solution.py:95
  40.6 3.0 %fusion.5 = bf16[128,16]{0,1:T(8,128)(2,1)S(1)} fusion(bf16[128,16]{0,1:T(8,128)(2,1)S(1)} %copy-done.7, bf16[128,8192]{1,0:T(8,128)(2,1)} %bitcast.52, bf16[8192,128]{1,0:T(8,128)(2,1)} %all-gather.6.cloned.1.call-done), kind=kOutput, calls=%fused_computation.13 | convolution fusion | flops 268978176 | bytes 4202496 | tf_op jit(solution)/shard_map/dot_general | solution.py:42
  43.7 2.4 %fusion.4 = bf16[128,16]{0,1:T(8,128)(2,1)S(1)} fusion(bf16[128,16]{0,1:T(8,128)(2,1)S(1)} %copy-done.7, bf16[128,8192]{1,0:T(8,128)(2,1)S(1)} %bitcast.51, bf16[8192,128]{1,0:T(8,128)(2,1)} %all-gather.6.cloned.1.call-done), kind=kOutput, calls=%fused_computation.12 | convolution fusion | flops 268978176 | bytes 4202496 | tf_op jit(solution)/shard_map/dot_general | solution.py:42
  46.2 0.1 fusion.15
  46.3 0.1 fusion.11
  46.4 32.8 %all-gather.4.cloned.1.call-done = bf16[8192,256]{1,0:T(8,128)(2,1)} async-done(((bf16[1024,256]{1,0:T(8,128)(2,1)}), bf16[8192,256]{1,0:T(8,128)(2,1)}) %all-gather.4.cloned.1.call-update) | async-done | bytes 4194320 | tf_op jit(solution)/shard_map/all_gather | solution.py:98
  79.2 3.1 %convolution_convert_fusion.1 = bf16[128,256]{1,0:T(8,128)(2,1)S(1)} fusion(bf16[128,8192]{1,0:T(8,128)(2,1)S(1)} %bitcast.50, bf16[8192,256]{1,0:T(8,128)(2,1)} %all-gather.4.cloned.1.call-done), kind=kOutput, calls=%fused_computation.1 | convolution fusion | flops 536903680 | bytes 6356992 | tf_op jit(solution)/shard_map/dot_general | solution.py:91
  82.3 0.1 fusion.13
  82.4 0.1 multiply_reduce_fusion
  82.5 0.1 copy-done.1
  82.7 0.7 copy-done.2
  83.3 0.7 convolution_convert_fusion.3
  84.1 0.1 fusion.17
  84.2 0.1 multiply_reduce_fusion.1
  84.3 0.1 copy.22
  84.4 0.1 copy.23
  84.5 0.1 fusion.10
  84.6 9.8 %all-gather = bf16[8,4,8192]{2,1,0:T(4,128)(2,1)S(1)} all-gather(bf16[1,4,8192]{2,1,0:T(4,128)(2,1)S(1)} %fusion.10), channel_id=1, replica_groups=mesh['fsdp'=8,'dp'=4] {'fsdp'}, dimensions={0}, use_global_device_ids=true | all-gather | bytes 589824 | tf_op jit(solution)/shard_map/all_gather | solution.py:124
  94.4 0.1 reshape.117
  94.5 0.1 multiply_convert_fusion.1
  94.7 0.8 convolution_multiply_fusion
  (25 shorter events, 0.5 us)
Async XLA Ops:
  7.2 36.5 %copy-start = (bf16[4,32,8192]{2,1,0:T(8,128)(2,1)S(1)}, bf16[4,32,8192]{2,1,0:T(8,128)(2,1)}, u32[]{:S(2)}) copy-start(bf16[4,32,8192]{2,1,0:T(8,128)(2,1)} %param.15) | copy-start | bytes 6291460
  7.2 15.6 %copy-start.6 = (bf16[128,16]{0,1:T(8,128)(2,1)S(1)}, bf16[128,16]{0,1:T(8,128)(2,1)}, u32[]{:S(2)}) copy-start(bf16[128,16]{0,1:T(8,128)(2,1)} %param.22) | copy-start | bytes 12292
  7.2 15.4 %copy-start.8 = (s32[4]{0:T(128)S(1)}, s32[4]{0:T(128)}, u32[]{:S(2)}) copy-start(s32[4]{0:T(128)} %param.17) | copy-start | bytes 52
  7.2 15.4 %copy-start.3 = (bf16[4,32,1024]{2,1,0:T(8,128)(2,1)S(1)}, bf16[4,32,1024]{2,1,0:T(8,128)(2,1)}, u32[]{:S(2)}) copy-start(bf16[4,32,1024]{2,1,0:T(8,128)(2,1)} %param.16) | copy-start | bytes 786436
  7.2 16.0 %copy-start.4 = (bf16[128,256]{1,0:T(8,128)(2,1)S(1)}, bf16[128,256]{1,0:T(8,128)(2,1)}, u32[]{:S(2)}) copy-start(bf16[128,256]{1,0:T(8,128)(2,1)} %param.21) | copy-start | bytes 196612
  7.2 33.4 %all-gather.6.cloned.1.call-start = ((), (), s32[]{:S(2)}) async-start(), calls=%async_computation.1 | async-start | bytes 2359296 | tf_op jit(solution)/shard_map/all_gather | solution.py:95
  8.0 71.3 %all-gather.4.cloned.1.call-start = ((), (), s32[]{:S(2)}) async-start(), calls=%async_computation | async-start | bytes 4718592 | tf_op jit(solution)/shard_map/all_gather | solution.py:98
  21.5 19.1 %copy-start.7 = (bf16[128,16]{0,1:T(8,128)(2,1)S(1)}, bf16[128,16]{0,1:T(8,128)(2,1)}, u32[]{:S(2)}) copy-start(bf16[128,16]{0,1:T(8,128)(2,1)} %param.23) | copy-start | bytes 12292
  79.2 3.4 %copy-start.1 = (bf16[8192,256]{1,0:T(8,128)(2,1)S(1)}, bf16[8192,256]{1,0:T(8,128)(2,1)}, u32[]{:S(2)}) copy-start(bf16[8192,256]{1,0:T(8,128)(2,1)} %all-gather.4.cloned.1.call-done) | copy-start | bytes 12582916
  79.2 4.1 %copy-start.2 = (bf16[4,32,8192]{2,1,0:T(8,128)(2,1)S(1)}, bf16[4,32,8192]{2,1,0:T(8,128)(2,1)}, u32[]{:S(2)}) copy-start(bf16[4,32,8192]{2,1,0:T(8,128)(2,1)} %param.12) | copy-start | bytes 6291460
  94.6 0.9 copy-start.5
Sparse Core Ops, SparseCore 0:
  9.9 30.5 all-gather.5
  42.5 36.7 all-gather.3
where the time goes:
time: 103 us; the launch traced here: 102 us
  waiting for transfers between devices  41.4 us (40%)
  blocking collectives  30.4 us (30%)
  between operations  14.2 us (14%)
  matrix products  12.4 us (12%)
  other arithmetic  2.39 us (2%)
  local copies, waits for them, and re-layouts  1.47 us (1%)
    all_gather x1, waiting for transfers between devices, body(): lax.all_gather(input_side_sketch, 'fsdp', axis=0, tiled=True)  32.8 us
    all_gather x1, blocking collectives, body(): lax.all_gather(adapter_up_matrix, 'fsdp', axis=0, tiled=True)  11 us
    all_gather x1, blocking collectives, body(): lax.all_gather(probe_normed, 'fsdp', axis=0, tiled=True)  9.82 us
    all_gather x1, blocking collectives, body(): lax.all_gather(output_side_sketch, 'fsdp', axis=0, tiled=True)  9.62 us
    all_gather x1, waiting for transfers between devices, body(): lax.all_gather(adapter_down_matrix, 'fsdp', axis=0, tiled=True)  7.27 us
    dot_general x2, matrix products, compute_sketch_features(): jnp.dot(down_round, rank_sketch_up, preferred_element_type=jnp.float32)  5.45 us
    dot_general x1, matrix products, combine_couple(): jnp.dot(probe_flat, shard_rows, preferred_element_type=jnp.float32)  3.05 us
  transfers between devices with their start and end apart: 2, of which 2 were waited for; matrix products, arithmetic and copies ran while one was open for 10% of the time, Pallas kernels for 0%

commit v1 on v0

v1 whole, which is shorter than its diff:
```python
import functools

import jax
import jax.numpy as jnp
from jax import lax
from jax.experimental import pallas as pl
from jax.experimental.pallas import tpu as pltpu
from jax.sharding import PartitionSpec as P

eps_mean = 1e-06
LAST = (((1,), (1,)), ((), ()))
VMEM = pl.BlockSpec(memory_space=pltpu.VMEM)
SMEM = pl.BlockSpec(memory_space=pltpu.SMEM)
MIB = 1 << 20


def dot(a, b):
    return jnp.dot(a, b, preferred_element_type=jnp.float32)


def dot_last(a, b):
    return lax.dot_general(a, b, LAST, preferred_element_type=jnp.float32)


def split_two(x):
    high = x.astype(jnp.bfloat16)
    return high, (x - high.astype(jnp.float32)).astype(jnp.bfloat16)


def fold_kernel(down_ref, up_ref, rank_down_ref, rank_up_ref, out_ref):
    first = (((0,), (1,)), ((), ()))
    rows = down_ref.shape[0]
    out_ref[:, :rows] = lax.dot_general(
        rank_up_ref[...], down_ref[...], first, preferred_element_type=jnp.float32
    ).astype(jnp.bfloat16)
    out_ref[:, rows:] = lax.dot_general(
        rank_down_ref[...], up_ref[...], first, preferred_element_type=jnp.float32
    ).astype(jnp.bfloat16)


def spread(small, lengths_ref, seq):
    ks, width = small.shape
    count = width // seq
    rows = lax.broadcasted_iota(jnp.int32, (count * ks, width), 0)
    cols = lax.broadcasted_iota(jnp.int32, (count * ks, width), 1)
    live = jnp.zeros((count * ks, width), jnp.bool_)
    for e in range(count):
        start = e * seq
        live = live | (
            (rows >= e * ks)
            & (rows < (e + 1) * ks)
            & (cols >= start)
            & (cols < start + lengths_ref[e])
        )
    tiled = jnp.concatenate([small] * count, axis=0)
    return jnp.where(live, tiled, 0.0).astype(jnp.bfloat16)


def rows_kernel(
    order, seq, halves,
    c_x, c_m, c_len, p_x, p_m, p_len, t_same, t_other,
    left_ref, right_ref,
):
    me = lax.axis_index("fsdp")
    ks = t_same.shape[0] * 2 // len(order)
    n = len(order)
    model, value = c_x.shape[1], c_m.shape[1]
    kd, ku = model // n, value // n
    sides = ((c_x, c_m, c_len), (p_x, p_m, p_len))
    tables = [
        (t_same if g < n // 2 else t_other)[(g % (n // 2)) * ks : (g % (n // 2) + 1) * ks, :]
        for g in range(n)
    ]
    part = ku // halves
    total = 2 * left_ref.shape[0] // 4
    for side, (x, m, lengths) in enumerate(sides):
        left_small = 0.0
        right_small = 0.0
        for g, k in enumerate(order):
            j = me ^ k
            left_small += dot_last(tables[g][:, kd:], m[:, pl.ds(pl.multiple_of(j * ku, ku), ku)])
        for g, k in enumerate(order):
            j = me ^ k
            right_small += dot_last(tables[g][:, :kd], x[:, pl.ds(pl.multiple_of(j * kd, kd), kd)])
        left_wide = spread(left_small.astype(jnp.bfloat16).astype(jnp.float32), lengths, seq)
        right_wide = spread(right_small.astype(jnp.bfloat16).astype(jnp.float32), lengths, seq)
        rows = left_wide.shape[0]
        at = side * rows
        for b in range(n):
            high, low = split_two(dot(left_wide, x[:, b * kd : (b + 1) * kd]))
            left_ref[at : at + rows, b * kd : (b + 1) * kd] = high
            left_ref[total + at : total + at + rows, b * kd : (b + 1) * kd] = low
        high, low = split_two(dot(right_wide, m[...]))
        for b in range(n * halves):
            right_ref[b, at : at + rows, :] = high[:, b * part : (b + 1) * part]
            right_ref[b, total + at : total + at + rows, :] = low[:, b * part : (b + 1) * part]


def join_kernel(keys, ks, s_rows, left_ref, right_ref, *refs):
    pieces, (c_out, p_out, left_scratch, right_scratch) = refs[: len(keys)], refs[len(keys) :]
    me = lax.axis_index("fsdp")
    halves = 1 + max(h for _, h in keys)
    left = 0.0
    right = 0.0
    for (k, h), piece in zip(keys, pieces):
        at = (me ^ k) * halves + h
        left += dot(left_ref[:, pl.ds(pl.multiple_of(at * s_rows, s_rows), s_rows)], piece[:s_rows, :])
        right += dot(right_ref[at], piece[s_rows:, :])
    total = left.shape[0] // 2
    left = left[:total] + left[total:]
    right = right[:total] + right[total:]
    count, cols = total // ks, left.shape[1]
    left = left.reshape(count, ks, cols)
    right = right.reshape(count, ks, cols)
    mean = jnp.sum(left * left + right * right, axis=(1, 2), keepdims=True) / (2 * ks * cols)
    scale = lax.rsqrt(mean + eps_mean)
    lanes = left_scratch.shape[2]
    for scratch, value in ((left_scratch, left), (right_scratch, right)):
        scaled = (value * scale).reshape(total, cols)
        for b in range(cols // lanes):
            scratch[b] = scaled[:, b * lanes : (b + 1) * lanes]
    half = count // 2
    for side, out in enumerate((c_out, p_out)):
        for t, scratch in enumerate((left_scratch, right_scratch)):
            for r in range(ks):
                for b in range(cols // lanes):
                    at = (t * ks + r) * cols + b * lanes
                    rows = pl.ds(side * half * ks + r, half, stride=ks)
                    out[:, at : at + lanes] = scratch[b, rows, :].astype(jnp.bfloat16)


def score_kernel(order, c_ref, same_ref, other_ref, out_ref):
    me = lax.axis_index("fsdp")
    feats = c_ref[...]
    mixed = jnp.concatenate([dot_last(feats, same_ref[...]), dot_last(feats, other_ref[...])], axis=1)
    width = mixed.shape[1]
    per = width // len(order)
    rows = lax.broadcasted_iota(jnp.int32, (width, width), 0)
    cols = lax.broadcasted_iota(jnp.int32, (width, width), 1)
    target = jnp.zeros((width, width), jnp.int32)
    for g, k in enumerate(order):
        target = jnp.where(rows // per == g, (me ^ k) * per + rows % per, target)
    place = (target == cols).astype(jnp.float32)
    out = lax.dot_general(
        mixed, place, (((1,), (0,)), ((), ())),
        preferred_element_type=jnp.float32, precision=lax.Precision.HIGHEST,
    )
    out_ref[...] = out / feats.shape[1]


def swap(x, k, axis, size):
    return lax.ppermute(x, axis, [(i, i ^ k) for i in range(size)])


def fast_body(n, c_x, c_m, c_len, p_x, p_m, p_len, down, up, sketch_in, sketch_out, rank_down, rank_up):
    examples, seq, model = c_x.shape
    value = c_m.shape[2]
    ks, kp = rank_down.shape[1], sketch_in.shape[1]
    s_shard, o_shard = sketch_in.shape[0], sketch_out.shape[0]
    sw = functools.partial(swap, axis="fsdp", size=n)
    order = (0, 2, 4, 6, 1, 3, 5, 7)
    halves = 2
    s_rows, o_rows = s_shard // halves, o_shard // halves

    h0, h1 = (
        jnp.concatenate(
            [sketch_in[h * s_rows : (h + 1) * s_rows], sketch_out[h * o_rows : (h + 1) * o_rows]]
        )
        for h in range(halves)
    )
    x0, y1 = sw(h0, 2), sw(h1, 4)

    table = pl.pallas_call(
        fold_kernel,
        out_shape=jax.ShapeDtypeStruct((ks, down.shape[0] + up.shape[0]), jnp.bfloat16),
        in_specs=[VMEM] * 4,
        out_specs=VMEM,
        compiler_params=pltpu.CompilerParams(vmem_limit_bytes=4 * MIB),
        name="fold_ranks",
    )(down, up, rank_down, rank_up)
    t_same = jnp.concatenate([table, sw(table, 2), sw(table, 4), sw(table, 6)])
    t_other = sw(t_same, 1)

    x1, y0 = sw(h1, 2), sw(h0, 4)
    d0, d1 = sw(x0, 4), sw(y1, 2)
    pieces = {(0, 0): h0, (0, 1): h1, (2, 0): x0, (2, 1): x1, (4, 0): y0, (4, 1): y1, (6, 0): d0, (6, 1): d1}
    for (k, h), piece in list(pieces.items()):
        pieces[(k ^ 1, h)] = sw(piece, 1)

    flat = (examples * seq, model)
    flat_m = (examples * seq, value)
    total = 2 * examples * ks
    left, right = pl.pallas_call(
        functools.partial(rows_kernel, order, seq, halves),
        out_shape=(
            jax.ShapeDtypeStruct((2 * total, model), jnp.bfloat16),
            jax.ShapeDtypeStruct((n * halves, 2 * total, o_rows), jnp.bfloat16),
        ),
        in_specs=[VMEM, VMEM, SMEM, VMEM, VMEM, SMEM, VMEM, VMEM],
        out_specs=(VMEM, VMEM),
        compiler_params=pltpu.CompilerParams(vmem_limit_bytes=24 * MIB),
        name="example_rows",
    )(
        c_x.reshape(flat), c_m.reshape(flat_m), c_len, p_x.reshape(flat), p_m.reshape(flat_m), p_len, t_same, t_other
    )

    keys = tuple(sorted(pieces))
    feats = jax.ShapeDtypeStruct((examples, 2 * ks * kp), jnp.bfloat16)
    c_feat, p_feat = pl.pallas_call(
        functools.partial(join_kernel, keys, ks, s_rows),
        out_shape=(feats, feats),
        in_specs=[VMEM] * (2 + len(keys)),
        out_specs=(VMEM, VMEM),
        scratch_shapes=[pltpu.VMEM((kp // 128, total, 128), jnp.float32)] * 2,
        compiler_params=pltpu.CompilerParams(vmem_limit_bytes=24 * MIB),
        name="join_features",
    )(left, right, *(pieces[key] for key in keys))

    same = jnp.concatenate([p_feat, sw(p_feat, 2), sw(p_feat, 4), sw(p_feat, 6)])
    other = sw(same, 1)
    scores = pl.pallas_call(
        functools.partial(score_kernel, order),
        out_shape=jax.ShapeDtypeStruct((examples, n * examples), jnp.float32),
        in_specs=[VMEM] * 3,
        out_specs=VMEM,
        compiler_params=pltpu.CompilerParams(vmem_limit_bytes=8 * MIB),
        name="score_rows",
    )(c_feat, same, other)
    return scores, c_feat


def plain_features(x, m, lengths, down, up, sketch_in, sketch_out, rank_down, rank_up):
    examples, seq, model = x.shape
    ks, kp = rank_down.shape[1], sketch_in.shape[1]
    live = (lax.broadcasted_iota(jnp.int32, (examples, seq), 1) < lengths[:, None]).astype(m.dtype)
    masked = (m * live[:, :, None]).reshape(examples * seq, -1)
    rows = x.reshape(examples * seq, model)
    grad_rows = dot(masked, up).astype(jnp.bfloat16)
    outward = dot(masked, sketch_out).astype(jnp.bfloat16)
    down_round = dot(rows, down).astype(jnp.bfloat16)
    inward = dot(rows, sketch_in).astype(jnp.bfloat16)
    left_small = dot(grad_rows, rank_down).astype(jnp.bfloat16)
    right_small = dot(down_round, rank_up).astype(jnp.bfloat16)

    def outer(small, wide):
        return jnp.einsum(
            "esk,esp->ekp",
            small.reshape(examples, seq, ks),
            wide.reshape(examples, seq, kp),
            preferred_element_type=jnp.float32,
        )

    joined = jnp.concatenate([outer(left_small, inward), outer(right_small, outward)], axis=1)
    joined = joined.reshape(examples, 2 * ks * kp)
    scale = lax.rsqrt(jnp.mean(joined * joined, axis=1, keepdims=True) + eps_mean)
    return (joined * scale).astype(jnp.bfloat16)


def plain_body(c_x, c_m, c_len, p_x, p_m, p_len, down, up, sketch_in, sketch_out, rank_down, rank_up):
    weights = [
        lax.all_gather(w, "fsdp", axis=0, tiled=True) for w in (down, up, sketch_in, sketch_out)
    ]
    p_feat = plain_features(p_x, p_m, p_len, *weights, rank_down, rank_up)
    c_feat = plain_features(c_x, c_m, c_len, *weights, rank_down, rank_up)
    every = lax.all_gather(p_feat, "fsdp", axis=0, tiled=True)
    return dot(c_feat, every.T) / c_feat.shape[1], c_feat


def solution(mesh):
    n = mesh.shape["fsdp"]
    rows = P(("dp", "fsdp"), None)
    cube = P(("dp", "fsdp"), None, None)
    line = P(("dp", "fsdp"))
    shard = P("fsdp", None)
    in_specs = (cube, cube, line, cube, cube, line, shard, shard, shard, shard, P(), P())

    def body(*args):
        if n == 1 << 3:
            return fast_body(n, *args)
        return plain_body(*args)

    return jax.shard_map(body, mesh=mesh, in_specs=in_specs, out_specs=(rows, rows), check_vma=False)
```

time: 103 us -> 53 us (0.51)
  blocking collectives: 30.4 us -> 0 us
  waiting for transfers between devices: 41.4 us -> 21.2 us
  starting transfers between devices: 0.08 us -> 15.7 us
  between operations: 14.2 us -> 0.79 us
  matrix products: 12.4 us -> 0 us
  Pallas kernels: 0 us -> 6.93 us
  local copies, waits for them, and re-layouts: 1.47 us -> 7.76 us
  other arithmetic: 2.39 us -> 0.21 us
    all_gather x2 -> x0, waiting for transfers between devices: 40 us -> none  [the longest x1 32.8 us: body(): lax.all_gather(input_side_sketch, 'fsdp', axis=0, tiled=True)]
    all_gather x3 -> x0, blocking collectives: 30.4 us -> none  [the longest x1 11 us: body(): lax.all_gather(adapter_up_matrix, 'fsdp', axis=0, tiled=True)]
    ppermute x0 -> x22, waiting for transfers between devices: none -> 21.2 us  [swap(): return lax.ppermute(x, axis, [(i, i ^ k) for i in range(size)])]
    ppermute x0 -> x22, starting transfers between devices: none -> 15.7 us  [swap(): return lax.ppermute(x, axis, [(i, i ^ k) for i in range(size)])]
    dot_general x13 -> x0, matrix products: 12.4 us -> none  [the longest x2 5.45 us: compute_sketch_features(): jnp.dot(down_round, rank_sketch_up, preferred_element_type=jnp.float32)]
    pallas_call x0 -> x4, Pallas kernels: none -> 6.93 us  [the longest x1 2.97 us: fast_body(): pl.pallas_call(functools.partial(rows_kernel, order, seq, halves), out_sh...]
    unnamed x21 -> x20, local copies, waits for them, and re-layouts: 1.14 us -> 5.91 us
    slice x0 -> x2, local copies, waits for them, and re-layouts: none -> 1.85 us  [the longest x1 1.06 us: fast_body(): sketch_in[h * s_rows:(h + 1) * s_rows]]
  transfers between devices with their start and end apart: 2 -> 22, of which waited for: 2 -> 8; matrix products, arithmetic and copies ran while one was open for 10% -> 4% of each run, Pallas kernels for 0% -> 6%
where the time goes in v1:
time: 53 us; the launch traced here: 52.6 us
  waiting for transfers between devices  21.2 us (40%)
  starting transfers between devices  15.7 us (30%)
  local copies, waits for them, and re-layouts  7.76 us (15%)
  Pallas kernels  6.93 us (13%)
  between operations  0.79 us (1%)
    ppermute x22, waiting for transfers between devices, swap(): return lax.ppermute(x, axis, [(i, i ^ k) for i in range(size)])  21.2 us
    ppermute x22, starting transfers between devices, swap(): return lax.ppermute(x, axis, [(i, i ^ k) for i in range(size)])  15.7 us
    unnamed x20, local copies, waits for them, and re-layouts  5.91 us
    pallas_call x1, Pallas kernels, fast_body(): pl.pallas_call(functools.partial(rows_kernel, order, seq, halves), out_sh...  2.97 us
    pallas_call x1, Pallas kernels, fast_body(): pl.pallas_call(functools.partial(join_kernel, keys, ks, s_rows), out_shap...  2.61 us
    pallas_call x1, Pallas kernels, fast_body(): pl.pallas_call(functools.partial(score_kernel, order), out_shape=jax.Shap...  1.14 us
    slice x1, local copies, waits for them, and re-layouts, fast_body(): sketch_in[h * s_rows:(h + 1) * s_rows]  1.06 us
  transfers between devices with their start and end apart: 22, of which 8 were waited for; matrix products, arithmetic and copies ran while one was open for 4% of the time, Pallas kernels for 6%

profile of v1, /device:TPU:0, one launch (start us, length us, event | category | flops | bytes accessed | tf_op | source)
XLA Modules:
  0.0 52.6 jit_solution(714608876088714231)
XLA Ops:
  0.7 1.0 %copy.14.rank_down_ref = bf16[128,16]{1,0:T(8,128)(2,1)S(1)} copy(bf16[128,16]{0,1:T(8,128)(2,1)} %param.22) | data formatting | bytes 8192 | tf_op args[10]
  1.6 0.8 %copy.15.rank_up_ref = bf16[128,16]{1,0:T(8,128)(2,1)S(1)} copy(bf16[128,16]{0,1:T(8,128)(2,1)} %param.23) | data formatting | bytes 8192 | tf_op args[11]
  2.4 0.9 %copy-done.4 = bf16[1024,128]{1,0:T(8,128)(2,1)S(1)} copy-done((bf16[1024,128]{1,0:T(8,128)(2,1)S(1)}, bf16[1024,128]{1,0:T(8,128)(2,1)}, u32[]{:S(2)}) %copy-start.4) | copy-done | bytes 262168
  3.4 0.8 %copy-done.6 = bf16[128,128]{1,0:T(8,128)(2,1)S(1)} copy-done((bf16[128,128]{1,0:T(8,128)(2,1)S(1)}, bf16[128,128]{1,0:T(8,128)(2,1)}, u32[]{:S(2)}) %copy-start.6) | copy-done | bytes 32792
  4.1 0.2 fold_ranks.1
  4.3 3.0 %collective-permute-start = (bf16[16,1152]{1,0:T(8,128)(2,1)S(1)}, bf16[16,1152]{1,0:T(8,128)(2,1)S(1)}, u32[]{:S(2)}, u32[]{:S(2)}) collective-permute-start(bf16[16,1152]{1,0:T(8,128)(2,1)S(1)} %fold_ranks.1), channel_id=1, source_target_pairs={{0,8},{4,12},{8,0},{12,4},{16,24},{20,28},{24,16},{28,20},{1,9},{5... | collective-permute-start | bytes 110600 | tf_op jit(solution)/shard_map/ppermute | solution.py:152
  7.3 1.5 %collective-permute-start.1 = (bf16[16,1152]{1,0:T(8,128)(2,1)S(1)}, bf16[16,1152]{1,0:T(8,128)(2,1)S(1)}, u32[]{:S(2)}, u32[]{:S(2)}) collective-permute-start(bf16[16,1152]{1,0:T(8,128)(2,1)S(1)} %fold_ranks.1), channel_id=1, source_target_pairs={{0,16},{4,20},{8,24},{12,28},{16,0},{20,4},{24,8},{28,12},{1,17},{... | collective-permute-start | bytes 110600 | tf_op jit(solution)/shard_map/ppermute | solution.py:152
  8.8 1.1 %fusion = (bf16[512,256]{1,0:T(8,128)(2,1)S(1)}, bf16[512,256]{1,0:T(8,128)(2,1)S(1)}) fusion(bf16[1024,256]{1,0:T(8,128)(2,1)} %param.20), kind=kLoop, calls=%fused_computation.4 | loop fusion | bytes 1048576 | tf_op jit(solution)/shard_map/slice | solution.py:167
  9.9 0.8 %fusion.1 = (bf16[64,256]{1,0:T(8,128)(2,1)S(1)}, bf16[64,256]{1,0:T(8,128)(2,1)S(1)}) fusion(bf16[128,256]{1,0:T(8,128)(2,1)} %param.21), kind=kLoop, calls=%fused_computation.5 | loop fusion | bytes 131072 | tf_op jit(solution)/shard_map/slice | solution.py:167
  10.7 2.0 %collective-permute-start.6 = (bf16[576,256]{1,0:T(8,128)(2,1)S(1)}, bf16[576,256]{1,0:T(8,128)(2,1)S(1)}, u32[]{:S(2)}, u32[]{:S(2)}) collective-permute-start(bf16[576,256]{1,0:T(8,128)(2,1)S(1)} %pad_maximum_fusion.refs_0_), channel_id=1, source_target_pairs={{0,8},{4,12},{8,0},{12,4},{16,24},{20,28},{24,16},{28,20},{1,9},{5... | collective-permute-start | bytes 884744 | tf_op jit(solution)/shard_map/ppermute | solution.py:152
  12.7 1.5 %collective-permute-start.10 = (bf16[576,256]{1,0:T(8,128)(2,1)S(1)}, bf16[576,256]{1,0:T(8,128)(2,1)S(1)}, u32[]{:S(2)}, u32[]{:S(2)}) collective-permute-start(bf16[576,256]{1,0:T(8,128)(2,1)S(1)} %pad_maximum_fusion.refs_0_), channel_id=1, source_target_pairs={{0,16},{4,20},{8,24},{12,28},{16,0},{20,4},{24,8},{28,12},{1,17},{... | collective-permute-start | bytes 884744 | tf_op jit(solution)/shard_map/ppermute | solution.py:152
  14.3 0.6 %collective-permute-start.11 = (bf16[576,256]{1,0:T(8,128)(2,1)S(1)}, bf16[576,256]{1,0:T(8,128)(2,1)S(1)}, u32[]{:S(2)}, u32[]{:S(2)}) collective-permute-start(bf16[576,256]{1,0:T(8,128)(2,1)S(1)} %pad_maximum_fusion.1.refs_1_), channel_id=1, source_target_pairs={{0,16},{4,20},{8,24},{12,28},{16,0},{20,4},{24,8},{28,12},{1,17},{... | collective-permute-start | bytes 884744 | tf_op jit(solution)/shard_map/ppermute | solution.py:152
  15.1 1.4 %collective-permute-done.3.t_other = bf16[64,1152]{1,0:T(8,128)(2,1)S(1)} collective-permute-done((bf16[64,1152]{1,0:T(8,128)(2,1)S(1)}, bf16[64,1152]{1,0:T(8,128)(2,1)S(1)}, u32[]{:S(2)}, u32[]{:S(2)}) %collective-permute-start.3) | collective-permute-done | bytes 147488 | tf_op jit(solution)/shard_map/ppermute | solution.py:152
  16.6 4.1 %collective-permute-done.6.refs_4_ = bf16[576,256]{1,0:T(8,128)(2,1)S(1)} collective-permute-done((bf16[576,256]{1,0:T(8,128)(2,1)S(1)}, bf16[576,256]{1,0:T(8,128)(2,1)S(1)}, u32[]{:S(2)}, u32[]{:S(2)}) %collective-permute-start.6) | collective-permute-done | bytes 294944 | tf_op jit(solution)/shard_map/ppermute | solution.py:152
  20.7 6.0 %collective-permute-done.11.refs_9_ = bf16[576,256]{1,0:T(8,128)(2,1)S(1)} collective-permute-done((bf16[576,256]{1,0:T(8,128)(2,1)S(1)}, bf16[576,256]{1,0:T(8,128)(2,1)S(1)}, u32[]{:S(2)}, u32[]{:S(2)}) %collective-permute-start.11) | collective-permute-done | bytes 294944 | tf_op jit(solution)/shard_map/ppermute | solution.py:152
  26.7 1.5 %collective-permute-start.14 = (bf16[576,256]{1,0:T(8,128)(2,1)S(1)}, bf16[576,256]{1,0:T(8,128)(2,1)S(1)}, u32[]{:S(2)}, u32[]{:S(2)}) collective-permute-start(bf16[576,256]{1,0:T(8,128)(2,1)S(1)} %collective-permute-done.6.refs_4_), channel_id=1, source_target_pairs={{0,16},{4,20},{8,24},{12,28},{16,0},{20,4},{24,8},{28,12},{1,17},{... | collective-permute-start | bytes 884744 | tf_op jit(solution)/shard_map/ppermute | solution.py:152
  28.2 0.5 %collective-permute-start.15 = (bf16[576,256]{1,0:T(8,128)(2,1)S(1)}, bf16[576,256]{1,0:T(8,128)(2,1)S(1)}, u32[]{:S(2)}, u32[]{:S(2)}) collective-permute-start(bf16[576,256]{1,0:T(8,128)(2,1)S(1)} %collective-permute-done.11.refs_9_), channel_id=1, source_target_pairs={{0,8},{4,12},{8,0},{12,4},{16,24},{20,28},{24,16},{28,20},{1,9},{5... | collective-permute-start | bytes 884744 | tf_op jit(solution)/shard_map/ppermute | solution.py:152
  28.8 0.5 collective-permute-start.8
  29.3 4.1 %collective-permute-done.14.refs_12_ = bf16[576,256]{1,0:T(8,128)(2,1)S(1)} collective-permute-done((bf16[576,256]{1,0:T(8,128)(2,1)S(1)}, bf16[576,256]{1,0:T(8,128)(2,1)S(1)}, u32[]{:S(2)}, u32[]{:S(2)}) %collective-permute-start.14) | collective-permute-done | bytes 294944 | tf_op jit(solution)/shard_map/ppermute | solution.py:152
  33.4 1.5 %collective-permute-done.15.refs_13_ = bf16[576,256]{1,0:T(8,128)(2,1)S(1)} collective-permute-done((bf16[576,256]{1,0:T(8,128)(2,1)S(1)}, bf16[576,256]{1,0:T(8,128)(2,1)S(1)}, u32[]{:S(2)}, u32[]{:S(2)}) %collective-permute-start.15) | collective-permute-done | bytes 294944 | tf_op jit(solution)/shard_map/ppermute | solution.py:152
  34.9 0.5 collective-permute-start.17
  35.5 1.6 %copy-done.1 = bf16[4,32,8192]{2,1,0:T(8,128)(2,1)S(1)} copy-done((bf16[4,32,8192]{2,1,0:T(8,128)(2,1)S(1)}, bf16[4,32,8192]{2,1,0:T(8,128)(2,1)}, u32[]{:S(2)}) %copy-start.1) | copy-done | bytes 2097176
  37.1 3.0 %example_rows.1 = (bf16[256,8192]{1,0:T(8,128)(2,1)S(1)}, bf16[16,256,64]{2,1,0:T(8,128)(2,1)S(1)}) custom-call(bf16[128,8192]{1,0:T(8,128)(2,1)S(1)} %bitcast.4, bf16[128,1024]{1,0:T(8,128)(2,1)S(1)} %bitcast.6, s32[4]{0:T(128)S(1)} %copy-done.7, bf16[128,8192]{1,0:T(8,128)(2,1)S(1)} %bitcast.5, bf16[128,1024]{1,0:T(8,128)(2,1)S(1)} %bitcast.7, ...), custom_call_target="tpu_custom_call" | custom-call | tf_op jit(solution)/shard_map/example_rows/pallas_call | solution.py:193
  40.1 2.6 %join_features.1 = (bf16[4,8192]{1,0:T(4,128)(2,1)}, bf16[4,8192]{1,0:T(4,128)(2,1)S(1)}) custom-call(bf16[256,8192]{1,0:T(8,128)(2,1)S(1)} %get-tuple-element.6.left_ref, bf16[16,256,64]{2,1,0:T(8,128)(2,1)S(1)} %get-tuple-element.7.right_ref, bf16[576,256]{1,0:T(8,128)(2,1)S(1)} %pad_maximum_fusion.refs_0_, ...), custom_call_target="tpu_custom_call" | custom-call | tf_op jit(solution)/shard_map/join_features/pallas_call | solution.py:209
  42.7 0.5 %collective-permute-start.18 = (bf16[4,8192]{1,0:T(4,128)(2,1)S(1)}, bf16[4,8192]{1,0:T(4,128)(2,1)S(1)}, u32[]{:S(2)}, u32[]{:S(2)}) collective-permute-start(bf16[4,8192]{1,0:T(4,128)(2,1)S(1)} %get-tuple-element.9), channel_id=1, source_target_pairs={{0,8},{4,12},{8,0},{12,4},{16,24},{20,28},{24,16},{28,20},{1,9},{5... | collective-permute-start | bytes 196616 | tf_op jit(solution)/shard_map/ppermute | solution.py:152
  43.3 0.3 collective-permute-start.19
  43.6 2.6 %collective-permute-start.20 = (bf16[4,8192]{1,0:T(4,128)(2,1)S(1)}, bf16[4,8192]{1,0:T(4,128)(2,1)S(1)}, u32[]{:S(2)}, u32[]{:S(2)}) collective-permute-start(bf16[4,8192]{1,0:T(4,128)(2,1)S(1)} %get-tuple-element.9), channel_id=1, source_target_pairs={{0,24},{4,28},{8,16},{12,20},{16,8},{20,12},{24,0},{28,4},{1,25},{... | collective-permute-start | bytes 196616 | tf_op jit(solution)/shard_map/ppermute | solution.py:152
  46.2 1.1 %collective-permute-done.18 = bf16[4,8192]{1,0:T(4,128)(2,1)S(1)} collective-permute-done((bf16[4,8192]{1,0:T(4,128)(2,1)S(1)}, bf16[4,8192]{1,0:T(4,128)(2,1)S(1)}, u32[]{:S(2)}, u32[]{:S(2)}) %collective-permute-start.18) | collective-permute-done | bytes 65568 | tf_op jit(solution)/shard_map/ppermute | solution.py:152
  47.3 1.6 %collective-permute-done.19 = bf16[4,8192]{1,0:T(4,128)(2,1)S(1)} collective-permute-done((bf16[4,8192]{1,0:T(4,128)(2,1)S(1)}, bf16[4,8192]{1,0:T(4,128)(2,1)S(1)}, u32[]{:S(2)}, u32[]{:S(2)}) %collective-permute-start.19) | collective-permute-done | bytes 65568 | tf_op jit(solution)/shard_map/ppermute | solution.py:152
  49.1 1.5 %collective-permute-done.21.other_ref = bf16[16,8192]{1,0:T(8,128)(2,1)S(1)} collective-permute-done((bf16[16,8192]{1,0:T(8,128)(2,1)S(1)}, bf16[16,8192]{1,0:T(8,128)(2,1)S(1)}, u32[]{:S(2)}, u32[]{:S(2)}) %collective-permute-start.21) | collective-permute-done | bytes 262176 | tf_op jit(solution)/shard_map/ppermute | solution.py:152
  50.6 0.8 %copy-done.5 = bf16[4,8192]{1,0:T(4,128)(2,1)S(1)} copy-done((bf16[4,8192]{1,0:T(4,128)(2,1)S(1)}, bf16[4,8192]{1,0:T(4,128)(2,1)}, u32[]{:S(2)}) %copy-start.5) | copy-done | bytes 65560
  51.4 1.1 %score_rows.1 = f32[4,32]{1,0:T(4,128)} custom-call(bf16[4,8192]{1,0:T(4,128)(2,1)S(1)} %copy-done.5, bf16[16,8192]{1,0:T(8,128)(2,1)S(1)} %pad_maximum_fusion.2.same_ref, bf16[16,8192]{1,0:T(8,128)(2,1)S(1)} %collective-permute-done.21.other_ref), custom_call_target="tpu_custom_call" | custom-call | tf_op jit(solution)/shard_map/score_rows/pallas_call | solution.py:221
  (42 shorter events, 0.8 us)
Async XLA Ops:
  0.6 34.8 %copy-start = (bf16[4,32,8192]{2,1,0:T(8,128)(2,1)S(1)}, bf16[4,32,8192]{2,1,0:T(8,128)(2,1)}, u32[]{:S(2)}) copy-start(bf16[4,32,8192]{2,1,0:T(8,128)(2,1)} %param.12) | copy-start | bytes 6291460
  0.6 34.8 %copy-start.2 = (bf16[4,32,1024]{2,1,0:T(8,128)(2,1)S(1)}, bf16[4,32,1024]{2,1,0:T(8,128)(2,1)}, u32[]{:S(2)}) copy-start(bf16[4,32,1024]{2,1,0:T(8,128)(2,1)} %param.13) | copy-start | bytes 786436
  0.7 34.8 %copy-start.3 = (bf16[4,32,1024]{2,1,0:T(8,128)(2,1)S(1)}, bf16[4,32,1024]{2,1,0:T(8,128)(2,1)}, u32[]{:S(2)}) copy-start(bf16[4,32,1024]{2,1,0:T(8,128)(2,1)} %param.16) | copy-start | bytes 786436
  2.4 1.0 %copy-start.4 = (bf16[1024,128]{1,0:T(8,128)(2,1)S(1)}, bf16[1024,128]{1,0:T(8,128)(2,1)}, u32[]{:S(2)}) copy-start(bf16[1024,128]{1,0:T(8,128)(2,1)} %down_ref.1) | copy-start | bytes 786436
  3.4 0.8 %copy-start.6 = (bf16[128,128]{1,0:T(8,128)(2,1)S(1)}, bf16[128,128]{1,0:T(8,128)(2,1)}, u32[]{:S(2)}) copy-start(bf16[128,128]{1,0:T(8,128)(2,1)} %up_ref.1) | copy-start | bytes 98308
  4.1 31.3 %copy-start.7 = (s32[4]{0:T(128)S(1)}, s32[4]{0:T(128)}, u32[]{:S(2)}) copy-start(s32[4]{0:T(128)} %c_len.1) | copy-start | bytes 52
  4.1 31.3 %copy-start.8 = (s32[4]{0:T(128)S(1)}, s32[4]{0:T(128)}, u32[]{:S(2)}) copy-start(s32[4]{0:T(128)} %p_len.1) | copy-start | bytes 52
  4.3 9.9 %collective-permute-start = (bf16[16,1152]{1,0:T(8,128)(2,1)S(1)}, bf16[16,1152]{1,0:T(8,128)(2,1)S(1)}, u32[]{:S(2)}, u32[]{:S(2)}) collective-permute-start(bf16[16,1152]{1,0:T(8,128)(2,1)S(1)} %fold_ranks.1), channel_id=1, source_target_pairs={{0,8},{4,12},{8,0},{12,4},{16,24},{20,28},{24,16},{28,20},{1,9},{5... | collective-permute-start | bytes 110600 | tf_op jit(solution)/shard_map/ppermute | solution.py:152
  7.3 7.6 %collective-permute-start.1 = (bf16[16,1152]{1,0:T(8,128)(2,1)S(1)}, bf16[16,1152]{1,0:T(8,128)(2,1)S(1)}, u32[]{:S(2)}, u32[]{:S(2)}) collective-permute-start(bf16[16,1152]{1,0:T(8,128)(2,1)S(1)} %fold_ranks.1), channel_id=1, source_target_pairs={{0,16},{4,20},{8,24},{12,28},{16,0},{20,4},{24,8},{28,12},{1,17},{... | collective-permute-start | bytes 110600 | tf_op jit(solution)/shard_map/ppermute | solution.py:152
  8.8 6.2 %collective-permute-start.2 = (bf16[16,1152]{1,0:T(8,128)(2,1)S(1)}, bf16[16,1152]{1,0:T(8,128)(2,1)S(1)}, u32[]{:S(2)}, u32[]{:S(2)}) collective-permute-start(bf16[16,1152]{1,0:T(8,128)(2,1)S(1)} %fold_ranks.1), channel_id=1, source_target_pairs={{0,24},{4,28},{8,16},{12,20},{16,8},{20,12},{24,0},{28,4},{1,25},{... | collective-permute-start | bytes 110600 | tf_op jit(solution)/shard_map/ppermute | solution.py:152
  10.7 10.0 %collective-permute-start.6 = (bf16[576,256]{1,0:T(8,128)(2,1)S(1)}, bf16[576,256]{1,0:T(8,128)(2,1)S(1)}, u32[]{:S(2)}, u32[]{:S(2)}) collective-permute-start(bf16[576,256]{1,0:T(8,128)(2,1)S(1)} %pad_maximum_fusion.refs_0_), channel_id=1, source_target_pairs={{0,8},{4,12},{8,0},{12,4},{16,24},{20,28},{24,16},{28,20},{1,9},{5... | collective-permute-start | bytes 884744 | tf_op jit(solution)/shard_map/ppermute | solution.py:152
  12.7 15.5 %collective-permute-start.10 = (bf16[576,256]{1,0:T(8,128)(2,1)S(1)}, bf16[576,256]{1,0:T(8,128)(2,1)S(1)}, u32[]{:S(2)}, u32[]{:S(2)}) collective-permute-start(bf16[576,256]{1,0:T(8,128)(2,1)S(1)} %pad_maximum_fusion.refs_0_), channel_id=1, source_target_pairs={{0,16},{4,20},{8,24},{12,28},{16,0},{20,4},{24,8},{28,12},{1,17},{... | collective-permute-start | bytes 884744 | tf_op jit(solution)/shard_map/ppermute | solution.py:152
  14.3 12.4 %collective-permute-start.11 = (bf16[576,256]{1,0:T(8,128)(2,1)S(1)}, bf16[576,256]{1,0:T(8,128)(2,1)S(1)}, u32[]{:S(2)}, u32[]{:S(2)}) collective-permute-start(bf16[576,256]{1,0:T(8,128)(2,1)S(1)} %pad_maximum_fusion.1.refs_1_), channel_id=1, source_target_pairs={{0,16},{4,20},{8,24},{12,28},{16,0},{20,4},{24,8},{28,12},{1,17},{... | collective-permute-start | bytes 884744 | tf_op jit(solution)/shard_map/ppermute | solution.py:152
  14.9 13.9 %collective-permute-start.7 = (bf16[576,256]{1,0:T(8,128)(2,1)S(1)}, bf16[576,256]{1,0:T(8,128)(2,1)S(1)}, u32[]{:S(2)}, u32[]{:S(2)}) collective-permute-start(bf16[576,256]{1,0:T(8,128)(2,1)S(1)} %pad_maximum_fusion.1.refs_1_), channel_id=1, source_target_pairs={{0,8},{4,12},{8,0},{12,4},{16,24},{20,28},{24,16},{28,20},{1,9},{5... | collective-permute-start | bytes 884744 | tf_op jit(solution)/shard_map/ppermute | solution.py:152
  15.0 1.4 %collective-permute-start.3 = (bf16[64,1152]{1,0:T(8,128)(2,1)S(1)}, bf16[64,1152]{1,0:T(8,128)(2,1)S(1)}, u32[]{:S(2)}, u32[]{:S(2)}) collective-permute-start(bf16[64,1152]{1,0:T(8,128)(2,1)S(1)} %pad_maximum_fusion.3.t_same), channel_id=1, source_target_pairs={{0,4},{4,0},{8,12},{12,8},{16,20},{20,16},{24,28},{28,24},{1,5},{5... | collective-permute-start | bytes 442376 | tf_op jit(solution)/shard_map/ppermute | solution.py:152
  16.4 12.3 %collective-permute-start.4 = (bf16[576,256]{1,0:T(8,128)(2,1)S(1)}, bf16[576,256]{1,0:T(8,128)(2,1)S(1)}, u32[]{:S(2)}, u32[]{:S(2)}) collective-permute-start(bf16[576,256]{1,0:T(8,128)(2,1)S(1)} %pad_maximum_fusion.refs_0_), channel_id=1, source_target_pairs={{0,4},{4,0},{8,12},{12,8},{16,20},{20,16},{24,28},{28,24},{1,5},{5... | collective-permute-start | bytes 884744 | tf_op jit(solution)/shard_map/ppermute | solution.py:152
  20.7 8.5 %collective-permute-start.5 = (bf16[576,256]{1,0:T(8,128)(2,1)S(1)}, bf16[576,256]{1,0:T(8,128)(2,1)S(1)}, u32[]{:S(2)}, u32[]{:S(2)}) collective-permute-start(bf16[576,256]{1,0:T(8,128)(2,1)S(1)} %pad_maximum_fusion.1.refs_1_), channel_id=1, source_target_pairs={{0,4},{4,0},{8,12},{12,8},{16,20},{20,16},{24,28},{28,24},{1,5},{5... | collective-permute-start | bytes 884744 | tf_op jit(solution)/shard_map/ppermute | solution.py:152
  26.7 6.7 %collective-permute-start.14 = (bf16[576,256]{1,0:T(8,128)(2,1)S(1)}, bf16[576,256]{1,0:T(8,128)(2,1)S(1)}, u32[]{:S(2)}, u32[]{:S(2)}) collective-permute-start(bf16[576,256]{1,0:T(8,128)(2,1)S(1)} %collective-permute-done.6.refs_4_), channel_id=1, source_target_pairs={{0,16},{4,20},{8,24},{12,28},{16,0},{20,4},{24,8},{28,12},{1,17},{... | collective-permute-start | bytes 884744 | tf_op jit(solution)/shard_map/ppermute | solution.py:152
  28.2 6.7 %collective-permute-start.15 = (bf16[576,256]{1,0:T(8,128)(2,1)S(1)}, bf16[576,256]{1,0:T(8,128)(2,1)S(1)}, u32[]{:S(2)}, u32[]{:S(2)}) collective-permute-start(bf16[576,256]{1,0:T(8,128)(2,1)S(1)} %collective-permute-done.11.refs_9_), channel_id=1, source_target_pairs={{0,8},{4,12},{8,0},{12,4},{16,24},{20,28},{24,16},{28,20},{1,9},{5... | collective-permute-start | bytes 884744 | tf_op jit(solution)/shard_map/ppermute | solution.py:152
  28.8 6.2 %collective-permute-start.13 = (bf16[576,256]{1,0:T(8,128)(2,1)S(1)}, bf16[576,256]{1,0:T(8,128)(2,1)S(1)}, u32[]{:S(2)}, u32[]{:S(2)}) collective-permute-start(bf16[576,256]{1,0:T(8,128)(2,1)S(1)} %collective-permute-done.11.refs_9_), channel_id=1, source_target_pairs={{0,4},{4,0},{8,12},{12,8},{16,20},{20,16},{24,28},{28,24},{1,5},{5... | collective-permute-start | bytes 884744 | tf_op jit(solution)/shard_map/ppermute | solution.py:152
  28.8 11.3 %collective-permute-start.8 = (bf16[576,256]{1,0:T(8,128)(2,1)S(1)}, bf16[576,256]{1,0:T(8,128)(2,1)S(1)}, u32[]{:S(2)}, u32[]{:S(2)}) collective-permute-start(bf16[576,256]{1,0:T(8,128)(2,1)S(1)} %collective-permute-done.6.refs_4_), channel_id=1, source_target_pairs={{0,4},{4,0},{8,12},{12,8},{16,20},{20,16},{24,28},{28,24},{1,5},{5... | collective-permute-start | bytes 884744 | tf_op jit(solution)/shard_map/ppermute | solution.py:152
  29.3 10.8 %collective-permute-start.12 = (bf16[576,256]{1,0:T(8,128)(2,1)S(1)}, bf16[576,256]{1,0:T(8,128)(2,1)S(1)}, u32[]{:S(2)}, u32[]{:S(2)}) collective-permute-start(bf16[576,256]{1,0:T(8,128)(2,1)S(1)} %collective-permute-done.10.refs_8_), channel_id=1, source_target_pairs={{0,4},{4,0},{8,12},{12,8},{16,20},{20,16},{24,28},{28,24},{1,5},{5... | collective-permute-start | bytes 884744 | tf_op jit(solution)/shard_map/ppermute | solution.py:152
  33.4 6.7 %collective-permute-start.9 = (bf16[576,256]{1,0:T(8,128)(2,1)S(1)}, bf16[576,256]{1,0:T(8,128)(2,1)S(1)}, u32[]{:S(2)}, u32[]{:S(2)}) collective-permute-start(bf16[576,256]{1,0:T(8,128)(2,1)S(1)} %collective-permute-done.7.refs_5_), channel_id=1, source_target_pairs={{0,4},{4,0},{8,12},{12,8},{16,20},{20,16},{24,28},{28,24},{1,5},{5... | collective-permute-start | bytes 884744 | tf_op jit(solution)/shard_map/ppermute | solution.py:152
  34.9 5.1 %collective-permute-start.16 = (bf16[576,256]{1,0:T(8,128)(2,1)S(1)}, bf16[576,256]{1,0:T(8,128)(2,1)S(1)}, u32[]{:S(2)}, u32[]{:S(2)}) collective-permute-start(bf16[576,256]{1,0:T(8,128)(2,1)S(1)} %collective-permute-done.14.refs_12_), channel_id=1, source_target_pairs={{0,4},{4,0},{8,12},{12,8},{16,20},{20,16},{24,28},{28,24},{1,5},{5... | collective-permute-start | bytes 884744 | tf_op jit(solution)/shard_map/ppermute | solution.py:152
  34.9 5.2 %collective-permute-start.17 = (bf16[576,256]{1,0:T(8,128)(2,1)S(1)}, bf16[576,256]{1,0:T(8,128)(2,1)S(1)}, u32[]{:S(2)}, u32[]{:S(2)}) collective-permute-start(bf16[576,256]{1,0:T(8,128)(2,1)S(1)} %collective-permute-done.15.refs_13_), channel_id=1, source_target_pairs={{0,4},{4,0},{8,12},{12,8},{16,20},{20,16},{24,28},{28,24},{1,5},{5... | collective-permute-start | bytes 884744 | tf_op jit(solution)/shard_map/ppermute | solution.py:152
  35.5 1.6 %copy-start.1 = (bf16[4,32,8192]{2,1,0:T(8,128)(2,1)S(1)}, bf16[4,32,8192]{2,1,0:T(8,128)(2,1)}, u32[]{:S(2)}) copy-start(bf16[4,32,8192]{2,1,0:T(8,128)(2,1)} %param.15) | copy-start | bytes 6291460
  42.7 4.5 %collective-permute-start.18 = (bf16[4,8192]{1,0:T(4,128)(2,1)S(1)}, bf16[4,8192]{1,0:T(4,128)(2,1)S(1)}, u32[]{:S(2)}, u32[]{:S(2)}) collective-permute-start(bf16[4,8192]{1,0:T(4,128)(2,1)S(1)} %get-tuple-element.9), channel_id=1, source_target_pairs={{0,8},{4,12},{8,0},{12,4},{16,24},{20,28},{24,16},{28,20},{1,9},{5... | collective-permute-start | bytes 196616 | tf_op jit(solution)/shard_map/ppermute | solution.py:152
  43.3 5.6 %collective-permute-start.19 = (bf16[4,8192]{1,0:T(4,128)(2,1)S(1)}, bf16[4,8192]{1,0:T(4,128)(2,1)S(1)}, u32[]{:S(2)}, u32[]{:S(2)}) collective-permute-start(bf16[4,8192]{1,0:T(4,128)(2,1)S(1)} %get-tuple-element.9), channel_id=1, source_target_pairs={{0,16},{4,20},{8,24},{12,28},{16,0},{20,4},{24,8},{28,12},{1,17},{... | collective-permute-start | bytes 196616 | tf_op jit(solution)/shard_map/ppermute | solution.py:152
  43.6 5.2 %collective-permute-start.20 = (bf16[4,8192]{1,0:T(4,128)(2,1)S(1)}, bf16[4,8192]{1,0:T(4,128)(2,1)S(1)}, u32[]{:S(2)}, u32[]{:S(2)}) collective-permute-start(bf16[4,8192]{1,0:T(4,128)(2,1)S(1)} %get-tuple-element.9), channel_id=1, source_target_pairs={{0,24},{4,28},{8,16},{12,20},{16,8},{20,12},{24,0},{28,4},{1,25},{... | collective-permute-start | bytes 196616 | tf_op jit(solution)/shard_map/ppermute | solution.py:152
  49.0 1.6 %collective-permute-start.21 = (bf16[16,8192]{1,0:T(8,128)(2,1)S(1)}, bf16[16,8192]{1,0:T(8,128)(2,1)S(1)}, u32[]{:S(2)}, u32[]{:S(2)}) collective-permute-start(bf16[16,8192]{1,0:T(8,128)(2,1)S(1)} %pad_maximum_fusion.2.same_ref), channel_id=1, source_target_pairs={{0,4},{4,0},{8,12},{12,8},{16,20},{20,16},{24,28},{28,24},{1,5},{5... | collective-permute-start | bytes 786440 | tf_op jit(solution)/shard_map/ppermute | solution.py:152
  50.6 0.8 %copy-start.5 = (bf16[4,8192]{1,0:T(4,128)(2,1)S(1)}, bf16[4,8192]{1,0:T(4,128)(2,1)}, u32[]{:S(2)}) copy-start(bf16[4,8192]{1,0:T(4,128)(2,1)} %get-tuple-element.5.c_ref) | copy-start | bytes 196612

commit v2 on v1

v2 whole, which is shorter than its diff:
```python
import functools

import jax
import jax.numpy as jnp
from jax import lax
from jax.experimental import pallas as pl
from jax.experimental.pallas import tpu as pltpu
from jax.sharding import PartitionSpec as P

eps_mean = 1e-06
LAST = (((1,), (1,)), ((), ()))
VMEM = pl.BlockSpec(memory_space=pltpu.VMEM)
SMEM = pl.BlockSpec(memory_space=pltpu.SMEM)
HBM = pl.BlockSpec(memory_space=pltpu.HBM)
MIB = 1 << 20


def in_hbm(*arrays):
    return tuple(pltpu.with_memory_space_constraint(a, pltpu.HBM) for a in arrays)


def dot(a, b):
    return jnp.dot(a, b, preferred_element_type=jnp.float32)


def dot_last(a, b):
    return lax.dot_general(a, b, LAST, preferred_element_type=jnp.float32)


def split_two(x):
    high = x.astype(jnp.bfloat16)
    return high, (x - high.astype(jnp.float32)).astype(jnp.bfloat16)


def partner(me, kind, other):
    odd = (me % 2) ^ other
    return me ^ other ^ (0, 2 + 2 * odd, 4 - 2 * odd, 6)[kind]


def pack_kernel(
    halves, down_hbm, up_hbm, rank_down_hbm, rank_up_hbm, in_hbm, out_hbm, *refs
):
    packed, own_ref, (down_ref, up_ref, rank_down_ref, rank_up_ref, sems) = (
        refs[:halves], refs[halves], refs[halves + 1 :],
    )
    s_rows, o_rows = in_hbm.shape[0] // halves, out_hbm.shape[0] // halves
    moves = [
        (down_hbm, down_ref),
        (up_hbm, up_ref),
        (rank_down_hbm, rank_down_ref),
        (rank_up_hbm, rank_up_ref),
    ]
    for h, piece in enumerate(packed):
        for to, at in ((piece, 0), (own_ref, h * (s_rows + o_rows))):
            moves.append((in_hbm.at[pl.ds(h * s_rows, s_rows)], to.at[pl.ds(at, s_rows)]))
            moves.append((out_hbm.at[pl.ds(h * o_rows, o_rows)], to.at[pl.ds(at + s_rows, o_rows)]))
    copies = [pltpu.make_async_copy(a, b, sems.at[i]) for i, (a, b) in enumerate(moves)]
    for copy in copies:
        copy.start()
    for copy in copies[:4]:
        copy.wait()
    down_table = dot_last(rank_up_ref[...], down_ref[...]).astype(jnp.bfloat16)
    up_table = dot_last(rank_down_ref[...], up_ref[...]).astype(jnp.bfloat16)
    ks, width = up_table.shape
    lanes = own_ref.shape[1]
    blocks = down_table.shape[1] // lanes
    at = s_rows + o_rows
    for piece in packed:
        for b in range(blocks):
            piece[at + b * ks : at + (b + 1) * ks, :] = down_table[:, b * lanes : (b + 1) * lanes]
        piece[at + blocks * ks : at + (blocks + 1) * ks, :] = jnp.zeros((ks, lanes), jnp.bfloat16)
        piece[at + blocks * ks : at + (blocks + 1) * ks, :width] = up_table
    for copy in copies[4:]:
        copy.wait()


def load_kernel(
    seq, ks, c_x_hbm, c_m_hbm, c_len_hbm, p_x_hbm, p_m_hbm, p_len_hbm,
    x_ref, m_ref, live_ref, c_len, p_len, sems,
):
    rows = c_x_hbm.shape[0]
    moves = (
        (c_len_hbm, c_len), (p_len_hbm, p_len),
        (c_m_hbm, m_ref.at[pl.ds(0, rows)]), (p_m_hbm, m_ref.at[pl.ds(rows, rows)]),
        (c_x_hbm, x_ref.at[pl.ds(0, rows)]), (p_x_hbm, x_ref.at[pl.ds(rows, rows)]),
    )
    copies = [pltpu.make_async_copy(a, b, sems.at[i]) for i, (a, b) in enumerate(moves)]
    for copy in copies:
        copy.start()
    for copy in copies[:2]:
        copy.wait()
    height, width = live_ref.shape
    rows = lax.broadcasted_iota(jnp.int32, (height, width), 0)
    cols = lax.broadcasted_iota(jnp.int32, (height, width), 1)
    live = jnp.zeros((height, width), jnp.bool_)
    count = width // ks
    for e in range(count):
        length = c_len[e] if e < count // 2 else p_len[e - count // 2]
        live = live | (
            (cols >= e * ks)
            & (cols < (e + 1) * ks)
            & (rows >= e * seq)
            & (rows < e * seq + length)
        )
    live_ref[...] = live.astype(jnp.float32)
    for copy in copies[2:]:
        copy.wait()


def rows_kernel(n, halves, x, m, live_ref, t_same, t_other, left_ref, right_ref):
    me = lax.axis_index("fsdp")
    model, value = x.shape[1], m.shape[1]
    kd, ku = model // n, value // n
    lanes = t_same.shape[1]
    blocks = kd // lanes
    ks = t_same.shape[0] // (n // 2) // (blocks + 1)
    held = [
        (partner(me, kind, other), (t_same, t_other)[other], kind * (blocks + 1) * ks)
        for other in range(2)
        for kind in range(n // 2)
    ]
    part = ku // halves
    total = left_ref.shape[0] // 2

    def spread(small):
        small = small.astype(jnp.bfloat16).astype(jnp.float32)
        wide = jnp.concatenate([small] * (live_ref.shape[1] // ks), axis=1)
        return jnp.where(live_ref[...] > 0, wide, 0.0).T.astype(jnp.bfloat16)

    left_small = 0.0
    right_small = 0.0
    for j, table, at in held:
        up = table[at + blocks * ks : at + (blocks + 1) * ks, :ku]
        left_small += dot_last(m[:, pl.ds(pl.multiple_of(j * ku, ku), ku)], up)
    left_wide = spread(left_small)
    for j, table, at in held:
        for b in range(blocks):
            cols = pl.ds(pl.multiple_of(j * kd + b * lanes, lanes), lanes)
            right_small += dot_last(x[:, cols], table[at + b * ks : at + (b + 1) * ks, :])
    for b in range(n):
        high, low = split_two(dot(left_wide, x[:, b * kd : (b + 1) * kd]))
        left_ref[:total, b * kd : (b + 1) * kd] = high
        left_ref[total:, b * kd : (b + 1) * kd] = low
    high, low = split_two(dot(spread(right_small), m[...]))
    for b in range(n * halves):
        right_ref[b, :total, :] = high[:, b * part : (b + 1) * part]
        right_ref[b, total:, :] = low[:, b * part : (b + 1) * part]


def products(places, s_rows, halves, left_ref, right_ref, refs):
    me = lax.axis_index("fsdp")
    o_rows = right_ref.shape[2]
    left = 0.0
    right = 0.0
    for ref, row, kind, other, half in places:
        at = partner(me, kind, other) * halves + half
        cols = pl.ds(pl.multiple_of(at * s_rows, s_rows), s_rows)
        left += dot(left_ref[:, cols], refs[ref][row : row + s_rows, :])
        right += dot(right_ref[at], refs[ref][row + s_rows : row + s_rows + o_rows, :])
    total = left.shape[0] // 2
    return left[:total] + left[total:], right[:total] + right[total:]


def early_kernel(places, s_rows, halves, left_ref, right_ref, *refs):
    left, right = products(places, s_rows, halves, left_ref, right_ref, refs[:-1])
    refs[-1][0] = left
    refs[-1][1] = right


def join_kernel(places, ks, s_rows, halves, left_ref, right_ref, sums_ref, *refs):
    refs, (c_out, c_keep, p_out, left_scratch, right_scratch) = refs[:-5], refs[-5:]
    left, right = products(places, s_rows, halves, left_ref, right_ref, refs)
    left += sums_ref[0]
    right += sums_ref[1]
    total = left.shape[0]
    count, cols = total // ks, left.shape[1]
    left = left.reshape(count, ks, cols)
    right = right.reshape(count, ks, cols)
    mean = jnp.sum(left * left + right * right, axis=(1, 2), keepdims=True) / (2 * ks * cols)
    scale = lax.rsqrt(mean + eps_mean)
    lanes = left_scratch.shape[2]
    for scratch, value in ((left_scratch, left), (right_scratch, right)):
        scaled = (value * scale).reshape(total, cols)
        for b in range(cols // lanes):
            scratch[b] = scaled[:, b * lanes : (b + 1) * lanes]
    half = count // 2
    for side, outs in enumerate(((c_out, c_keep), (p_out,))):
        for t, scratch in enumerate((left_scratch, right_scratch)):
            for r in range(ks):
                for b in range(cols // lanes):
                    at = (t * ks + r) * cols + b * lanes
                    rows = pl.ds(side * half * ks + r, half, stride=ks)
                    value = scratch[b, rows, :].astype(jnp.bfloat16)
                    for out in outs:
                        out[:, at : at + lanes] = value


def score_kernel(order, c_ref, same_ref, other_ref, out_ref):
    me = lax.axis_index("fsdp")
    feats = c_ref[...]
    mixed = jnp.concatenate([dot_last(feats, same_ref[...]), dot_last(feats, other_ref[...])], axis=1)
    width = mixed.shape[1]
    per = width // len(order)
    rows = lax.broadcasted_iota(jnp.int32, (width, width), 0)
    cols = lax.broadcasted_iota(jnp.int32, (width, width), 1)
    target = jnp.zeros((width, width), jnp.int32)
    for g, k in enumerate(order):
        target = jnp.where(rows // per == g, (me ^ k) * per + rows % per, target)
    place = (target == cols).astype(jnp.float32)
    out = lax.dot_general(
        mixed, place, (((1,), (0,)), ((), ())),
        preferred_element_type=jnp.float32, precision=lax.Precision.HIGHEST,
    )
    out_ref[...] = out / feats.shape[1]


def swap(x, k, axis, size):
    return lax.ppermute(x, axis, [(i, i ^ k) for i in range(size)])


def fast_body(n, c_x, c_m, c_len, p_x, p_m, p_len, down, up, sketch_in, sketch_out, rank_down, rank_up):
    examples, seq, model = c_x.shape
    value = c_m.shape[2]
    ks, kp = rank_down.shape[1], sketch_in.shape[1]
    s_shard, o_shard = sketch_in.shape[0], sketch_out.shape[0]
    sw = functools.partial(swap, axis="fsdp", size=n)
    order = (0, 2, 4, 6, 1, 3, 5, 7)
    halves = 2
    s_rows, o_rows = s_shard // halves, o_shard // halves

    def along(x, first, second):
        return lax.ppermute(x, "fsdp", [(i, i ^ (second if i % 2 else first)) for i in range(n)])

    along_u = functools.partial(along, first=2, second=4)
    along_v = functools.partial(along, first=4, second=2)
    half = s_rows + o_rows
    t_rows = (s_shard // kp + 1) * ks

    def array(rows, like=sketch_in):
        return jax.ShapeDtypeStruct((rows, like.shape[1]), like.dtype)

    h0, h1, own = pl.pallas_call(
        functools.partial(pack_kernel, halves),
        out_shape=(array(half + t_rows), array(half + t_rows), array(2 * half)),
        in_specs=[HBM] * 6,
        out_specs=(VMEM,) * 3,
        scratch_shapes=[
            pltpu.VMEM(down.shape, down.dtype),
            pltpu.VMEM(up.shape, up.dtype),
            pltpu.VMEM(rank_down.shape[::-1], rank_down.dtype),
            pltpu.VMEM(rank_up.shape[::-1], rank_up.dtype),
            pltpu.SemaphoreType.DMA((4 + 4 * halves,)),
        ],
        compiler_params=pltpu.CompilerParams(vmem_limit_bytes=8 * MIB),
        name="pack_weights",
    )(*in_hbm(down, up, rank_down.T, rank_up.T, sketch_in, sketch_out))

    flat = (examples * seq, model)
    flat_m = (examples * seq, value)
    total = 2 * examples * ks
    rows = pl.pallas_call(
        functools.partial(load_kernel, seq, ks),
        out_shape=(
            jax.ShapeDtypeStruct((2 * examples * seq, model), c_x.dtype),
            jax.ShapeDtypeStruct((2 * examples * seq, value), c_m.dtype),
            jax.ShapeDtypeStruct((2 * examples * seq, total), jnp.float32),
        ),
        in_specs=[HBM] * 6,
        out_specs=(VMEM,) * 3,
        scratch_shapes=[
            pltpu.SMEM(c_len.shape, c_len.dtype),
            pltpu.SMEM(p_len.shape, p_len.dtype),
            pltpu.SemaphoreType.DMA((6,)),
        ],
        compiler_params=pltpu.CompilerParams(vmem_limit_bytes=8 * MIB),
        name="load_rows",
    )(*in_hbm(c_x.reshape(flat), c_m.reshape(flat_m), c_len, p_x.reshape(flat), p_m.reshape(flat_m), p_len))

    u0, v1 = along_u(h0), along_v(h1)
    c_own = sw(own, 1)
    u1, v0 = along_u(h1[:half]), along_v(h0[:half])
    u0, v1, c_own, rows = lax.optimization_barrier((u0, v1, c_own, rows))
    t_d = along_v(u0[half:])
    d0, d1 = along_v(u0[:half]), along_u(v1[:half])
    t_same = jnp.concatenate([h0[half:], u0[half:], v1[half:], t_d])
    t_other = sw(t_same, 1)
    u0, v1 = u0[:half], v1[:half]
    t_same, u1, v0 = lax.optimization_barrier((t_same, u1, v0))
    c_uv = sw(jnp.concatenate([u0, u1, v0, v1]), 1)

    left, right = pl.pallas_call(
        functools.partial(rows_kernel, n, halves),
        out_shape=(
            jax.ShapeDtypeStruct((2 * total, model), jnp.bfloat16),
            jax.ShapeDtypeStruct((n * halves, 2 * total, o_rows), jnp.bfloat16),
        ),
        in_specs=[VMEM] * 5,
        out_specs=(VMEM, VMEM),
        compiler_params=pltpu.CompilerParams(vmem_limit_bytes=16 * MIB),
        name="example_rows",
    )(*rows, t_same, t_other)

    early = (
        (0, 0, 0, 0, 0), (1, 0, 0, 0, 1), (2, 0, 0, 1, 0), (2, half, 0, 1, 1),
        (3, 0, 1, 0, 0), (4, 0, 1, 0, 1), (5, 0, 2, 0, 0), (6, 0, 2, 0, 1),
        (7, 0, 1, 1, 0), (7, half, 1, 1, 1), (7, 2 * half, 2, 1, 0), (7, 3 * half, 2, 1, 1),
    )
    sums = pl.pallas_call(
        functools.partial(early_kernel, early, s_rows, halves),
        out_shape=jax.ShapeDtypeStruct((2, total, kp), jnp.float32),
        in_specs=[VMEM] * 10,
        out_specs=VMEM,
        compiler_params=pltpu.CompilerParams(vmem_limit_bytes=16 * MIB),
        name="early_products",
    )(left, right, h0, h1, c_own, u0, u1, v0, v1, c_uv)

    sums, d0, d1 = lax.optimization_barrier((sums, d0, d1))
    late = ((0, 0, 3, 0, 0), (1, 0, 3, 0, 1), (2, 0, 3, 1, 0), (3, 0, 3, 1, 1))
    feats = jax.ShapeDtypeStruct((examples, 2 * ks * kp), jnp.bfloat16)
    c_feat, c_keep, p_feat = pl.pallas_call(
        functools.partial(join_kernel, late, ks, s_rows, halves),
        out_shape=(feats, feats, feats),
        in_specs=[VMEM] * 7,
        out_specs=(VMEM, VMEM, VMEM),
        scratch_shapes=[pltpu.VMEM((kp // 128, total, 128), jnp.float32)] * 2,
        compiler_params=pltpu.CompilerParams(vmem_limit_bytes=16 * MIB),
        name="join_features",
    )(left, right, sums, d0, d1, sw(d0, 1), sw(d1, 1))

    same = jnp.concatenate([p_feat, sw(p_feat, 2), sw(p_feat, 4), sw(p_feat, 6)])
    other = sw(same, 1)
    scores = pl.pallas_call(
        functools.partial(score_kernel, order),
        out_shape=jax.ShapeDtypeStruct((examples, n * examples), jnp.float32),
        in_specs=[VMEM] * 3,
        out_specs=VMEM,
        compiler_params=pltpu.CompilerParams(vmem_limit_bytes=8 * MIB),
        name="score_rows",
    )(c_keep, same, other)
    return scores, c_feat


def plain_features(x, m, lengths, down, up, sketch_in, sketch_out, rank_down, rank_up):
    examples, seq, model = x.shape
    ks, kp = rank_down.shape[1], sketch_in.shape[1]
    live = (lax.broadcasted_iota(jnp.int32, (examples, seq), 1) < lengths[:, None]).astype(m.dtype)
    masked = (m * live[:, :, None]).reshape(examples * seq, -1)
    rows = x.reshape(examples * seq, model)
    grad_rows = dot(masked, up).astype(jnp.bfloat16)
    outward = dot(masked, sketch_out).astype(jnp.bfloat16)
    down_round = dot(rows, down).astype(jnp.bfloat16)
    inward = dot(rows, sketch_in).astype(jnp.bfloat16)
    left_small = dot(grad_rows, rank_down).astype(jnp.bfloat16)
    right_small = dot(down_round, rank_up).astype(jnp.bfloat16)

    def outer(small, wide):
        return jnp.einsum(
            "esk,esp->ekp",
            small.reshape(examples, seq, ks),
            wide.reshape(examples, seq, kp),
            preferred_element_type=jnp.float32,
        )

    joined = jnp.concatenate([outer(left_small, inward), outer(right_small, outward)], axis=1)
    joined = joined.reshape(examples, 2 * ks * kp)
    scale = lax.rsqrt(jnp.mean(joined * joined, axis=1, keepdims=True) + eps_mean)
    return (joined * scale).astype(jnp.bfloat16)


def plain_body(c_x, c_m, c_len, p_x, p_m, p_len, down, up, sketch_in, sketch_out, rank_down, rank_up):
    weights = [
        lax.all_gather(w, "fsdp", axis=0, tiled=True) for w in (down, up, sketch_in, sketch_out)
    ]
    p_feat = plain_features(p_x, p_m, p_len, *weights, rank_down, rank_up)
    c_feat = plain_features(c_x, c_m, c_len, *weights, rank_down, rank_up)
    every = lax.all_gather(p_feat, "fsdp", axis=0, tiled=True)
    return dot(c_feat, every.T) / c_feat.shape[1], c_feat


def solution(mesh):
    n = mesh.shape["fsdp"]
    rows = P(("dp", "fsdp"), None)
    cube = P(("dp", "fsdp"), None, None)
    line = P(("dp", "fsdp"))
    shard = P("fsdp", None)
    in_specs = (cube, cube, line, cube, cube, line, shard, shard, shard, shard, P(), P())

    def body(*args):
        if n == 1 << 3:
            return fast_body(n, *args)
        return plain_body(*args)

    return jax.shard_map(body, mesh=mesh, in_specs=in_specs, out_specs=(rows, rows), check_vma=False)
```

time: 53 us -> 44 us (0.83)
  local copies, waits for them, and re-layouts: 7.76 us -> 0.1 us
  Pallas kernels: 6.93 us -> 10.6 us
  starting transfers between devices: 15.7 us -> 13 us
  waiting for transfers between devices: 21.2 us -> 19.2 us
    ppermute x22 -> x9, waiting for transfers between devices: 21.2 us -> 8.06 us  [swap(): return lax.ppermute(x, axis, [(i, i ^ k) for i in range(size)])]
    ppermute x0 -> x7, waiting for transfers between devices: none -> 11.2 us  [along(): lax.ppermute(x, 'fsdp', [(i, i ^ (second if i % 2 else first)) for i in r...]
    ppermute x22 -> x9, starting transfers between devices: 15.7 us -> 4.73 us  [swap(): return lax.ppermute(x, axis, [(i, i ^ k) for i in range(size)])]
    ppermute x0 -> x7, starting transfers between devices: none -> 8.23 us  [along(): lax.ppermute(x, 'fsdp', [(i, i ^ (second if i % 2 else first)) for i in r...]
    unnamed x20 -> x0, local copies, waits for them, and re-layouts: 5.91 us -> none
    pallas_call x3 -> x5, Pallas kernels: 5.79 us -> 9.41 us  [the longest x1 2.72 us: fast_body(): pl.pallas_call(functools.partial(rows_kernel, n, halves), out_shape=(jax....]
    slice x2 -> x7, local copies, waits for them, and re-layouts: 1.85 us -> 0.1 us  [the longest x2 0.04 us: fast_body(): u0, v1 = (u0[:half], v1[:half])]
  transfers between devices with their start and end apart: 22 -> 16, of which waited for: 8 -> 11; matrix products, arithmetic and copies ran while one was open for 4% -> 0% of each run, Pallas kernels for 6% -> 15%
where the time goes in v2:
time: 44 us; the launch traced here: 43.8 us
  waiting for transfers between devices  19.2 us (44%)
  starting transfers between devices  13 us (30%)
  Pallas kernels  10.6 us (24%)
  between operations  0.77 us (2%)
    ppermute x7, waiting for transfers between devices, along(): lax.ppermute(x, 'fsdp', [(i, i ^ (second if i % 2 else first)) for i in r...  11.2 us
    ppermute x7, starting transfers between devices, along(): lax.ppermute(x, 'fsdp', [(i, i ^ (second if i % 2 else first)) for i in r...  8.23 us
    ppermute x9, waiting for transfers between devices, swap(): return lax.ppermute(x, axis, [(i, i ^ k) for i in range(size)])  8.06 us
    ppermute x9, starting transfers between devices, swap(): return lax.ppermute(x, axis, [(i, i ^ k) for i in range(size)])  4.73 us
    pallas_call x1, Pallas kernels, fast_body(): pl.pallas_call(functools.partial(rows_kernel, n, halves), out_shape=(jax....  2.72 us
    pallas_call x1, Pallas kernels, fast_body(): pl.pallas_call(functools.partial(load_kernel, seq, ks), out_shape=(jax.Sh...  2.45 us
    pallas_call x1, Pallas kernels, fast_body(): pl.pallas_call(functools.partial(pack_kernel, halves), out_shape=(array(h...  1.47 us
    pallas_call x1, Pallas kernels, fast_body(): pl.pallas_call(functools.partial(early_kernel, early, s_rows, halves), ou...  1.41 us
  transfers between devices with their start and end apart: 16, of which 11 were waited for; matrix products, arithmetic and copies ran while one was open for 0% of the time, Pallas kernels for 15%

profile of v2, /device:TPU:0, one launch (start us, length us, event | category | flops | bytes accessed | tf_op | source)
XLA Modules:
  0.0 43.8 jit_solution(1898346400345955610)
XLA Ops:
  0.6 1.5 %pack_weights.1 = (bf16[656,256]{1,0:T(8,128)(2,1)S(1)}, bf16[656,256]{1,0:T(8,128)(2,1)S(1)}, bf16[1152,256]{1,0:T(8,128)(2,1)S(1)}) custom-call(bf16[1024,128]{1,0:T(8,128)(2,1)} %down_hbm.1, bf16[128,128]{1,0:T(8,128)(2,1)} %up_hbm.1, bf16[16,128]{1,0:T(8,128)(2,1)} %bitcast.10, bf16[16,128]{1,0:T(8,128)(2,1)} %bitcast.11, bf16[1024,256]{1,0:T(8,128)(2,1)} %in_hbm.1, ...), custom_call_target="tpu_custom_call" | custom-call | tf_op jit(solution)/shard_map/pack_weights/pallas_call | solution.py:242
  2.1 0.5 %collective-permute-start.2 = (bf16[1152,256]{1,0:T(8,128)(2,1)S(1)}, bf16[1152,256]{1,0:T(8,128)(2,1)S(1)}, u32[]{:S(2)}, u32[]{:S(2)}) collective-permute-start(bf16[1152,256]{1,0:T(8,128)(2,1)S(1)} %get-tuple-element.27), channel_id=1, source_target_pairs={{0,4},{4,0},{8,12},{12,8},{16,20},{20,16},{24,28},{28,24},{1,5},{5... | collective-permute-start | bytes 1769480 | tf_op jit(solution)/shard_map/ppermute | solution.py:218
  2.6 2.6 %collective-permute-start.1 = (bf16[656,256]{1,0:T(8,128)(2,1)S(1)}, bf16[656,256]{1,0:T(8,128)(2,1)S(1)}, u32[]{:S(2)}, u32[]{:S(2)}) collective-permute-start(bf16[656,256]{1,0:T(8,128)(2,1)S(1)} %get-tuple-element.26.refs_1_), channel_id=1, source_target_pairs={{0,16},{4,12},{8,24},{12,4},{16,0},{20,28},{24,8},{28,20},{1,17},{... | collective-permute-start | bytes 1007624 | tf_op jit(solution)/shard_map/ppermute | solution.py:232
  5.2 1.5 %collective-permute-start = (bf16[656,256]{1,0:T(8,128)(2,1)S(1)}, bf16[656,256]{1,0:T(8,128)(2,1)S(1)}, u32[]{:S(2)}, u32[]{:S(2)}) collective-permute-start(bf16[656,256]{1,0:T(8,128)(2,1)S(1)} %get-tuple-element.25.refs_0_), channel_id=1, source_target_pairs={{0,8},{4,20},{8,0},{12,28},{16,24},{20,4},{24,16},{28,12},{1,9},{5... | collective-permute-start | bytes 1007624 | tf_op jit(solution)/shard_map/ppermute | solution.py:232
  6.7 0.6 %collective-permute-start.5 = (bf16[576,256]{1,0:T(8,128)(2,1)S(1)}, bf16[576,256]{1,0:T(8,128)(2,1)S(1)}, u32[]{:S(2)}, u32[]{:S(2)}) collective-permute-start(bf16[576,256]{1,0:T(8,128)(2,1)S(1)} %slice.28), channel_id=1, source_target_pairs={{0,16},{4,12},{8,24},{12,4},{16,0},{20,28},{24,8},{28,20},{1,17},{... | collective-permute-start | bytes 884744 | tf_op jit(solution)/shard_map/ppermute | solution.py:232
  7.3 0.2 collective-permute-start.4
  7.5 2.5 %load_rows.1 = (bf16[256,8192]{1,0:T(8,128)(2,1)S(1)}, bf16[256,1024]{1,0:T(8,128)(2,1)S(1)}, f32[256,128]{1,0:T(8,128)S(1)}) custom-call(bf16[128,8192]{1,0:T(8,128)(2,1)} %bitcast.6, bf16[128,1024]{1,0:T(8,128)(2,1)} %bitcast.8, s32[4]{0:T(128)} %c_len_hbm.1, bf16[128,8192]{1,0:T(8,128)(2,1)} %bitcast.7, bf16[128,1024]{1,0:T(8,128)(2,1)} %bitcast.9, ...), custom_call_target="tpu_custom_call" | custom-call | tf_op jit(solution)/shard_map/load_rows/pallas_call | solution.py:261
  10.0 2.9 %collective-permute-done.1 = bf16[656,256]{1,0:T(8,128)(2,1)S(1)} collective-permute-done((bf16[656,256]{1,0:T(8,128)(2,1)S(1)}, bf16[656,256]{1,0:T(8,128)(2,1)S(1)}, u32[]{:S(2)}, u32[]{:S(2)}) %collective-permute-start.1) | collective-permute-done | bytes 335904 | tf_op jit(solution)/shard_map/ppermute | solution.py:232
  12.9 3.2 %collective-permute-done = bf16[656,256]{1,0:T(8,128)(2,1)S(1)} collective-permute-done((bf16[656,256]{1,0:T(8,128)(2,1)S(1)}, bf16[656,256]{1,0:T(8,128)(2,1)S(1)}, u32[]{:S(2)}, u32[]{:S(2)}) %collective-permute-start) | collective-permute-done | bytes 335904 | tf_op jit(solution)/shard_map/ppermute | solution.py:232
  16.2 4.4 %collective-permute-done.3 = bf16[80,256]{1,0:T(8,128)(2,1)S(1)} collective-permute-done((bf16[80,256]{1,0:T(8,128)(2,1)S(1)}, bf16[80,256]{1,0:T(8,128)(2,1)S(1)}, u32[]{:S(2)}, u32[]{:S(2)}) %collective-permute-start.3) | collective-permute-done | bytes 40992 | tf_op jit(solution)/shard_map/ppermute | solution.py:232
  20.7 0.1 pad_maximum_fusion
  20.7 0.1 collective-permute-start.7
  20.9 1.6 %collective-permute-start.9 = (bf16[576,256]{1,0:T(8,128)(2,1)S(1)}, bf16[576,256]{1,0:T(8,128)(2,1)S(1)}, u32[]{:S(2)}, u32[]{:S(2)}) collective-permute-start(bf16[576,256]{1,0:T(8,128)(2,1)S(1)} %slice.30.refs_6_), channel_id=1, source_target_pairs={{0,8},{4,20},{8,0},{12,28},{16,24},{20,4},{24,16},{28,12},{1,9},{5... | collective-permute-start | bytes 884744 | tf_op jit(solution)/shard_map/ppermute | solution.py:232
  22.5 1.7 %collective-permute-start.8 = (bf16[576,256]{1,0:T(8,128)(2,1)S(1)}, bf16[576,256]{1,0:T(8,128)(2,1)S(1)}, u32[]{:S(2)}, u32[]{:S(2)}) collective-permute-start(bf16[576,256]{1,0:T(8,128)(2,1)S(1)} %slice.29.refs_3_), channel_id=1, source_target_pairs={{0,16},{4,12},{8,24},{12,4},{16,0},{20,28},{24,8},{28,20},{1,17},{... | collective-permute-start | bytes 884744 | tf_op jit(solution)/shard_map/ppermute | solution.py:232
  24.2 1.4 %collective-permute-done.6.t_other = bf16[320,256]{1,0:T(8,128)(2,1)S(1)} collective-permute-done((bf16[320,256]{1,0:T(8,128)(2,1)S(1)}, bf16[320,256]{1,0:T(8,128)(2,1)S(1)}, u32[]{:S(2)}, u32[]{:S(2)}) %collective-permute-start.6) | collective-permute-done | bytes 163872 | tf_op jit(solution)/shard_map/ppermute | solution.py:218
  25.6 2.7 %example_rows.1 = (bf16[256,8192]{1,0:T(8,128)(2,1)S(1)}, bf16[16,256,64]{2,1,0:T(8,128)(2,1)S(1)}) custom-call(bf16[256,8192]{1,0:T(8,128)(2,1)S(1)} %get-tuple-element.31.x, bf16[256,1024]{1,0:T(8,128)(2,1)S(1)} %get-tuple-element.32.m, f32[256,128]{1,0:T(8,128)S(1)} %get-tuple-element.33.live_ref, bf16[320,256]{1,0:T(8,128)(2,1)S(1)} %pad_maximum_fusion.2.t_same, ...), custom_call_target="tpu_custom_call" | custom-call | tf_op jit(solution)/shard_map/example_rows/pallas_call | solution.py:291
  28.3 1.4 %early_products.1.sums_ref = f32[2,128,256]{2,1,0:T(8,128)S(1)} custom-call(bf16[256,8192]{1,0:T(8,128)(2,1)S(1)} %get-tuple-element.37.left_ref, bf16[16,256,64]{2,1,0:T(8,128)(2,1)S(1)} %get-tuple-element.38.right_ref, bf16[656,256]{1,0:T(8,128)(2,1)S(1)} %get-tuple-element.25.refs_0_, bf16[656,256]{1,0:T(8,128)(2,1)S(1)} %get-tuple-element.26.refs_1_, ...), custom_call_target="tpu_custom_call" | custom-call | tf_op jit(solution)/shard_map/early_products/pallas_call | solution.py:308
  29.8 0.7 %collective-permute-done.8.refs_0_ = bf16[576,256]{1,0:T(8,128)(2,1)S(1)} collective-permute-done((bf16[576,256]{1,0:T(8,128)(2,1)S(1)}, bf16[576,256]{1,0:T(8,128)(2,1)S(1)}, u32[]{:S(2)}, u32[]{:S(2)}) %collective-permute-start.8) | collective-permute-done | bytes 294944 | tf_op jit(solution)/shard_map/ppermute | solution.py:232
  30.4 0.2 collective-permute-start.10
  30.6 0.3 collective-permute-start.11
  30.9 1.1 %collective-permute-done.10.refs_2_ = bf16[576,256]{1,0:T(8,128)(2,1)S(1)} collective-permute-done((bf16[576,256]{1,0:T(8,128)(2,1)S(1)}, bf16[576,256]{1,0:T(8,128)(2,1)S(1)}, u32[]{:S(2)}, u32[]{:S(2)}) %collective-permute-start.10) | collective-permute-done | bytes 294944 | tf_op jit(solution)/shard_map/ppermute | solution.py:218
  32.0 0.4 collective-permute-done.11.refs_3_
  32.4 1.4 %join_features.1 = (bf16[4,8192]{1,0:T(4,128)(2,1)}, bf16[4,8192]{1,0:T(4,128)(2,1)S(1)}, bf16[4,8192]{1,0:T(4,128)(2,1)S(1)}) custom-call(bf16[256,8192]{1,0:T(8,128)(2,1)S(1)} %get-tuple-element.37.left_ref, bf16[16,256,64]{2,1,0:T(8,128)(2,1)S(1)} %get-tuple-element.38.right_ref, f32[2,128,256]{2,1,0:T(8,128)S(1)} %early_products.1.sums_ref, ...), custom_call_target="tpu_custom_call" | custom-call | tf_op jit(solution)/shard_map/join_features/pallas_call | solution.py:320
  33.8 2.6 %collective-permute-start.14 = (bf16[4,8192]{1,0:T(4,128)(2,1)S(1)}, bf16[4,8192]{1,0:T(4,128)(2,1)S(1)}, u32[]{:S(2)}, u32[]{:S(2)}) collective-permute-start(bf16[4,8192]{1,0:T(4,128)(2,1)S(1)} %get-tuple-element.46), channel_id=1, source_target_pairs={{0,24},{4,28},{8,16},{12,20},{16,8},{20,12},{24,0},{28,4},{1,25},{... | collective-permute-start | bytes 196616 | tf_op jit(solution)/shard_map/ppermute | solution.py:218
  36.4 0.3 collective-permute-start.13
  36.7 0.6 %collective-permute-start.12 = (bf16[4,8192]{1,0:T(4,128)(2,1)S(1)}, bf16[4,8192]{1,0:T(4,128)(2,1)S(1)}, u32[]{:S(2)}, u32[]{:S(2)}) collective-permute-start(bf16[4,8192]{1,0:T(4,128)(2,1)S(1)} %get-tuple-element.46), channel_id=1, source_target_pairs={{0,8},{4,12},{8,0},{12,4},{16,24},{20,28},{24,16},{28,20},{1,9},{5... | collective-permute-start | bytes 196616 | tf_op jit(solution)/shard_map/ppermute | solution.py:218
  37.3 1.7 %collective-permute-done.14 = bf16[4,8192]{1,0:T(4,128)(2,1)S(1)} collective-permute-done((bf16[4,8192]{1,0:T(4,128)(2,1)S(1)}, bf16[4,8192]{1,0:T(4,128)(2,1)S(1)}, u32[]{:S(2)}, u32[]{:S(2)}) %collective-permute-start.14) | collective-permute-done | bytes 65568 | tf_op jit(solution)/shard_map/ppermute | solution.py:218
  39.0 1.7 %collective-permute-done.13 = bf16[4,8192]{1,0:T(4,128)(2,1)S(1)} collective-permute-done((bf16[4,8192]{1,0:T(4,128)(2,1)S(1)}, bf16[4,8192]{1,0:T(4,128)(2,1)S(1)}, u32[]{:S(2)}, u32[]{:S(2)}) %collective-permute-start.13) | collective-permute-done | bytes 65568 | tf_op jit(solution)/shard_map/ppermute | solution.py:218
  40.6 0.3 collective-permute-done.12
  40.9 0.2 pad_maximum_fusion.1.same_ref
  41.2 1.5 %collective-permute-done.15.other_ref = bf16[16,8192]{1,0:T(8,128)(2,1)S(1)} collective-permute-done((bf16[16,8192]{1,0:T(8,128)(2,1)S(1)}, bf16[16,8192]{1,0:T(8,128)(2,1)S(1)}, u32[]{:S(2)}, u32[]{:S(2)}) %collective-permute-start.15) | collective-permute-done | bytes 262176 | tf_op jit(solution)/shard_map/ppermute | solution.py:218
  42.7 1.1 %score_rows.1 = f32[4,32]{1,0:T(4,128)} custom-call(bf16[4,8192]{1,0:T(4,128)(2,1)S(1)} %get-tuple-element.45.c_ref, bf16[16,8192]{1,0:T(8,128)(2,1)S(1)} %pad_maximum_fusion.1.same_ref, bf16[16,8192]{1,0:T(8,128)(2,1)S(1)} %collective-permute-done.15.other_ref), custom_call_target="tpu_custom_call" | custom-call | tf_op jit(solution)/shard_map/score_rows/pallas_call | solution.py:332
  (16 shorter events, 0.3 us)
Async XLA Ops:
  2.1 13.9 %collective-permute-start.2 = (bf16[1152,256]{1,0:T(8,128)(2,1)S(1)}, bf16[1152,256]{1,0:T(8,128)(2,1)S(1)}, u32[]{:S(2)}, u32[]{:S(2)}) collective-permute-start(bf16[1152,256]{1,0:T(8,128)(2,1)S(1)} %get-tuple-element.27), channel_id=1, source_target_pairs={{0,4},{4,0},{8,12},{12,8},{16,20},{20,16},{24,28},{28,24},{1,5},{5... | collective-permute-start | bytes 1769480 | tf_op jit(solution)/shard_map/ppermute | solution.py:218
  2.6 10.2 %collective-permute-start.1 = (bf16[656,256]{1,0:T(8,128)(2,1)S(1)}, bf16[656,256]{1,0:T(8,128)(2,1)S(1)}, u32[]{:S(2)}, u32[]{:S(2)}) collective-permute-start(bf16[656,256]{1,0:T(8,128)(2,1)S(1)} %get-tuple-element.26.refs_1_), channel_id=1, source_target_pairs={{0,16},{4,12},{8,24},{12,4},{16,0},{20,28},{24,8},{28,20},{1,17},{... | collective-permute-start | bytes 1007624 | tf_op jit(solution)/shard_map/ppermute | solution.py:232
  5.2 10.8 %collective-permute-start = (bf16[656,256]{1,0:T(8,128)(2,1)S(1)}, bf16[656,256]{1,0:T(8,128)(2,1)S(1)}, u32[]{:S(2)}, u32[]{:S(2)}) collective-permute-start(bf16[656,256]{1,0:T(8,128)(2,1)S(1)} %get-tuple-element.25.refs_0_), channel_id=1, source_target_pairs={{0,8},{4,20},{8,0},{12,28},{16,24},{20,4},{24,16},{28,12},{1,9},{5... | collective-permute-start | bytes 1007624 | tf_op jit(solution)/shard_map/ppermute | solution.py:232
  6.7 13.9 %collective-permute-start.5 = (bf16[576,256]{1,0:T(8,128)(2,1)S(1)}, bf16[576,256]{1,0:T(8,128)(2,1)S(1)}, u32[]{:S(2)}, u32[]{:S(2)}) collective-permute-start(bf16[576,256]{1,0:T(8,128)(2,1)S(1)} %slice.28), channel_id=1, source_target_pairs={{0,16},{4,12},{8,24},{12,4},{16,0},{20,28},{24,8},{28,20},{1,17},{... | collective-permute-start | bytes 884744 | tf_op jit(solution)/shard_map/ppermute | solution.py:232
  7.3 13.3 %collective-permute-start.4 = (bf16[576,256]{1,0:T(8,128)(2,1)S(1)}, bf16[576,256]{1,0:T(8,128)(2,1)S(1)}, u32[]{:S(2)}, u32[]{:S(2)}) collective-permute-start(bf16[576,256]{1,0:T(8,128)(2,1)S(1)} %slice.27), channel_id=1, source_target_pairs={{0,8},{4,20},{8,0},{12,28},{16,24},{20,4},{24,16},{28,12},{1,9},{5... | collective-permute-start | bytes 884744 | tf_op jit(solution)/shard_map/ppermute | solution.py:232
  16.1 4.6 %collective-permute-start.3 = (bf16[80,256]{1,0:T(8,128)(2,1)S(1)}, bf16[80,256]{1,0:T(8,128)(2,1)S(1)}, u32[]{:S(2)}, u32[]{:S(2)}) collective-permute-start(bf16[80,256]{1,0:T(8,128)(2,1)S(1)} %slice.25), channel_id=1, source_target_pairs={{0,16},{4,12},{8,24},{12,4},{16,0},{20,28},{24,8},{28,20},{1,17},{... | collective-permute-start | bytes 122888 | tf_op jit(solution)/shard_map/ppermute | solution.py:232
  20.7 7.6 %collective-permute-start.7 = (bf16[2304,256]{1,0:T(8,128)(2,1)S(1)}, bf16[2304,256]{1,0:T(8,128)(2,1)S(1)}, u32[]{:S(2)}, u32[]{:S(2)}) collective-permute-start(bf16[2304,256]{1,0:T(8,128)(2,1)S(1)} %pad_maximum_fusion), channel_id=1, source_target_pairs={{0,4},{4,0},{8,12},{12,8},{16,20},{20,16},{24,28},{28,24},{1,5},{5... | collective-permute-start | bytes 3538952 | tf_op jit(solution)/shard_map/ppermute | solution.py:218
  20.9 8.9 %collective-permute-start.9 = (bf16[576,256]{1,0:T(8,128)(2,1)S(1)}, bf16[576,256]{1,0:T(8,128)(2,1)S(1)}, u32[]{:S(2)}, u32[]{:S(2)}) collective-permute-start(bf16[576,256]{1,0:T(8,128)(2,1)S(1)} %slice.30.refs_6_), channel_id=1, source_target_pairs={{0,8},{4,20},{8,0},{12,28},{16,24},{20,4},{24,16},{28,12},{1,9},{5... | collective-permute-start | bytes 884744 | tf_op jit(solution)/shard_map/ppermute | solution.py:232
  22.5 7.9 %collective-permute-start.8 = (bf16[576,256]{1,0:T(8,128)(2,1)S(1)}, bf16[576,256]{1,0:T(8,128)(2,1)S(1)}, u32[]{:S(2)}, u32[]{:S(2)}) collective-permute-start(bf16[576,256]{1,0:T(8,128)(2,1)S(1)} %slice.29.refs_3_), channel_id=1, source_target_pairs={{0,16},{4,12},{8,24},{12,4},{16,0},{20,28},{24,8},{28,20},{1,17},{... | collective-permute-start | bytes 884744 | tf_op jit(solution)/shard_map/ppermute | solution.py:232
  24.2 1.4 %collective-permute-start.6 = (bf16[320,256]{1,0:T(8,128)(2,1)S(1)}, bf16[320,256]{1,0:T(8,128)(2,1)S(1)}, u32[]{:S(2)}, u32[]{:S(2)}) collective-permute-start(bf16[320,256]{1,0:T(8,128)(2,1)S(1)} %pad_maximum_fusion.2.t_same), channel_id=1, source_target_pairs={{0,4},{4,0},{8,12},{12,8},{16,20},{20,16},{24,28},{28,24},{1,5},{5... | collective-permute-start | bytes 491528 | tf_op jit(solution)/shard_map/ppermute | solution.py:218
  30.4 1.6 %collective-permute-start.10 = (bf16[576,256]{1,0:T(8,128)(2,1)S(1)}, bf16[576,256]{1,0:T(8,128)(2,1)S(1)}, u32[]{:S(2)}, u32[]{:S(2)}) collective-permute-start(bf16[576,256]{1,0:T(8,128)(2,1)S(1)} %collective-permute-done.8.refs_0_), channel_id=1, source_target_pairs={{0,4},{4,0},{8,12},{12,8},{16,20},{20,16},{24,28},{28,24},{1,5},{5... | collective-permute-start | bytes 884744 | tf_op jit(solution)/shard_map/ppermute | solution.py:218
  30.6 1.8 %collective-permute-start.11 = (bf16[576,256]{1,0:T(8,128)(2,1)S(1)}, bf16[576,256]{1,0:T(8,128)(2,1)S(1)}, u32[]{:S(2)}, u32[]{:S(2)}) collective-permute-start(bf16[576,256]{1,0:T(8,128)(2,1)S(1)} %collective-permute-done.9.refs_1_), channel_id=1, source_target_pairs={{0,4},{4,0},{8,12},{12,8},{16,20},{20,16},{24,28},{28,24},{1,5},{5... | collective-permute-start | bytes 884744 | tf_op jit(solution)/shard_map/ppermute | solution.py:218
  33.8 5.2 %collective-permute-start.14 = (bf16[4,8192]{1,0:T(4,128)(2,1)S(1)}, bf16[4,8192]{1,0:T(4,128)(2,1)S(1)}, u32[]{:S(2)}, u32[]{:S(2)}) collective-permute-start(bf16[4,8192]{1,0:T(4,128)(2,1)S(1)} %get-tuple-element.46), channel_id=1, source_target_pairs={{0,24},{4,28},{8,16},{12,20},{16,8},{20,12},{24,0},{28,4},{1,25},{... | collective-permute-start | bytes 196616 | tf_op jit(solution)/shard_map/ppermute | solution.py:218
  36.4 4.3 %collective-permute-start.13 = (bf16[4,8192]{1,0:T(4,128)(2,1)S(1)}, bf16[4,8192]{1,0:T(4,128)(2,1)S(1)}, u32[]{:S(2)}, u32[]{:S(2)}) collective-permute-start(bf16[4,8192]{1,0:T(4,128)(2,1)S(1)} %get-tuple-element.46), channel_id=1, source_target_pairs={{0,16},{4,20},{8,24},{12,28},{16,0},{20,4},{24,8},{28,12},{1,17},{... | collective-permute-start | bytes 196616 | tf_op jit(solution)/shard_map/ppermute | solution.py:218
  36.7 4.3 %collective-permute-start.12 = (bf16[4,8192]{1,0:T(4,128)(2,1)S(1)}, bf16[4,8192]{1,0:T(4,128)(2,1)S(1)}, u32[]{:S(2)}, u32[]{:S(2)}) collective-permute-start(bf16[4,8192]{1,0:T(4,128)(2,1)S(1)} %get-tuple-element.46), channel_id=1, source_target_pairs={{0,8},{4,12},{8,0},{12,4},{16,24},{20,28},{24,16},{28,20},{1,9},{5... | collective-permute-start | bytes 196616 | tf_op jit(solution)/shard_map/ppermute | solution.py:218
  41.1 1.6 %collective-permute-start.15 = (bf16[16,8192]{1,0:T(8,128)(2,1)S(1)}, bf16[16,8192]{1,0:T(8,128)(2,1)S(1)}, u32[]{:S(2)}, u32[]{:S(2)}) collective-permute-start(bf16[16,8192]{1,0:T(8,128)(2,1)S(1)} %pad_maximum_fusion.1.same_ref), channel_id=1, source_target_pairs={{0,4},{4,0},{8,12},{12,8},{16,20},{20,16},{24,28},{28,24},{1,5},{5... | collective-permute-start | bytes 786440 | tf_op jit(solution)/shard_map/ppermute | solution.py:218

commit v3 on v1

v3 whole, which is shorter than its diff:
```python
import functools

import jax
import jax.numpy as jnp
from jax import lax
from jax.experimental import pallas as pl
from jax.experimental.pallas import tpu as pltpu
from jax.sharding import PartitionSpec as P

eps_mean = 1e-06
LAST = (((1,), (1,)), ((), ()))
VMEM = pl.BlockSpec(memory_space=pltpu.VMEM)
SMEM = pl.BlockSpec(memory_space=pltpu.SMEM)
HBM = pl.BlockSpec(memory_space=pltpu.HBM)
MIB = 1 << 20
SHORT = pl.CostEstimate(flops=1, bytes_accessed=1, transcendentals=0)


def in_hbm(*arrays):
    return tuple(pltpu.with_memory_space_constraint(a, pltpu.HBM) for a in arrays)


def dot(a, b):
    return jnp.dot(a, b, preferred_element_type=jnp.float32)


def dot_last(a, b):
    return lax.dot_general(a, b, LAST, preferred_element_type=jnp.float32)


def first_way(core, plane):
    return 2 + 2 * ((core + plane) % 2)


def partner(me, kind, plane):
    first = first_way(me % 2, plane)
    return me ^ (0, first, 6 - first, 6)[kind]


def pack_kernel(
    down_hbm, up_hbm, rank_down_hbm, rank_up_hbm, in_hbm, out_hbm,
    extra_ref, own_ref, tail_ref, down_ref, up_ref, rank_down_ref, rank_up_ref, sems,
):
    s_rows, o_rows = in_hbm.shape[0], out_hbm.shape[0]
    tail = tail_ref.shape[0] - o_rows
    moves = (
        (down_hbm, down_ref),
        (up_hbm, up_ref),
        (rank_down_hbm, rank_down_ref),
        (rank_up_hbm, rank_up_ref),
        (out_hbm, extra_ref.at[pl.ds(0, o_rows)]),
        (out_hbm, tail_ref.at[pl.ds(tail, o_rows)]),
        (in_hbm.at[pl.ds(s_rows - tail, tail)], tail_ref.at[pl.ds(0, tail)]),
        (in_hbm, own_ref),
    )
    copies = [pltpu.make_async_copy(a, b, sems.at[i]) for i, (a, b) in enumerate(moves)]
    for copy in copies:
        copy.start()
    for copy in copies[:4]:
        copy.wait()
    down_table = dot_last(rank_up_ref[...], down_ref[...]).astype(jnp.bfloat16)
    up_table = dot_last(rank_down_ref[...], up_ref[...]).astype(jnp.bfloat16)
    ks, width = up_table.shape
    lanes = extra_ref.shape[1]
    blocks = down_table.shape[1] // lanes
    for b in range(blocks):
        at = o_rows + b * ks
        extra_ref[at : at + ks, :] = down_table[:, b * lanes : (b + 1) * lanes]
    at = o_rows + blocks * ks
    extra_ref[at:, :] = jnp.zeros((ks, lanes), jnp.bfloat16)
    extra_ref[at:, :width] = up_table
    for copy in copies[4:]:
        copy.wait()


def load_kernel(
    n, seq, ks, c_x_hbm, c_m_hbm, c_len_hbm, p_x_hbm, p_m_hbm, p_len_hbm,
    x_ref, m_ref, live_ref, send_ref, c_len, p_len, sems,
):
    half = c_x_hbm.shape[0]
    moves = (
        (c_len_hbm, c_len), (p_len_hbm, p_len),
        (c_m_hbm, m_ref.at[pl.ds(0, half)]), (p_m_hbm, m_ref.at[pl.ds(half, half)]),
        (c_x_hbm, x_ref.at[pl.ds(0, half)]), (p_x_hbm, x_ref.at[pl.ds(half, half)]),
    )
    copies = [pltpu.make_async_copy(a, b, sems.at[i]) for i, (a, b) in enumerate(moves)]
    for copy in copies:
        copy.start()
    for copy in copies[:2]:
        copy.wait()
    _, height, width = live_ref.shape
    rows = lax.broadcasted_iota(jnp.int32, (height, width), 0)
    cols = lax.broadcasted_iota(jnp.int32, (height, width), 1)
    for side, lengths in enumerate((c_len, p_len)):
        live = jnp.zeros((height, width), jnp.bool_)
        for e in range(width // ks):
            live = live | (
                (cols >= e * ks)
                & (cols < (e + 1) * ks)
                & (rows >= e * seq)
                & (rows < e * seq + lengths[e])
            )
        live_ref[side] = live.astype(jnp.float32)
    for copy in copies[2:]:
        copy.wait()
    other = 1 - lax.axis_index("fsdp") % 2
    at = 0
    for ref in (x_ref, m_ref):
        wide = ref.shape[1] // n
        for b in range(n // 2):
            first = pl.multiple_of((2 * b + other) * wide, wide)
            send_ref[:, at : at + wide] = ref[:, pl.ds(first, wide)]
            at += wide


def small_sums(n, ks, x, m, tables):
    kd, ku = x.shape[1] // n, m.shape[1] // n
    left = 0.0
    right = 0.0
    for j, ref, at in tables:
        lanes = ref.shape[1]
        blocks = kd // lanes
        up = ref[at + blocks * ks : at + (blocks + 1) * ks, :ku]
        left += dot_last(m[:, pl.ds(pl.multiple_of(j * ku, ku), ku)], up)
        for b in range(blocks):
            cols = pl.ds(pl.multiple_of(j * kd + b * lanes, lanes), lanes)
            right += dot_last(x[:, cols], ref[at + b * ks : at + (b + 1) * ks, :])
    return left, right


def small_kernel(n, ks, places, x, m, *refs):
    me, plane = lax.axis_index("fsdp"), lax.axis_index("dp")
    tables = [(partner(me ^ other, kind, plane), refs[r], at) for r, at, kind, other in places]
    refs[-1][0], refs[-1][1] = small_sums(n, ks, x, m, tables)


def products(n, places, x, m, xo, refs):
    me, plane = lax.axis_index("fsdp"), lax.axis_index("dp")
    kd, ku = x.shape[1] // n, m.shape[1] // n
    sums = [[0.0, 0.0], [0.0, 0.0]]
    for ref, row, kind, sketch, first, count in places:
        j = partner(me, kind, plane)
        piece = refs[ref][row : row + count, :]
        source, wide, base = ((x, kd, 0), (m, ku, (n // 2) * kd))[sketch]
        here = source[:, pl.ds(pl.multiple_of(j * wide + first, 128), count)]
        there = xo[:, pl.ds(pl.multiple_of(base + (j // 2) * wide + first, 128), count)]
        sums[0][sketch] += dot(here, piece)
        sums[1][sketch] += dot(there, piece)
    return sums


def early_kernel(n, places, x, m, xo, *refs):
    sums = products(n, places, x, m, xo, refs[:-1])
    for i in range(2):
        for t in range(2):
            refs[-1][i, t] = sums[i][t]


def late_kernel(n, places, side, table_places, x, m, xo, early, *refs):
    refs, (own_ref, send_ref) = refs[:-2], refs[-2:]
    half = x.shape[0] // 2
    rows = pl.ds(side * half, half)
    sums = products(n, places, x.at[rows], m.at[rows], xo.at[rows], refs)
    for t in range(2):
        own_ref[t] = sums[0][t] + early[0, t, rows, :]
        send_ref[t * half : (t + 1) * half, :] = (sums[1][t] + early[1, t, rows, :]).astype(jnp.bfloat16)
    at = 2 * half
    for ref, row, count in table_places:
        send_ref[at : at + count, :] = refs[ref][row : row + count, :]
        at += count


def join_kernel(n, ks, side, places, x, m, live, own, got, got_tables, first_small, more_small, *refs):
    outs, (left_scratch, right_scratch) = refs[:-2], refs[-2:]
    me, plane = lax.axis_index("fsdp"), lax.axis_index("dp")
    half = x.shape[0] // 2
    rows = pl.ds(side * half, half)
    tables = [(partner(me ^ other, kind, plane), got_tables, at) for at, kind, other in places]
    parts = small_sums(n, ks, x.at[rows], m.at[rows], tables)
    joined = []
    for t in range(2):
        small = parts[t] + first_small[t, rows, :] + more_small[t, rows, :]
        small = small.astype(jnp.bfloat16).astype(jnp.float32)
        wide = jnp.concatenate([small] * (live.shape[2] // ks), axis=1)
        factor = jnp.where(live[side] > 0, wide, 0.0).T.astype(jnp.bfloat16)
        total = own[t] + got[t * half : (t + 1) * half, :].astype(jnp.float32)
        joined.append(dot(factor, total.astype(jnp.bfloat16)))
    left, right = joined
    total = left.shape[0]
    count, cols = total // ks, left.shape[1]
    left = left.reshape(count, ks, cols)
    right = right.reshape(count, ks, cols)
    mean = jnp.sum(left * left + right * right, axis=(1, 2), keepdims=True) / (2 * ks * cols)
    scale = lax.rsqrt(mean + eps_mean)
    lanes = left_scratch.shape[2]
    for scratch, value in ((left_scratch, left), (right_scratch, right)):
        scaled = (value * scale).reshape(total, cols)
        for b in range(cols // lanes):
            scratch[b] = scaled[:, b * lanes : (b + 1) * lanes]
    for t, scratch in enumerate((left_scratch, right_scratch)):
        for r in range(ks):
            for b in range(cols // lanes):
                at = (t * ks + r) * cols + b * lanes
                value = scratch[b, pl.ds(r, count, stride=ks), :].astype(jnp.bfloat16)
                for out in outs:
                    out[:, at : at + lanes] = value


def same_kernel(c_ref, same_ref, out_ref):
    out_ref[...] = dot_last(c_ref[...], same_ref[...])


def score_kernel(order, c_ref, same_scores, other_ref, out_ref):
    me = lax.axis_index("fsdp")
    feats = c_ref[...]
    mixed = jnp.concatenate([same_scores[...], dot_last(feats, other_ref[...])], axis=1)
    width = mixed.shape[1]
    per = width // len(order)
    rows = lax.broadcasted_iota(jnp.int32, (width, width), 0)
    cols = lax.broadcasted_iota(jnp.int32, (width, width), 1)
    target = jnp.zeros((width, width), jnp.int32)
    for g, k in enumerate(order):
        target = jnp.where(rows // per == g, (me ^ k) * per + rows % per, target)
    place = (target == cols).astype(jnp.float32)
    out = lax.dot_general(
        mixed, place, (((1,), (0,)), ((), ())),
        preferred_element_type=jnp.float32, precision=lax.Precision.HIGHEST,
    )
    out_ref[...] = out / feats.shape[1]


def swap(x, k, axis, size):
    return lax.ppermute(x, axis, [(i, i ^ k) for i in range(size)])


def fast_body(n, planes, c_x, c_m, c_len, p_x, p_m, p_len, down, up, sketch_in, sketch_out, rank_down, rank_up):
    examples, seq, model = c_x.shape
    value = c_m.shape[2]
    ks, kp = rank_down.shape[1], sketch_in.shape[1]
    s_rows, o_rows = sketch_in.shape[0], sketch_out.shape[0]
    t_rows = (s_rows // kp + 1) * ks
    sw = functools.partial(swap, axis="fsdp", size=n)
    order = (0, 2, 4, 6, 1, 3, 5, 7)

    def along(x, second):
        pairs = []
        for i in range(n):
            for z in range(planes):
                way = first_way(i % 2, z)
                pairs.append((i * planes + z, (i ^ (6 - way if second else way)) * planes + z))
        return lax.ppermute(x, ("fsdp", "dp"), pairs)

    def array(*shape, dtype=jnp.bfloat16):
        return jax.ShapeDtypeStruct(shape, dtype)

    def kernel(f, name, outs, operands, in_specs=None, scratch=(), limit=8):
        return pl.pallas_call(
            f,
            out_shape=outs,
            in_specs=in_specs or [VMEM] * len(operands),
            out_specs=(VMEM,) * len(outs) if isinstance(outs, tuple) else VMEM,
            scratch_shapes=scratch,
            compiler_params=pltpu.CompilerParams(vmem_limit_bytes=limit * MIB),
            cost_estimate=SHORT,
            name=name,
        )(*operands)

    beside = s_rows * 5 // 8 // 128 * 128
    extra, own, tail = kernel(
        pack_kernel,
        "pack_weights",
        (array(o_rows + t_rows, kp), array(s_rows, kp), array(s_rows - beside + o_rows, kp)),
        in_hbm(down, up, rank_down.T, rank_up.T, sketch_in, sketch_out),
        in_specs=[HBM] * 6,
        scratch=[
            pltpu.VMEM(down.shape, down.dtype),
            pltpu.VMEM(up.shape, up.dtype),
            pltpu.VMEM(rank_down.shape[::-1], rank_down.dtype),
            pltpu.VMEM(rank_up.shape[::-1], rank_up.dtype),
            pltpu.SemaphoreType.DMA((8,)),
        ],
    )
    flat = (examples * seq, model)
    flat_m = (examples * seq, value)
    rows, total = 2 * examples * seq, 2 * examples * ks
    x, m, live, send = kernel(
        functools.partial(load_kernel, n, seq, ks),
        "load_rows",
        (
            array(rows, model),
            array(rows, value),
            array(2, rows // 2, total // 2, dtype=jnp.float32),
            array(rows, (model + value) // 2),
        ),
        in_hbm(c_x.reshape(flat), c_m.reshape(flat_m), c_len, p_x.reshape(flat), p_m.reshape(flat_m), p_len),
        in_specs=[HBM] * 6,
        scratch=[
            pltpu.SMEM(c_len.shape, c_len.dtype),
            pltpu.SMEM(p_len.shape, p_len.dtype),
            pltpu.SemaphoreType.DMA((6,)),
        ],
    )

    first, first_extra = along(sketch_in, False), along(extra, False)
    first, first_extra, x, m, live, send = lax.optimization_barrier((first, first_extra, x, m, live, send))

    more = along(jnp.concatenate([first, first_extra, tail]), True)
    rest = swap(jnp.concatenate([first[:beside], first_extra[o_rows:]]), 1, "dp", planes)
    xo = sw(send, 1)
    t_first = jnp.concatenate([extra[o_rows:], first_extra[o_rows:]])
    t_other = sw(t_first, 1)

    first_small = kernel(
        functools.partial(small_kernel, n, ks, ((0, 0, 0, 0), (0, t_rows, 1, 0), (1, 0, 0, 1), (1, t_rows, 1, 1))),
        "first_factors",
        array(2, rows, ks, dtype=jnp.float32),
        (x, m, t_first, t_other),
    )
    early = kernel(
        functools.partial(
            early_kernel, n,
            ((0, 0, 0, 0, 0, s_rows), (1, 0, 0, 1, 0, o_rows), (2, 0, 1, 0, 0, s_rows), (3, 0, 1, 1, 0, o_rows)),
        ),
        "early_products",
        array(2, 2, rows, kp, dtype=jnp.float32),
        (x, m, xo, own, extra, first, first_extra),
    )
    early, first_small = lax.optimization_barrier((early, first_small))

    t_at = s_rows + o_rows
    tail_at = t_at + t_rows
    left_rows = s_rows - beside
    late_places = (
        (0, 0, 3, 0, 0, s_rows), (0, s_rows, 3, 1, 0, o_rows),
        (0, tail_at, 2, 0, beside, left_rows), (0, tail_at + left_rows, 2, 1, 0, o_rows),
        (1, 0, 2, 0, 0, beside),
    )
    tables = ((0, t_at, t_rows), (1, beside, t_rows))

    def late(side, name, tables):
        return kernel(
            functools.partial(late_kernel, n, late_places, side, tables),
            name,
            (
                array(2, rows // 2, kp, dtype=jnp.float32),
                array(rows + sum(count for _, _, count in tables), kp),
            ),
            (x, m, xo, early, more, rest),
        )

    p_own, p_send = late(1, "probe_products", tables)
    p_got = sw(p_send, 1)
    more_small = kernel(
        functools.partial(small_kernel, n, ks, ((0, t_at, 3, 0), (1, beside, 2, 0))),
        "more_factors",
        array(2, rows, ks, dtype=jnp.float32),
        (x, m, more, rest),
    )
    got_places = ((rows, 3, 1), (rows + t_rows, 2, 1))
    feats = array(examples, 2 * ks * kp)
    scratch = [pltpu.VMEM((kp // 128, total // 2, 128), jnp.float32)] * 2

    def join(side, name, outs, own, got):
        return kernel(
            functools.partial(join_kernel, n, ks, side, got_places),
            name,
            outs,
            (x, m, live, own, got, p_got, first_small, more_small),
            scratch=scratch,
        )

    p_feat = join(1, "probe_features", feats, p_own, p_got)
    c_own, c_send = late(0, "candidate_products", ())
    c_feat, c_keep = join(0, "candidate_features", (feats, feats), c_own, sw(c_send, 1))

    got = [sw(p_feat, k) for k in (2, 4, 6)]
    c_keep, *got = lax.optimization_barrier((c_keep, *got))
    same = jnp.concatenate([p_feat, *got])
    other = sw(same, 1)
    same_scores = kernel(
        same_kernel, "same_scores", array(examples, n // 2 * examples, dtype=jnp.float32), (c_keep, same)
    )
    scores = kernel(
        functools.partial(score_kernel, order),
        "score_rows",
        array(examples, n * examples, dtype=jnp.float32),
        (c_keep, same_scores, other),
    )
    return scores, c_feat


def plain_features(x, m, lengths, down, up, sketch_in, sketch_out, rank_down, rank_up):
    examples, seq, model = x.shape
    ks, kp = rank_down.shape[1], sketch_in.shape[1]
    live = (lax.broadcasted_iota(jnp.int32, (examples, seq), 1) < lengths[:, None]).astype(m.dtype)
    masked = (m * live[:, :, None]).reshape(examples * seq, -1)
    rows = x.reshape(examples * seq, model)
    grad_rows = dot(masked, up).astype(jnp.bfloat16)
    outward = dot(masked, sketch_out).astype(jnp.bfloat16)
    down_round = dot(rows, down).astype(jnp.bfloat16)
    inward = dot(rows, sketch_in).astype(jnp.bfloat16)
    left_small = dot(grad_rows, rank_down).astype(jnp.bfloat16)
    right_small = dot(down_round, rank_up).astype(jnp.bfloat16)

    def outer(small, wide):
        return jnp.einsum(
            "esk,esp->ekp",
            small.reshape(examples, seq, ks),
            wide.reshape(examples, seq, kp),
            preferred_element_type=jnp.float32,
        )

    joined = jnp.concatenate([outer(left_small, inward), outer(right_small, outward)], axis=1)
    joined = joined.reshape(examples, 2 * ks * kp)
    scale = lax.rsqrt(jnp.mean(joined * joined, axis=1, keepdims=True) + eps_mean)
    return (joined * scale).astype(jnp.bfloat16)


def plain_body(c_x, c_m, c_len, p_x, p_m, p_len, down, up, sketch_in, sketch_out, rank_down, rank_up):
    weights = [
        lax.all_gather(w, "fsdp", axis=0, tiled=True) for w in (down, up, sketch_in, sketch_out)
    ]
    p_feat = plain_features(p_x, p_m, p_len, *weights, rank_down, rank_up)
    c_feat = plain_features(c_x, c_m, c_len, *weights, rank_down, rank_up)
    every = lax.all_gather(p_feat, "fsdp", axis=0, tiled=True)
    return dot(c_feat, every.T) / c_feat.shape[1], c_feat


def solution(mesh):
    n, planes = mesh.shape["fsdp"], mesh.shape["dp"]
    rows = P(("dp", "fsdp"), None)
    cube = P(("dp", "fsdp"), None, None)
    line = P(("dp", "fsdp"))
    shard = P("fsdp", None)
    in_specs = (cube, cube, line, cube, cube, line, shard, shard, shard, shard, P(), P())

    def body(*args):
        if n == 1 << 3 and planes % 2 == 0:
            return fast_body(n, planes, *args)
        return plain_body(*args)

    return jax.shard_map(body, mesh=mesh, in_specs=in_specs, out_specs=(rows, rows), check_vma=False)
```

time: 53 us -> 40.1 us (0.76)
  local copies, waits for them, and re-layouts: 7.76 us -> 0.03 us
  starting transfers between devices: 15.7 us -> 11.2 us
  waiting for transfers between devices: 21.2 us -> 17.2 us
  Pallas kernels: 6.93 us -> 10.5 us
    ppermute x22 -> x9, starting transfers between devices: 15.7 us -> 5.99 us  [swap(): return lax.ppermute(x, axis, [(i, i ^ k) for i in range(size)])]
    ppermute x22 -> x9, waiting for transfers between devices: 21.2 us -> 12.5 us  [swap(): return lax.ppermute(x, axis, [(i, i ^ k) for i in range(size)])]
    unnamed x20 -> x0, local copies, waits for them, and re-layouts: 5.91 us -> none
    ppermute x0 -> x3, starting transfers between devices: none -> 5.2 us  [along(): return lax.ppermute(x, ('fsdp', 'dp'), pairs)]
    ppermute x0 -> x3, waiting for transfers between devices: none -> 4.64 us  [along(): return lax.ppermute(x, ('fsdp', 'dp'), pairs)]
    pallas_call x4 -> x11, Pallas kernels: 6.93 us -> 10.5 us  [kernel(): pl.pallas_call(f, out_shape=outs, in_specs=in_specs or [VMEM] * len(opera...]
    slice x2 -> x3, local copies, waits for them, and re-layouts: 1.85 us -> 0.03 us  [the longest x1 0.02 us: fast_body(): first[:beside]]
  transfers between devices with their start and end apart: 22 -> 12, of which waited for: 8 -> 7; matrix products, arithmetic and copies ran while one was open for 4% -> 0% of each run, Pallas kernels for 6% -> 22%
where the time goes in v3:
time: 40.1 us; the launch traced here: 39.9 us
  waiting for transfers between devices  17.2 us (43%)
  starting transfers between devices  11.2 us (28%)
  Pallas kernels  10.5 us (26%)
  between operations  0.76 us (2%)
    ppermute x9, waiting for transfers between devices, swap(): return lax.ppermute(x, axis, [(i, i ^ k) for i in range(size)])  12.5 us
    pallas_call x11, Pallas kernels, kernel(): pl.pallas_call(f, out_shape=outs, in_specs=in_specs or [VMEM] * len(opera...  10.5 us
    ppermute x9, starting transfers between devices, swap(): return lax.ppermute(x, axis, [(i, i ^ k) for i in range(size)])  5.99 us
    ppermute x3, starting transfers between devices, along(): return lax.ppermute(x, ('fsdp', 'dp'), pairs)  5.2 us
    ppermute x3, waiting for transfers between devices, along(): return lax.ppermute(x, ('fsdp', 'dp'), pairs)  4.64 us
  transfers between devices with their start and end apart: 12, of which 7 were waited for; matrix products, arithmetic and copies ran while one was open for 0% of the time, Pallas kernels for 22%

profile of v3, /device:TPU:0, one launch (start us, length us, event | category | flops | bytes accessed | tf_op | source)
XLA Modules:
  0.0 39.9 jit_solution(9113023176112994211)
XLA Ops:
  0.6 3.0 %collective-permute-start = (bf16[1024,256]{1,0:T(8,128)(2,1)}, bf16[1024,256]{1,0:T(8,128)(2,1)S(1)}, u32[]{:S(2)}, u32[]{:S(2)}) collective-permute-start(bf16[1024,256]{1,0:T(8,128)(2,1)} %in_hbm.1), channel_id=1, source_target_pairs={{0,8},{1,17},{2,10},{3,19},{4,20},{5,13},{6,22},{7,15},{8,0},{9,25... | collective-permute-start | bytes 1572872 | tf_op jit(solution)/shard_map/ppermute | solution.py:251
  3.6 1.4 %pack_weights.1 = (bf16[208,256]{1,0:T(8,128)(2,1)S(1)}, bf16[1024,256]{1,0:T(8,128)(2,1)S(1)}, bf16[512,256]{1,0:T(8,128)(2,1)S(1)}) custom-call(bf16[1024,128]{1,0:T(8,128)(2,1)} %down_hbm.1, bf16[128,128]{1,0:T(8,128)(2,1)} %up_hbm.1, bf16[16,128]{1,0:T(8,128)(2,1)} %bitcast.10, bf16[16,128]{1,0:T(8,128)(2,1)} %bitcast.11, bf16[1024,256]{1,0:T(8,128)(2,1)} %in_hbm.1, ...), custom_call_target="tpu_custom_call" | custom-call | flops 1 | bytes 1 | tf_op jit(solution)/shard_map/pack_weights/pallas_call | solution.py:257
  5.0 0.1 collective-permute-start.1
  5.1 2.7 %load_rows.1 = (bf16[256,8192]{1,0:T(8,128)(2,1)S(1)}, bf16[256,1024]{1,0:T(8,128)(2,1)S(1)}, f32[2,128,64]{2,1,0:T(8,128)S(1)}, bf16[256,4608]{1,0:T(8,128)(2,1)S(1)}) custom-call(bf16[128,8192]{1,0:T(8,128)(2,1)} %bitcast.6, bf16[128,1024]{1,0:T(8,128)(2,1)} %bitcast.8, s32[4]{0:T(128)} %c_len_hbm.1, bf16[128,8192]{1,0:T(8,128)(2,1)} %bitcast.7, ...), custom_call_target="tpu_custom_call" | custom-call | flops 1 | bytes 1 | tf_op jit(solution)/shard_map/load_rows/pallas_call | solution.py:257
  7.8 4.4 %collective-permute-done.1.refs_3_ = bf16[208,256]{1,0:T(8,128)(2,1)S(1)} collective-permute-done((bf16[208,256]{1,0:T(8,128)(2,1)S(1)}, bf16[208,256]{1,0:T(8,128)(2,1)S(1)}, u32[]{:S(2)}, u32[]{:S(2)}) %collective-permute-start.1) | collective-permute-done | bytes 106528 | tf_op jit(solution)/shard_map/ppermute | solution.py:251
  12.2 0.0 collective-permute-start.2
  12.2 0.1 pad_maximum_fusion
  12.2 2.1 %collective-permute-start.4 = (bf16[1744,256]{1,0:T(8,128)(2,1)S(1)}, bf16[1744,256]{1,0:T(8,128)(2,1)S(1)}, u32[]{:S(2)}, u32[]{:S(2)}) collective-permute-start(bf16[1744,256]{1,0:T(8,128)(2,1)S(1)} %pad_maximum_fusion), channel_id=1, source_target_pairs={{0,16},{1,9},{2,18},{3,11},{4,12},{5,21},{6,14},{7,23},{8,24},{9,1... | collective-permute-start | bytes 2678792 | tf_op jit(solution)/shard_map/ppermute | solution.py:251
  14.4 1.6 %collective-permute-start.5 = (bf16[720,256]{1,0:T(8,128)(2,1)S(1)}, bf16[720,256]{1,0:T(8,128)(2,1)S(1)}, u32[]{:S(2)}, u32[]{:S(2)}) collective-permute-start(bf16[720,256]{1,0:T(8,128)(2,1)S(1)} %pad_maximum_fusion.1), channel_id=1, source_target_pairs={{0,1},{1,0},{2,3},{3,2},{4,5},{5,4},{6,7},{7,6},{8,9},{9,8},{10,11... | collective-permute-start | bytes 1105928 | tf_op jit(solution)/shard_map/ppermute | solution.py:233
  16.0 0.1 collective-permute-start.3
  16.1 1.3 %collective-permute-done.3.refs_1_ = bf16[160,256]{1,0:T(8,128)(2,1)S(1)} collective-permute-done((bf16[160,256]{1,0:T(8,128)(2,1)S(1)}, bf16[160,256]{1,0:T(8,128)(2,1)S(1)}, u32[]{:S(2)}, u32[]{:S(2)}) %collective-permute-start.3) | collective-permute-done | bytes 81952 | tf_op jit(solution)/shard_map/ppermute | solution.py:233
  17.4 0.7 %first_factors.1.first_small = f32[2,256,16]{2,1,0:T(8,128)S(1)} custom-call(bf16[256,8192]{1,0:T(8,128)(2,1)S(1)} %get-tuple-element.32.x, bf16[256,1024]{1,0:T(8,128)(2,1)S(1)} %get-tuple-element.33.m, bf16[160,256]{1,0:T(8,128)(2,1)S(1)} %pad_maximum_fusion.3.refs_0_, bf16[160,256]{1,0:T(8,128)(2,1)S(1)} %collective-permute-done.3.refs_1_), custom_call_target="tpu_custom_call" | custom-call | flops 1 | bytes 1 | tf_op jit(solution)/shard_map/first_factors/pallas_call | solution.py:257
  18.1 0.9 %early_products.1.early = f32[2,2,256,256]{3,2,1,0:T(8,128)S(1)} custom-call(bf16[256,8192]{1,0:T(8,128)(2,1)S(1)} %get-tuple-element.32.x, bf16[256,1024]{1,0:T(8,128)(2,1)S(1)} %get-tuple-element.33.m, bf16[256,4608]{1,0:T(8,128)(2,1)S(1)} %collective-permute-done.2.xo, bf16[1024,256]{1,0:T(8,128)(2,1)S(1)} %get-tuple-element.36.refs_0_, ...), custom_call_target="tpu_custom_call" | custom-call | flops 1 | bytes 1 | tf_op jit(solution)/shard_map/early_products/pallas_call | solution.py:257
  19.0 6.2 %collective-permute-done.5.refs_1_ = bf16[720,256]{1,0:T(8,128)(2,1)S(1)} collective-permute-done((bf16[720,256]{1,0:T(8,128)(2,1)S(1)}, bf16[720,256]{1,0:T(8,128)(2,1)S(1)}, u32[]{:S(2)}, u32[]{:S(2)}) %collective-permute-start.5) | collective-permute-done | bytes 368672 | tf_op jit(solution)/shard_map/ppermute | solution.py:233
  25.2 0.3 collective-permute-done.4.refs_0_
  25.4 0.5 %probe_products.1 = (f32[2,128,256]{2,1,0:T(8,128)S(1)}, bf16[416,256]{1,0:T(8,128)(2,1)S(1)}) custom-call(bf16[256,8192]{1,0:T(8,128)(2,1)S(1)} %get-tuple-element.32.x, bf16[256,1024]{1,0:T(8,128)(2,1)S(1)} %get-tuple-element.33.m, bf16[256,4608]{1,0:T(8,128)(2,1)S(1)} %collective-permute-done.2.xo, f32[2,2,256,256]{3,2,1,0:T(8,128)S(1)} %early_products.1.early, ...), custom_call_target="tpu_custom_call" | custom-call | flops 1 | bytes 1 | tf_op jit(solution)/shard_map/probe_products/pallas_call | solution.py:257
  26.0 0.1 collective-permute-start.7
  26.1 0.6 %candidate_products.1 = (f32[2,128,256]{2,1,0:T(8,128)S(1)}, bf16[256,256]{1,0:T(8,128)(2,1)S(1)}) custom-call(bf16[256,8192]{1,0:T(8,128)(2,1)S(1)} %get-tuple-element.32.x, bf16[256,1024]{1,0:T(8,128)(2,1)S(1)} %get-tuple-element.33.m, bf16[256,4608]{1,0:T(8,128)(2,1)S(1)} %collective-permute-done.2.xo, f32[2,2,256,256]{3,2,1,0:T(8,128)S(1)} %early_products.1.early, ...), custom_call_target="tpu_custom_call" | custom-call | flops 1 | bytes 1 | tf_op jit(solution)/shard_map/candidate_products/pallas_call | solution.py:257
  26.6 0.6 %collective-permute-start.6 = (bf16[256,256]{1,0:T(8,128)(2,1)S(1)}, bf16[256,256]{1,0:T(8,128)(2,1)S(1)}, u32[]{:S(2)}, u32[]{:S(2)}) collective-permute-start(bf16[256,256]{1,0:T(8,128)(2,1)S(1)} %get-tuple-element.42), channel_id=1, source_target_pairs={{0,4},{4,0},{8,12},{12,8},{16,20},{20,16},{24,28},{28,24},{1,5},{5... | collective-permute-start | bytes 393224 | tf_op jit(solution)/shard_map/ppermute | solution.py:233
  27.2 0.4 %more_factors.1.more_small = f32[2,256,16]{2,1,0:T(8,128)S(1)} custom-call(bf16[256,8192]{1,0:T(8,128)(2,1)S(1)} %get-tuple-element.32.x, bf16[256,1024]{1,0:T(8,128)(2,1)S(1)} %get-tuple-element.33.m, bf16[1744,256]{1,0:T(8,128)(2,1)S(1)} %collective-permute-done.4.refs_0_, bf16[720,256]{1,0:T(8,128)(2,1)S(1)} %collective-permute-done.5.refs_1_), custom_call_target="tpu_custom_call" | custom-call | flops 1 | bytes 1 | tf_op jit(solution)/shard_map/more_factors/pallas_call | solution.py:257
  27.6 0.7 %probe_features.1 = bf16[4,8192]{1,0:T(4,128)(2,1)S(1)} custom-call(bf16[256,8192]{1,0:T(8,128)(2,1)S(1)} %get-tuple-element.32.x, bf16[256,1024]{1,0:T(8,128)(2,1)S(1)} %get-tuple-element.33.m, f32[2,128,64]{2,1,0:T(8,128)S(1)} %get-tuple-element.34.live, f32[2,128,256]{2,1,0:T(8,128)S(1)} %get-tuple-element.46.own, ...), custom_call_target="tpu_custom_call" | custom-call | flops 1 | bytes 1 | tf_op jit(solution)/shard_map/probe_features/pallas_call | solution.py:257
  28.4 2.1 %collective-permute-start.8 = (bf16[4,8192]{1,0:T(4,128)(2,1)S(1)}, bf16[4,8192]{1,0:T(4,128)(2,1)S(1)}, u32[]{:S(2)}, u32[]{:S(2)}) collective-permute-start(bf16[4,8192]{1,0:T(4,128)(2,1)S(1)} %probe_features.1), channel_id=1, source_target_pairs={{0,8},{4,12},{8,0},{12,4},{16,24},{20,28},{24,16},{28,20},{1,9},{5... | collective-permute-start | bytes 196616 | tf_op jit(solution)/shard_map/ppermute | solution.py:233
  30.4 1.5 %collective-permute-start.9 = (bf16[4,8192]{1,0:T(4,128)(2,1)S(1)}, bf16[4,8192]{1,0:T(4,128)(2,1)S(1)}, u32[]{:S(2)}, u32[]{:S(2)}) collective-permute-start(bf16[4,8192]{1,0:T(4,128)(2,1)S(1)} %probe_features.1), channel_id=1, source_target_pairs={{0,16},{4,20},{8,24},{12,28},{16,0},{20,4},{24,8},{28,12},{1,17},{... | collective-permute-start | bytes 196616 | tf_op jit(solution)/shard_map/ppermute | solution.py:233
  31.9 0.0 collective-permute-start.10
  32.0 1.4 %candidate_features.1 = (bf16[4,8192]{1,0:T(4,128)(2,1)}, bf16[4,8192]{1,0:T(4,128)(2,1)S(1)}) custom-call(bf16[256,8192]{1,0:T(8,128)(2,1)S(1)} %get-tuple-element.32.x, bf16[256,1024]{1,0:T(8,128)(2,1)S(1)} %get-tuple-element.33.m, f32[2,128,64]{2,1,0:T(8,128)S(1)} %get-tuple-element.34.live, f32[2,128,256]{2,1,0:T(8,128)S(1)} %get-tuple-element.41.own, ...), custom_call_target="tpu_custom_call" | custom-call | flops 1 | bytes 1 | tf_op jit(solution)/shard_map/candidate_features/pallas_call | solution.py:257
  33.3 1.4 %collective-permute-done.9 = bf16[4,8192]{1,0:T(4,128)(2,1)S(1)} collective-permute-done((bf16[4,8192]{1,0:T(4,128)(2,1)S(1)}, bf16[4,8192]{1,0:T(4,128)(2,1)S(1)}, u32[]{:S(2)}, u32[]{:S(2)}) %collective-permute-start.9) | collective-permute-done | bytes 65568 | tf_op jit(solution)/shard_map/ppermute | solution.py:233
  34.7 2.4 %collective-permute-done.10 = bf16[4,8192]{1,0:T(4,128)(2,1)S(1)} collective-permute-done((bf16[4,8192]{1,0:T(4,128)(2,1)S(1)}, bf16[4,8192]{1,0:T(4,128)(2,1)S(1)}, u32[]{:S(2)}, u32[]{:S(2)}) %collective-permute-start.10) | collective-permute-done | bytes 65568 | tf_op jit(solution)/shard_map/ppermute | solution.py:233
  37.1 0.2 pad_maximum_fusion.2.same_ref
  37.3 0.1 collective-permute-start.11
  37.3 0.2 same_scores.1
  37.6 1.3 %collective-permute-done.11.other_ref = bf16[16,8192]{1,0:T(8,128)(2,1)S(1)} collective-permute-done((bf16[16,8192]{1,0:T(8,128)(2,1)S(1)}, bf16[16,8192]{1,0:T(8,128)(2,1)S(1)}, u32[]{:S(2)}, u32[]{:S(2)}) %collective-permute-start.11) | collective-permute-done | bytes 262176 | tf_op jit(solution)/shard_map/ppermute | solution.py:233
  38.9 1.0 %score_rows.1 = f32[4,32]{1,0:T(4,128)} custom-call(bf16[4,8192]{1,0:T(4,128)(2,1)S(1)} %get-tuple-element.47.c_ref, f32[4,16]{1,0:T(4,128)S(1)} %same_scores.1, bf16[16,8192]{1,0:T(8,128)(2,1)S(1)} %collective-permute-done.11.other_ref), custom_call_target="tpu_custom_call" | custom-call | flops 1 | bytes 1 | tf_op jit(solution)/shard_map/score_rows/pallas_call | solution.py:257
  (10 shorter events, 0.1 us)
Async XLA Ops:
  0.6 11.5 %collective-permute-start = (bf16[1024,256]{1,0:T(8,128)(2,1)}, bf16[1024,256]{1,0:T(8,128)(2,1)S(1)}, u32[]{:S(2)}, u32[]{:S(2)}) collective-permute-start(bf16[1024,256]{1,0:T(8,128)(2,1)} %in_hbm.1), channel_id=1, source_target_pairs={{0,8},{1,17},{2,10},{3,19},{4,20},{5,13},{6,22},{7,15},{8,0},{9,25... | collective-permute-start | bytes 1572872 | tf_op jit(solution)/shard_map/ppermute | solution.py:251
  5.0 7.1 %collective-permute-start.1 = (bf16[208,256]{1,0:T(8,128)(2,1)S(1)}, bf16[208,256]{1,0:T(8,128)(2,1)S(1)}, u32[]{:S(2)}, u32[]{:S(2)}) collective-permute-start(bf16[208,256]{1,0:T(8,128)(2,1)S(1)} %get-tuple-element.27.refs_1_), channel_id=1, source_target_pairs={{0,8},{1,17},{2,10},{3,19},{4,20},{5,13},{6,22},{7,15},{8,0},{9,25... | collective-permute-start | bytes 319496 | tf_op jit(solution)/shard_map/ppermute | solution.py:251
  12.2 6.0 %collective-permute-start.2 = (bf16[256,4608]{1,0:T(8,128)(2,1)S(1)}, bf16[256,4608]{1,0:T(8,128)(2,1)S(1)}, u32[]{:S(2)}, u32[]{:S(2)}) collective-permute-start(bf16[256,4608]{1,0:T(8,128)(2,1)S(1)} %get-tuple-element.35), channel_id=1, source_target_pairs={{0,4},{4,0},{8,12},{12,8},{16,20},{20,16},{24,28},{28,24},{1,5},{5... | collective-permute-start | bytes 7077896 | tf_op jit(solution)/shard_map/ppermute | solution.py:233
  12.2 13.2 %collective-permute-start.4 = (bf16[1744,256]{1,0:T(8,128)(2,1)S(1)}, bf16[1744,256]{1,0:T(8,128)(2,1)S(1)}, u32[]{:S(2)}, u32[]{:S(2)}) collective-permute-start(bf16[1744,256]{1,0:T(8,128)(2,1)S(1)} %pad_maximum_fusion), channel_id=1, source_target_pairs={{0,16},{1,9},{2,18},{3,11},{4,12},{5,21},{6,14},{7,23},{8,24},{9,1... | collective-permute-start | bytes 2678792 | tf_op jit(solution)/shard_map/ppermute | solution.py:251
  14.4 10.8 %collective-permute-start.5 = (bf16[720,256]{1,0:T(8,128)(2,1)S(1)}, bf16[720,256]{1,0:T(8,128)(2,1)S(1)}, u32[]{:S(2)}, u32[]{:S(2)}) collective-permute-start(bf16[720,256]{1,0:T(8,128)(2,1)S(1)} %pad_maximum_fusion.1), channel_id=1, source_target_pairs={{0,1},{1,0},{2,3},{3,2},{4,5},{5,4},{6,7},{7,6},{8,9},{9,8},{10,11... | collective-permute-start | bytes 1105928 | tf_op jit(solution)/shard_map/ppermute | solution.py:233
  16.0 1.3 %collective-permute-start.3 = (bf16[160,256]{1,0:T(8,128)(2,1)S(1)}, bf16[160,256]{1,0:T(8,128)(2,1)S(1)}, u32[]{:S(2)}, u32[]{:S(2)}) collective-permute-start(bf16[160,256]{1,0:T(8,128)(2,1)S(1)} %pad_maximum_fusion.3.refs_0_), channel_id=1, source_target_pairs={{0,4},{4,0},{8,12},{12,8},{16,20},{20,16},{24,28},{28,24},{1,5},{5... | collective-permute-start | bytes 245768 | tf_op jit(solution)/shard_map/ppermute | solution.py:233
  26.0 1.6 %collective-permute-start.7 = (bf16[416,256]{1,0:T(8,128)(2,1)S(1)}, bf16[416,256]{1,0:T(8,128)(2,1)S(1)}, u32[]{:S(2)}, u32[]{:S(2)}) collective-permute-start(bf16[416,256]{1,0:T(8,128)(2,1)S(1)} %get-tuple-element.43), channel_id=1, source_target_pairs={{0,4},{4,0},{8,12},{12,8},{16,20},{20,16},{24,28},{28,24},{1,5},{5... | collective-permute-start | bytes 638984 | tf_op jit(solution)/shard_map/ppermute | solution.py:233
  26.6 5.3 %collective-permute-start.6 = (bf16[256,256]{1,0:T(8,128)(2,1)S(1)}, bf16[256,256]{1,0:T(8,128)(2,1)S(1)}, u32[]{:S(2)}, u32[]{:S(2)}) collective-permute-start(bf16[256,256]{1,0:T(8,128)(2,1)S(1)} %get-tuple-element.42), channel_id=1, source_target_pairs={{0,4},{4,0},{8,12},{12,8},{16,20},{20,16},{24,28},{28,24},{1,5},{5... | collective-permute-start | bytes 393224 | tf_op jit(solution)/shard_map/ppermute | solution.py:233
  28.4 5.0 %collective-permute-start.8 = (bf16[4,8192]{1,0:T(4,128)(2,1)S(1)}, bf16[4,8192]{1,0:T(4,128)(2,1)S(1)}, u32[]{:S(2)}, u32[]{:S(2)}) collective-permute-start(bf16[4,8192]{1,0:T(4,128)(2,1)S(1)} %probe_features.1), channel_id=1, source_target_pairs={{0,8},{4,12},{8,0},{12,4},{16,24},{20,28},{24,16},{28,20},{1,9},{5... | collective-permute-start | bytes 196616 | tf_op jit(solution)/shard_map/ppermute | solution.py:233
  30.4 4.3 %collective-permute-start.9 = (bf16[4,8192]{1,0:T(4,128)(2,1)S(1)}, bf16[4,8192]{1,0:T(4,128)(2,1)S(1)}, u32[]{:S(2)}, u32[]{:S(2)}) collective-permute-start(bf16[4,8192]{1,0:T(4,128)(2,1)S(1)} %probe_features.1), channel_id=1, source_target_pairs={{0,16},{4,20},{8,24},{12,28},{16,0},{20,4},{24,8},{28,12},{1,17},{... | collective-permute-start | bytes 196616 | tf_op jit(solution)/shard_map/ppermute | solution.py:233
  31.9 5.2 %collective-permute-start.10 = (bf16[4,8192]{1,0:T(4,128)(2,1)S(1)}, bf16[4,8192]{1,0:T(4,128)(2,1)S(1)}, u32[]{:S(2)}, u32[]{:S(2)}) collective-permute-start(bf16[4,8192]{1,0:T(4,128)(2,1)S(1)} %probe_features.1), channel_id=1, source_target_pairs={{0,24},{4,28},{8,16},{12,20},{16,8},{20,12},{24,0},{28,4},{1,25},{... | collective-permute-start | bytes 196616 | tf_op jit(solution)/shard_map/ppermute | solution.py:233
  37.3 1.6 %collective-permute-start.11 = (bf16[16,8192]{1,0:T(8,128)(2,1)S(1)}, bf16[16,8192]{1,0:T(8,128)(2,1)S(1)}, u32[]{:S(2)}, u32[]{:S(2)}) collective-permute-start(bf16[16,8192]{1,0:T(8,128)(2,1)S(1)} %pad_maximum_fusion.2.same_ref), channel_id=1, source_target_pairs={{0,4},{4,0},{8,12},{12,8},{16,20},{20,16},{24,28},{28,24},{1,5},{5... | collective-permute-start | bytes 786440 | tf_op jit(solution)/shard_map/ppermute | solution.py:233

commit v4 on v3

v4 whole, which is shorter than its diff:
```python
import functools

import jax
import jax.numpy as jnp
from jax import lax
from jax.experimental import pallas as pl
from jax.experimental.pallas import tpu as pltpu
from jax.sharding import PartitionSpec as P

eps_mean = 1e-06
LAST = (((1,), (1,)), ((), ()))
VMEM = pl.BlockSpec(memory_space=pltpu.VMEM)
SMEM = pl.BlockSpec(memory_space=pltpu.SMEM)
HBM = pl.BlockSpec(memory_space=pltpu.HBM)
MIB = 1 << 20
SHORT = pl.CostEstimate(flops=1, bytes_accessed=1, transcendentals=0)


def in_hbm(*arrays):
    return tuple(pltpu.with_memory_space_constraint(a, pltpu.HBM) for a in arrays)


def dot(a, b):
    return jnp.dot(a, b, preferred_element_type=jnp.float32)


def dot_last(a, b):
    return lax.dot_general(a, b, LAST, preferred_element_type=jnp.float32)


def split_two(x):
    high = x.astype(jnp.bfloat16)
    return high, (x - high.astype(jnp.float32)).astype(jnp.bfloat16)


def first_way(core, plane):
    return 2 + 2 * ((core + plane) % 2)


def partner(me, kind, plane):
    first = first_way(me % 2, plane)
    return me ^ (0, first, 6 - first, 6)[kind]


def pack_kernel(
    down_hbm, up_hbm, rank_down_hbm, rank_up_hbm, in_hbm, out_hbm,
    extra_ref, own_ref, tail_ref, down_ref, up_ref, rank_down_ref, rank_up_ref, sems,
):
    s_rows, o_rows = in_hbm.shape[0], out_hbm.shape[0]
    tail = tail_ref.shape[0] - o_rows
    moves = (
        (down_hbm, down_ref),
        (up_hbm, up_ref),
        (rank_down_hbm, rank_down_ref),
        (rank_up_hbm, rank_up_ref),
        (out_hbm, extra_ref.at[pl.ds(0, o_rows)]),
        (out_hbm, tail_ref.at[pl.ds(tail, o_rows)]),
        (in_hbm.at[pl.ds(s_rows - tail, tail)], tail_ref.at[pl.ds(0, tail)]),
        (in_hbm, own_ref),
    )
    copies = [pltpu.make_async_copy(a, b, sems.at[i]) for i, (a, b) in enumerate(moves)]
    for copy in copies:
        copy.start()
    for copy in copies[:4]:
        copy.wait()
    down_table = dot_last(rank_up_ref[...], down_ref[...]).astype(jnp.bfloat16)
    up_table = dot_last(rank_down_ref[...], up_ref[...]).astype(jnp.bfloat16)
    ks, width = up_table.shape
    lanes = extra_ref.shape[1]
    blocks = down_table.shape[1] // lanes
    for b in range(blocks):
        at = o_rows + b * ks
        extra_ref[at : at + ks, :] = down_table[:, b * lanes : (b + 1) * lanes]
    at = o_rows + blocks * ks
    extra_ref[at:, :] = jnp.zeros((ks, lanes), jnp.bfloat16)
    extra_ref[at:, :width] = up_table
    for copy in copies[4:]:
        copy.wait()


def load_kernel(
    n, seq, c_x_hbm, c_m_hbm, c_len_hbm, p_x_hbm, p_m_hbm, p_len_hbm,
    x_ref, m_ref, send_ref, c_len, p_len, sems,
):
    half = c_x_hbm.shape[0]
    moves = (
        (c_len_hbm, c_len), (p_len_hbm, p_len),
        (c_m_hbm, m_ref.at[pl.ds(0, half)]), (p_m_hbm, m_ref.at[pl.ds(half, half)]),
        (c_x_hbm, x_ref.at[pl.ds(0, half)]), (p_x_hbm, x_ref.at[pl.ds(half, half)]),
    )
    copies = [pltpu.make_async_copy(a, b, sems.at[i]) for i, (a, b) in enumerate(moves)]
    for copy in copies:
        copy.start()
    for copy in copies:
        copy.wait()
    for side, lengths in enumerate((c_len, p_len)):
        for e in range(half // seq):
            rows = pl.ds(side * half + e * seq, seq)
            for ref in (x_ref, m_ref):
                dead = lax.broadcasted_iota(jnp.int32, (seq, ref.shape[1]), 0) >= lengths[e]
                ref[rows, :] = jnp.where(dead, jnp.zeros((), ref.dtype), ref[rows, :])
    other = 1 - lax.axis_index("fsdp") % 2
    at = 0
    for ref in (x_ref, m_ref):
        wide = ref.shape[1] // n
        for b in range(n // 2):
            first = pl.multiple_of((2 * b + other) * wide, wide)
            send_ref[:, at : at + wide] = ref[:, pl.ds(first, wide)]
            at += wide


def spans(n, x, m, xo, j, sketch, first, count):
    source, wide, base = ((x, x.shape[1] // n, 0), (m, m.shape[1] // n, (n // 2) * (x.shape[1] // n)))[sketch]
    here = pl.ds(pl.multiple_of(j * wide + first, 128), count)
    there = pl.ds(pl.multiple_of(base + (j // 2) * wide + first, 128), count)
    return source[:, here], xo[:, there]


def small_sums(n, ks, places, x, m, xo, refs):
    me, plane = lax.axis_index("fsdp"), lax.axis_index("dp")
    ku = m.shape[1] // n
    sums = [[0.0, 0.0], [0.0, 0.0]]
    for r, at, kind in places:
        j = partner(me, kind, plane)
        lanes = refs[r].shape[1]
        blocks = x.shape[1] // n // lanes
        up = refs[r][at + blocks * ks : at + (blocks + 1) * ks, :ku]
        for who, rows in enumerate(spans(n, x, m, xo, j, 1, 0, ku)):
            sums[who][0] += dot_last(rows, up)
        table = jnp.concatenate([refs[r][at + b * ks : at + (b + 1) * ks, :] for b in range(blocks)], axis=1)
        for who, rows in enumerate(spans(n, x, m, xo, j, 0, 0, blocks * lanes)):
            sums[who][1] += dot_last(rows, table)
    return sums


def products(n, places, x, m, xo, refs):
    me, plane = lax.axis_index("fsdp"), lax.axis_index("dp")
    sums = [[0.0, 0.0], [0.0, 0.0]]
    for ref, row, kind, sketch, first, count in places:
        piece = refs[ref][row : row + count, :]
        for who, rows in enumerate(spans(n, x, m, xo, partner(me, kind, plane), sketch, first, count)):
            sums[who][sketch] += dot(rows, piece)
    return sums


def early_kernel(n, ks, places, tables, x, m, xo, *refs):
    refs, (sums_ref, small_ref) = refs[:-2], refs[-2:]
    sums = products(n, places, x, m, xo, refs)
    small = small_sums(n, ks, tables, x, m, xo, refs)
    for who in range(2):
        for t in range(2):
            sums_ref[who, t] = sums[who][t]
            small_ref[who, t] = small[who][t]


def late_kernel(n, ks, side, places, tables, x, m, xo, sums, early_small, *refs):
    refs, (keep, keep_small, send, wide, narrow) = refs[:-5], refs[-5:]
    core = lax.axis_index("fsdp") % 2
    half = x.shape[0] // 2
    rows = pl.ds(side * half, half)
    views = x.at[rows], m.at[rows], xo.at[rows]
    late = products(n, places, *views, refs)
    late_small = small_sums(n, ks, tables, *views, refs)
    for t in range(2):
        for who in range(2):
            wide[t, who * half : (who + 1) * half, :] = late[who][t] + sums[who, t, rows, :]
        both = [late_small[who][t] + early_small[who, t, rows, :] for who in range(2)]
        narrow[t] = jnp.concatenate(both, axis=0).T
    keep[...] = wide[core]
    keep_small[...] = narrow[core]
    for who in range(2):
        first = (1 - who) * half
        send[who * half : (who + 1) * half, :] = wide[1 - core, first : first + half, :].astype(jnp.bfloat16)
    small = narrow[1 - core]
    high, low = split_two(jnp.concatenate([small[:, half:], small[:, :half]], axis=1))
    send[2 * half : 2 * half + ks, :] = high
    send[2 * half + ks :, :] = low


def gradients(seq, keep, keep_small, got):
    rows, ks = keep.shape[0], keep_small.shape[0]
    small = keep_small[...] + got[rows : rows + ks, :].astype(jnp.float32) + got[rows + ks :, :].astype(jnp.float32)
    count = rows // seq
    tiled = jnp.concatenate([small] * count, axis=0)
    e_row = lax.broadcasted_iota(jnp.int32, tiled.shape, 0) // ks
    e_col = lax.broadcasted_iota(jnp.int32, tiled.shape, 1) // seq
    factor = jnp.where(e_row == e_col, tiled, 0.0).astype(jnp.bfloat16)
    total = keep[...] + got[:rows, :].astype(jnp.float32)
    return dot(factor, total.astype(jnp.bfloat16))


def flatten(grads, ks, out, scratch, base=0):
    cols, lanes = grads.shape[1], scratch.shape[2]
    for b in range(cols // lanes):
        scratch[b] = grads[:, b * lanes : (b + 1) * lanes]
    for k in range(ks):
        for b in range(cols // lanes):
            at = base + k * cols + b * lanes
            rows = pl.ds(k, grads.shape[0] // ks, stride=ks)
            out[:, at : at + lanes] = scratch[b, rows, :].astype(out.dtype)


def probe_kernel(seq, keep, keep_small, got, out, scratch):
    flatten(gradients(seq, keep, keep_small, got), keep_small.shape[0], out, scratch)


def candidate_kernel(seq, keep, keep_small, got, out, own, send, scratch):
    grads = gradients(seq, keep, keep_small, got)
    flatten(grads, keep_small.shape[0], out, scratch)
    half = grads.shape[0] // 2
    own[...] = grads[:half]
    send[...] = grads[half:]


def feature_kernel(ks, own, got, out, scratch):
    core = lax.axis_index("fsdp") % 2
    left = jnp.where(core == 0, own[...], got[...])
    right = jnp.where(core == 0, got[...], own[...])
    rows, cols = left.shape
    square = (left * left + right * right).reshape(rows // ks, ks, cols)
    scale = lax.rsqrt(jnp.sum(square, axis=(1, 2), keepdims=True) / (2 * ks * cols) + eps_mean)
    for t, part in enumerate((left, right)):
        scaled = (part.reshape(rows // ks, ks, cols) * scale).reshape(rows, cols)
        flatten(scaled, ks, out, scratch, t * ks * cols)


def score_kernel(kinds, c_ref, *refs):
    probes, (own_ref, send_ref) = refs[:-2], refs[-2:]
    me = lax.axis_index("fsdp")
    cands = c_ref[...]
    per = cands.shape[0] // 2
    held = jnp.concatenate([ref[...] for ref in probes], axis=0)
    width = held.shape[0]
    mixed = dot_last(jnp.concatenate([cands, held], axis=0), held)
    scores, gram = mixed[: 2 * per], mixed[2 * per :]

    def diagonal(square, axis):
        rows = lax.broadcasted_iota(jnp.int32, square.shape, 0)
        cols = lax.broadcasted_iota(jnp.int32, square.shape, 1)
        return jnp.sum(jnp.where(rows == cols, square, 0.0), axis=axis, keepdims=True)

    rows = jnp.concatenate([scores, jnp.broadcast_to(diagonal(gram, 0), scores.shape)], axis=0)
    group = lax.broadcasted_iota(jnp.int32, rows.shape, 1) // per
    placed = jnp.zeros(rows.shape, jnp.float32)
    for g in range(width // per):
        block = jnp.concatenate([rows[:, g * per : (g + 1) * per]] * (width // per), axis=1)
        placed = jnp.where(group == (me ^ kinds[g // 2] ^ (g % 2)), block, placed)
    squares = jnp.broadcast_to(diagonal(dot_last(cands, cands), 1), (2 * per, width))
    for i, ref in enumerate((own_ref, send_ref)):
        ref[:per, :] = placed[i * per : (i + 1) * per]
        ref[per : 2 * per, :] = placed[2 * per : 3 * per]
        ref[2 * per :, :] = squares[i * per : (i + 1) * per]


def final_kernel(entries, own, got, out):
    total = own[...] + got[...]
    per = out.shape[0]
    scale = lax.rsqrt(total[per:] / entries + eps_mean)
    out[...] = total[:per] * scale[:per] * scale[per:] / entries


def swap(x, k, axis, size):
    return lax.ppermute(x, axis, [(i, i ^ k) for i in range(size)])


def fast_body(n, planes, c_x, c_m, c_len, p_x, p_m, p_len, down, up, sketch_in, sketch_out, rank_down, rank_up):
    examples, seq, model = c_x.shape
    value = c_m.shape[2]
    ks, kp = rank_down.shape[1], sketch_in.shape[1]
    s_rows, o_rows = sketch_in.shape[0], sketch_out.shape[0]
    t_rows = (s_rows // kp + 1) * ks
    sw = functools.partial(swap, axis="fsdp", size=n)

    def along(x, second):
        pairs = []
        for i in range(n):
            for z in range(planes):
                way = first_way(i % 2, z)
                pairs.append((i * planes + z, (i ^ (6 - way if second else way)) * planes + z))
        return lax.ppermute(x, ("fsdp", "dp"), pairs)

    def array(*shape, dtype=jnp.bfloat16):
        return jax.ShapeDtypeStruct(shape, dtype)

    def kernel(f, name, outs, operands, in_specs=None, scratch=(), limit=8):
        return pl.pallas_call(
            f,
            out_shape=outs,
            in_specs=in_specs or [VMEM] * len(operands),
            out_specs=(VMEM,) * len(outs) if isinstance(outs, tuple) else VMEM,
            scratch_shapes=scratch,
            compiler_params=pltpu.CompilerParams(vmem_limit_bytes=limit * MIB),
            cost_estimate=SHORT,
            name=name,
        )(*operands)

    beside = s_rows * 5 // 8 // 128 * 128
    extra, own, tail = kernel(
        pack_kernel,
        "pack_weights",
        (array(o_rows + t_rows, kp), array(s_rows, kp), array(s_rows - beside + o_rows, kp)),
        in_hbm(down, up, rank_down.T, rank_up.T, sketch_in, sketch_out),
        in_specs=[HBM] * 6,
        scratch=[
            pltpu.VMEM(down.shape, down.dtype),
            pltpu.VMEM(up.shape, up.dtype),
            pltpu.VMEM(rank_down.shape[::-1], rank_down.dtype),
            pltpu.VMEM(rank_up.shape[::-1], rank_up.dtype),
            pltpu.SemaphoreType.DMA((8,)),
        ],
    )
    flat = (examples * seq, model)
    flat_m = (examples * seq, value)
    rows = 2 * examples * seq
    x, m, send = kernel(
        functools.partial(load_kernel, n, seq),
        "load_rows",
        (array(rows, model), array(rows, value), array(rows, (model + value) // 2)),
        in_hbm(c_x.reshape(flat), c_m.reshape(flat_m), c_len, p_x.reshape(flat), p_m.reshape(flat_m), p_len),
        in_specs=[HBM] * 6,
        scratch=[
            pltpu.SMEM(c_len.shape, c_len.dtype),
            pltpu.SMEM(p_len.shape, p_len.dtype),
            pltpu.SemaphoreType.DMA((6,)),
        ],
    )

    first, first_extra = along(sketch_in, False), along(extra, False)
    first, first_extra, x, m, send = lax.optimization_barrier((first, first_extra, x, m, send))

    more = along(jnp.concatenate([first, first_extra, tail]), True)
    rest = swap(jnp.concatenate([first[:beside], first_extra[o_rows:]]), 1, "dp", planes)
    xo = sw(send, 1)

    f32 = jnp.float32
    early_places = (
        (0, 0, 0, 0, 0, s_rows), (1, 0, 0, 1, 0, o_rows), (2, 0, 1, 0, 0, s_rows), (3, 0, 1, 1, 0, o_rows),
    )
    sums, small = kernel(
        functools.partial(early_kernel, n, ks, early_places, ((1, o_rows, 0), (3, o_rows, 1))),
        "early_products",
        (array(2, 2, rows, kp, dtype=f32), array(2, 2, rows, ks, dtype=f32)),
        (x, m, xo, own, extra, first, first_extra),
    )
    t_at = s_rows + o_rows
    tail_at = t_at + t_rows
    left_rows = s_rows - beside
    late_places = (
        (0, 0, 3, 0, 0, s_rows), (0, s_rows, 3, 1, 0, o_rows),
        (0, tail_at, 2, 0, beside, left_rows), (0, tail_at + left_rows, 2, 1, 0, o_rows),
        (1, 0, 2, 0, 0, beside),
    )

    def late(side, name):
        keep, keep_small, out = kernel(
            functools.partial(late_kernel, n, ks, side, late_places, ((0, t_at, 3), (1, beside, 2))),
            name,
            (array(rows, kp, dtype=f32), array(ks, rows, dtype=f32), array(rows + 2 * ks, kp)),
            (x, m, xo, sums, small, more, rest),
            scratch=[pltpu.VMEM((2, rows, kp), f32), pltpu.VMEM((2, ks, rows), f32)],
        )
        return keep, keep_small, sw(out, 1)

    total = 2 * examples * ks
    side = array(2 * examples, ks * kp)

    def scratch(count):
        return [pltpu.VMEM((kp // 128, count, 128), f32)]

    p_side = kernel(
        functools.partial(probe_kernel, seq), "probe_sides", side, late(1, "probe_products"), scratch=scratch(total)
    )
    grads = array(total // 2, kp, dtype=f32)
    c_side, c_grads, c_send = kernel(
        functools.partial(candidate_kernel, seq),
        "candidate_sides",
        (side, grads, grads),
        late(0, "candidate_products"),
        scratch=scratch(total),
    )
    c_feat = kernel(
        functools.partial(feature_kernel, ks),
        "candidate_features",
        array(examples, 2 * ks * kp),
        (c_grads, sw(c_send, 1)),
        scratch=scratch(total // 2),
    )

    kinds = (0, 6, 4, 2)
    got = [sw(p_side, k) for k in kinds[1:]]
    c_side, *got = lax.optimization_barrier((c_side, *got))
    part = array(3 * examples, n * examples, dtype=f32)
    scores, to_other = kernel(
        functools.partial(score_kernel, kinds), "score_shares", (part, part), (c_side, p_side, *got)
    )
    scores = kernel(
        functools.partial(final_kernel, 2 * ks * kp),
        "scores",
        array(examples, n * examples, dtype=f32),
        (scores, sw(to_other, 1)),
    )
    return scores, c_feat


def plain_features(x, m, lengths, down, up, sketch_in, sketch_out, rank_down, rank_up):
    examples, seq, model = x.shape
    ks, kp = rank_down.shape[1], sketch_in.shape[1]
    live = (lax.broadcasted_iota(jnp.int32, (examples, seq), 1) < lengths[:, None]).astype(m.dtype)
    masked = (m * live[:, :, None]).reshape(examples * seq, -1)
    rows = x.reshape(examples * seq, model)
    grad_rows = dot(masked, up).astype(jnp.bfloat16)
    outward = dot(masked, sketch_out).astype(jnp.bfloat16)
    down_round = dot(rows, down).astype(jnp.bfloat16)
    inward = dot(rows, sketch_in).astype(jnp.bfloat16)
    left_small = dot(grad_rows, rank_down).astype(jnp.bfloat16)
    right_small = dot(down_round, rank_up).astype(jnp.bfloat16)

    def outer(small, wide):
        return jnp.einsum(
            "esk,esp->ekp",
            small.reshape(examples, seq, ks),
            wide.reshape(examples, seq, kp),
            preferred_element_type=jnp.float32,
        )

    joined = jnp.concatenate([outer(left_small, inward), outer(right_small, outward)], axis=1)
    joined = joined.reshape(examples, 2 * ks * kp)
    scale = lax.rsqrt(jnp.mean(joined * joined, axis=1, keepdims=True) + eps_mean)
    return (joined * scale).astype(jnp.bfloat16)


def plain_body(c_x, c_m, c_len, p_x, p_m, p_len, down, up, sketch_in, sketch_out, rank_down, rank_up):
    weights = [
        lax.all_gather(w, "fsdp", axis=0, tiled=True) for w in (down, up, sketch_in, sketch_out)
    ]
    p_feat = plain_features(p_x, p_m, p_len, *weights, rank_down, rank_up)
    c_feat = plain_features(c_x, c_m, c_len, *weights, rank_down, rank_up)
    every = lax.all_gather(p_feat, "fsdp", axis=0, tiled=True)
    return dot(c_feat, every.T) / c_feat.shape[1], c_feat


def solution(mesh):
    n, planes = mesh.shape["fsdp"], mesh.shape["dp"]
    rows = P(("dp", "fsdp"), None)
    cube = P(("dp", "fsdp"), None, None)
    line = P(("dp", "fsdp"))
    shard = P("fsdp", None)
    in_specs = (cube, cube, line, cube, cube, line, shard, shard, shard, shard, P(), P())

    def body(*args):
        if n == 1 << 3 and planes % 2 == 0:
            return fast_body(n, planes, *args)
        return plain_body(*args)

    return jax.shard_map(body, mesh=mesh, in_specs=in_specs, out_specs=(rows, rows), check_vma=False)
```

time: 40.1 us -> 38.4 us (0.958)
  waiting for transfers between devices: 17.2 us -> 15.5 us
    ppermute x3, waiting for transfers between devices: 4.64 us -> 3.66 us  [along(): return lax.ppermute(x, ('fsdp', 'dp'), pairs)]
    ppermute x9, waiting for transfers between devices: 12.5 us -> 11.9 us  [swap(): return lax.ppermute(x, axis, [(i, i ^ k) for i in range(size)])]
    pallas_call x11 -> x10, Pallas kernels: 10.5 us -> 10.7 us  [kernel(): pl.pallas_call(f, out_shape=outs, in_specs=in_specs or [VMEM] * len(opera...]
  transfers between devices with their start and end apart: 12 -> 12, of which waited for: 7 -> 8; matrix products, arithmetic and copies ran while one was open for 0% -> 0% of each run, Pallas kernels for 22% -> 24%
where the time goes in v4:
time: 38.4 us; the launch traced here: 38.3 us
  waiting for transfers between devices  15.5 us (40%)
  starting transfers between devices  11.2 us (29%)
  Pallas kernels  10.7 us (28%)
  between operations  0.74 us (2%)
    ppermute x9, waiting for transfers between devices, swap(): return lax.ppermute(x, axis, [(i, i ^ k) for i in range(size)])  11.9 us
    pallas_call x10, Pallas kernels, kernel(): pl.pallas_call(f, out_shape=outs, in_specs=in_specs or [VMEM] * len(opera...  10.7 us
    ppermute x9, starting transfers between devices, swap(): return lax.ppermute(x, axis, [(i, i ^ k) for i in range(size)])  5.99 us
    ppermute x3, starting transfers between devices, along(): return lax.ppermute(x, ('fsdp', 'dp'), pairs)  5.2 us
    ppermute x3, waiting for transfers between devices, along(): return lax.ppermute(x, ('fsdp', 'dp'), pairs)  3.66 us
  transfers between devices with their start and end apart: 12, of which 8 were waited for; matrix products, arithmetic and copies ran while one was open for 0% of the time, Pallas kernels for 24%

profile of v4, /device:TPU:0, one launch (start us, length us, event | category | flops | bytes accessed | tf_op | source)
XLA Modules:
  0.0 38.3 jit_solution(9700457996464935809)
XLA Ops:
  0.6 3.0 %collective-permute-start = (bf16[1024,256]{1,0:T(8,128)(2,1)}, bf16[1024,256]{1,0:T(8,128)(2,1)S(1)}, u32[]{:S(2)}, u32[]{:S(2)}) collective-permute-start(bf16[1024,256]{1,0:T(8,128)(2,1)} %in_hbm.1), channel_id=1, source_target_pairs={{0,8},{1,17},{2,10},{3,19},{4,20},{5,13},{6,22},{7,15},{8,0},{9,25... | collective-permute-start | bytes 1572872 | tf_op jit(solution)/shard_map/ppermute | solution.py:280
  3.6 1.4 %pack_weights.1 = (bf16[208,256]{1,0:T(8,128)(2,1)S(1)}, bf16[1024,256]{1,0:T(8,128)(2,1)S(1)}, bf16[512,256]{1,0:T(8,128)(2,1)S(1)}) custom-call(bf16[1024,128]{1,0:T(8,128)(2,1)} %down_hbm.1, bf16[128,128]{1,0:T(8,128)(2,1)} %up_hbm.1, bf16[16,128]{1,0:T(8,128)(2,1)} %bitcast.10, bf16[16,128]{1,0:T(8,128)(2,1)} %bitcast.11, bf16[1024,256]{1,0:T(8,128)(2,1)} %in_hbm.1, ...), custom_call_target="tpu_custom_call" | custom-call | flops 1 | bytes 1 | tf_op jit(solution)/shard_map/pack_weights/pallas_call | solution.py:286
  5.0 0.1 collective-permute-start.1
  5.1 3.6 %load_rows.1 = (bf16[256,8192]{1,0:T(8,128)(2,1)S(1)}, bf16[256,1024]{1,0:T(8,128)(2,1)S(1)}, bf16[256,4608]{1,0:T(8,128)(2,1)S(1)}) custom-call(bf16[128,8192]{1,0:T(8,128)(2,1)} %bitcast.6, bf16[128,1024]{1,0:T(8,128)(2,1)} %bitcast.8, s32[4]{0:T(128)} %c_len_hbm.1, bf16[128,8192]{1,0:T(8,128)(2,1)} %bitcast.7, bf16[128,1024]{1,0:T(8,128)(2,1)} %bitcast.9, ...), custom_call_target="tpu_custom_call" | custom-call | flops 1 | bytes 1 | tf_op jit(solution)/shard_map/load_rows/pallas_call | solution.py:286
  8.8 3.4 %collective-permute-done.1.refs_3_ = bf16[208,256]{1,0:T(8,128)(2,1)S(1)} collective-permute-done((bf16[208,256]{1,0:T(8,128)(2,1)S(1)}, bf16[208,256]{1,0:T(8,128)(2,1)S(1)}, u32[]{:S(2)}, u32[]{:S(2)}) %collective-permute-start.1) | collective-permute-done | bytes 106528 | tf_op jit(solution)/shard_map/ppermute | solution.py:280
  12.1 0.0 collective-permute-done.refs_2_
  12.2 0.1 pad_maximum_fusion
  12.2 2.1 %collective-permute-start.3 = (bf16[1744,256]{1,0:T(8,128)(2,1)S(1)}, bf16[1744,256]{1,0:T(8,128)(2,1)S(1)}, u32[]{:S(2)}, u32[]{:S(2)}) collective-permute-start(bf16[1744,256]{1,0:T(8,128)(2,1)S(1)} %pad_maximum_fusion), channel_id=1, source_target_pairs={{0,16},{1,9},{2,18},{3,11},{4,12},{5,21},{6,14},{7,23},{8,24},{9,1... | collective-permute-start | bytes 2678792 | tf_op jit(solution)/shard_map/ppermute | solution.py:280
  14.4 1.6 %collective-permute-start.4 = (bf16[720,256]{1,0:T(8,128)(2,1)S(1)}, bf16[720,256]{1,0:T(8,128)(2,1)S(1)}, u32[]{:S(2)}, u32[]{:S(2)}) collective-permute-start(bf16[720,256]{1,0:T(8,128)(2,1)S(1)} %pad_maximum_fusion.1), channel_id=1, source_target_pairs={{0,1},{1,0},{2,3},{3,2},{4,5},{5,4},{6,7},{7,6},{8,9},{9,8},{10,11... | collective-permute-start | bytes 1105928 | tf_op jit(solution)/shard_map/ppermute | solution.py:263
  16.0 0.7 %collective-permute-done.2.xo = bf16[256,4608]{1,0:T(8,128)(2,1)S(1)} collective-permute-done((bf16[256,4608]{1,0:T(8,128)(2,1)S(1)}, bf16[256,4608]{1,0:T(8,128)(2,1)S(1)}, u32[]{:S(2)}, u32[]{:S(2)}) %collective-permute-start.2) | collective-permute-done | bytes 2359328 | tf_op jit(solution)/shard_map/ppermute | solution.py:263
  16.7 1.5 %early_products.1 = (f32[2,2,256,256]{3,2,1,0:T(8,128)S(1)}, f32[2,2,256,16]{3,2,1,0:T(8,128)S(1)}) custom-call(bf16[256,8192]{1,0:T(8,128)(2,1)S(1)} %get-tuple-element.34.x, bf16[256,1024]{1,0:T(8,128)(2,1)S(1)} %get-tuple-element.35.m, bf16[256,4608]{1,0:T(8,128)(2,1)S(1)} %collective-permute-done.2.xo, bf16[1024,256]{1,0:T(8,128)(2,1)S(1)} %get-tuple-element.37.refs_0_, ...), custom_call_target="tpu_custom_call" | custom-call | flops 1 | bytes 1 | tf_op jit(solution)/shard_map/early_products/pallas_call | solution.py:286
  18.1 7.0 %collective-permute-done.4.refs_1_ = bf16[720,256]{1,0:T(8,128)(2,1)S(1)} collective-permute-done((bf16[720,256]{1,0:T(8,128)(2,1)S(1)}, bf16[720,256]{1,0:T(8,128)(2,1)S(1)}, u32[]{:S(2)}, u32[]{:S(2)}) %collective-permute-start.4) | collective-permute-done | bytes 368672 | tf_op jit(solution)/shard_map/ppermute | solution.py:263
  25.2 0.3 collective-permute-done.3.refs_0_
  25.4 1.0 %probe_products.1 = (f32[256,256]{1,0:T(8,128)S(1)}, f32[16,256]{1,0:T(8,128)S(1)}, bf16[288,256]{1,0:T(8,128)(2,1)S(1)}) custom-call(bf16[256,8192]{1,0:T(8,128)(2,1)S(1)} %get-tuple-element.34.x, bf16[256,1024]{1,0:T(8,128)(2,1)S(1)} %get-tuple-element.35.m, bf16[256,4608]{1,0:T(8,128)(2,1)S(1)} %collective-permute-done.2.xo, ...), custom_call_target="tpu_custom_call" | custom-call | flops 1 | bytes 1 | tf_op jit(solution)/shard_map/probe_products/pallas_call | solution.py:286
  26.5 0.0 collective-permute-start.6
  26.5 1.0 %candidate_products.1 = (f32[256,256]{1,0:T(8,128)S(1)}, f32[16,256]{1,0:T(8,128)S(1)}, bf16[288,256]{1,0:T(8,128)(2,1)S(1)}) custom-call(bf16[256,8192]{1,0:T(8,128)(2,1)S(1)} %get-tuple-element.34.x, bf16[256,1024]{1,0:T(8,128)(2,1)S(1)} %get-tuple-element.35.m, bf16[256,4608]{1,0:T(8,128)(2,1)S(1)} %collective-permute-done.2.xo, ...), custom_call_target="tpu_custom_call" | custom-call | flops 1 | bytes 1 | tf_op jit(solution)/shard_map/candidate_products/pallas_call | solution.py:286
  27.5 0.5 %collective-permute-start.5 = (bf16[288,256]{1,0:T(8,128)(2,1)S(1)}, bf16[288,256]{1,0:T(8,128)(2,1)S(1)}, u32[]{:S(2)}, u32[]{:S(2)}) collective-permute-start(bf16[288,256]{1,0:T(8,128)(2,1)S(1)} %get-tuple-element.45), channel_id=1, source_target_pairs={{0,4},{4,0},{8,12},{12,8},{16,20},{20,16},{24,28},{28,24},{1,5},{5... | collective-permute-start | bytes 442376 | tf_op jit(solution)/shard_map/ppermute | solution.py:263
  28.0 0.2 probe_sides.1.refs_0_
  28.3 3.0 %collective-permute-start.7 = (bf16[8,4096]{1,0:T(8,128)(2,1)S(1)}, bf16[8,4096]{1,0:T(8,128)(2,1)S(1)}, u32[]{:S(2)}, u32[]{:S(2)}) collective-permute-start(bf16[8,4096]{1,0:T(8,128)(2,1)S(1)} %probe_sides.1.refs_0_), channel_id=1, source_target_pairs={{0,24},{4,28},{8,16},{12,20},{16,8},{20,12},{24,0},{28,4},{1,25},{... | collective-permute-start | bytes 196616 | tf_op jit(solution)/shard_map/ppermute | solution.py:263
  31.3 0.5 %collective-permute-start.8 = (bf16[8,4096]{1,0:T(8,128)(2,1)S(1)}, bf16[8,4096]{1,0:T(8,128)(2,1)S(1)}, u32[]{:S(2)}, u32[]{:S(2)}) collective-permute-start(bf16[8,4096]{1,0:T(8,128)(2,1)S(1)} %probe_sides.1.refs_0_), channel_id=1, source_target_pairs={{0,16},{4,20},{8,24},{12,28},{16,0},{20,4},{24,8},{28,12},{1,17},{... | collective-permute-start | bytes 196616 | tf_op jit(solution)/shard_map/ppermute | solution.py:263
  31.8 0.1 collective-permute-start.9
  31.9 0.0 collective-permute-done.5.got
  31.9 0.2 candidate_sides.1
  32.1 0.1 collective-permute-start.11
  32.2 1.3 %collective-permute-done.7.refs_1_ = bf16[8,4096]{1,0:T(8,128)(2,1)S(1)} collective-permute-done((bf16[8,4096]{1,0:T(8,128)(2,1)S(1)}, bf16[8,4096]{1,0:T(8,128)(2,1)S(1)}, u32[]{:S(2)}, u32[]{:S(2)}) %collective-permute-start.7) | collective-permute-done | bytes 65568 | tf_op jit(solution)/shard_map/ppermute | solution.py:263
  33.6 2.0 %collective-permute-done.8.refs_2_ = bf16[8,4096]{1,0:T(8,128)(2,1)S(1)} collective-permute-done((bf16[8,4096]{1,0:T(8,128)(2,1)S(1)}, bf16[8,4096]{1,0:T(8,128)(2,1)S(1)}, u32[]{:S(2)}, u32[]{:S(2)}) %collective-permute-start.8) | collective-permute-done | bytes 65568 | tf_op jit(solution)/shard_map/ppermute | solution.py:263
  35.5 0.5 %collective-permute-done.9.refs_3_ = bf16[8,4096]{1,0:T(8,128)(2,1)S(1)} collective-permute-done((bf16[8,4096]{1,0:T(8,128)(2,1)S(1)}, bf16[8,4096]{1,0:T(8,128)(2,1)S(1)}, u32[]{:S(2)}, u32[]{:S(2)}) %collective-permute-start.9) | collective-permute-done | bytes 65568 | tf_op jit(solution)/shard_map/ppermute | solution.py:263
  36.1 0.4 %score_shares.1 = (f32[12,32]{1,0:T(8,128)S(1)}, f32[12,32]{1,0:T(8,128)S(1)}) custom-call(bf16[8,4096]{1,0:T(8,128)(2,1)S(1)} %get-tuple-element.50.c_ref, bf16[8,4096]{1,0:T(8,128)(2,1)S(1)} %probe_sides.1.refs_0_, bf16[8,4096]{1,0:T(8,128)(2,1)S(1)} %collective-permute-done.7.refs_1_, bf16[8,4096]{1,0:T(8,128)(2,1)S(1)} %collective-permute-done.8.refs_2_, ...), custom_call_target="tpu_custom_call" | custom-call | flops 1 | bytes 1 | tf_op jit(solution)/shard_map/score_shares/pallas_call | solution.py:286
  36.5 0.1 collective-permute-start.10
  36.5 0.8 %candidate_features.1 = bf16[4,8192]{1,0:T(4,128)(2,1)} custom-call(f32[64,256]{1,0:T(8,128)S(1)} %get-tuple-element.56.own, f32[64,256]{1,0:T(8,128)S(1)} %collective-permute-done.11.got), custom_call_target="tpu_custom_call" | custom-call | flops 1 | bytes 1 | tf_op jit(solution)/shard_map/candidate_features/pallas_call | solution.py:286
  37.4 0.3 collective-permute-done.10.got
  37.7 0.6 %scores.1 = f32[4,32]{1,0:T(4,128)} custom-call(f32[12,32]{1,0:T(8,128)S(1)} %get-tuple-element.54.own, f32[12,32]{1,0:T(8,128)S(1)} %collective-permute-done.10.got), custom_call_target="tpu_custom_call" | custom-call | flops 1 | bytes 1 | tf_op jit(solution)/shard_map/scores/pallas_call | solution.py:286
  (6 shorter events, 0.1 us)
Async XLA Ops:
  0.6 11.5 %collective-permute-start = (bf16[1024,256]{1,0:T(8,128)(2,1)}, bf16[1024,256]{1,0:T(8,128)(2,1)S(1)}, u32[]{:S(2)}, u32[]{:S(2)}) collective-permute-start(bf16[1024,256]{1,0:T(8,128)(2,1)} %in_hbm.1), channel_id=1, source_target_pairs={{0,8},{1,17},{2,10},{3,19},{4,20},{5,13},{6,22},{7,15},{8,0},{9,25... | collective-permute-start | bytes 1572872 | tf_op jit(solution)/shard_map/ppermute | solution.py:280
  5.0 7.1 %collective-permute-start.1 = (bf16[208,256]{1,0:T(8,128)(2,1)S(1)}, bf16[208,256]{1,0:T(8,128)(2,1)S(1)}, u32[]{:S(2)}, u32[]{:S(2)}) collective-permute-start(bf16[208,256]{1,0:T(8,128)(2,1)S(1)} %get-tuple-element.30.refs_1_), channel_id=1, source_target_pairs={{0,8},{1,17},{2,10},{3,19},{4,20},{5,13},{6,22},{7,15},{8,0},{9,25... | collective-permute-start | bytes 319496 | tf_op jit(solution)/shard_map/ppermute | solution.py:280
  12.2 4.5 %collective-permute-start.2 = (bf16[256,4608]{1,0:T(8,128)(2,1)S(1)}, bf16[256,4608]{1,0:T(8,128)(2,1)S(1)}, u32[]{:S(2)}, u32[]{:S(2)}) collective-permute-start(bf16[256,4608]{1,0:T(8,128)(2,1)S(1)} %get-tuple-element.36), channel_id=1, source_target_pairs={{0,4},{4,0},{8,12},{12,8},{16,20},{20,16},{24,28},{28,24},{1,5},{5... | collective-permute-start | bytes 7077896 | tf_op jit(solution)/shard_map/ppermute | solution.py:263
  12.2 13.2 %collective-permute-start.3 = (bf16[1744,256]{1,0:T(8,128)(2,1)S(1)}, bf16[1744,256]{1,0:T(8,128)(2,1)S(1)}, u32[]{:S(2)}, u32[]{:S(2)}) collective-permute-start(bf16[1744,256]{1,0:T(8,128)(2,1)S(1)} %pad_maximum_fusion), channel_id=1, source_target_pairs={{0,16},{1,9},{2,18},{3,11},{4,12},{5,21},{6,14},{7,23},{8,24},{9,1... | collective-permute-start | bytes 2678792 | tf_op jit(solution)/shard_map/ppermute | solution.py:280
  14.4 10.8 %collective-permute-start.4 = (bf16[720,256]{1,0:T(8,128)(2,1)S(1)}, bf16[720,256]{1,0:T(8,128)(2,1)S(1)}, u32[]{:S(2)}, u32[]{:S(2)}) collective-permute-start(bf16[720,256]{1,0:T(8,128)(2,1)S(1)} %pad_maximum_fusion.1), channel_id=1, source_target_pairs={{0,1},{1,0},{2,3},{3,2},{4,5},{5,4},{6,7},{7,6},{8,9},{9,8},{10,11... | collective-permute-start | bytes 1105928 | tf_op jit(solution)/shard_map/ppermute | solution.py:263
  26.5 1.6 %collective-permute-start.6 = (bf16[288,256]{1,0:T(8,128)(2,1)S(1)}, bf16[288,256]{1,0:T(8,128)(2,1)S(1)}, u32[]{:S(2)}, u32[]{:S(2)}) collective-permute-start(bf16[288,256]{1,0:T(8,128)(2,1)S(1)} %get-tuple-element.49), channel_id=1, source_target_pairs={{0,4},{4,0},{8,12},{12,8},{16,20},{20,16},{24,28},{28,24},{1,5},{5... | collective-permute-start | bytes 442376 | tf_op jit(solution)/shard_map/ppermute | solution.py:263
  27.5 4.4 %collective-permute-start.5 = (bf16[288,256]{1,0:T(8,128)(2,1)S(1)}, bf16[288,256]{1,0:T(8,128)(2,1)S(1)}, u32[]{:S(2)}, u32[]{:S(2)}) collective-permute-start(bf16[288,256]{1,0:T(8,128)(2,1)S(1)} %get-tuple-element.45), channel_id=1, source_target_pairs={{0,4},{4,0},{8,12},{12,8},{16,20},{20,16},{24,28},{28,24},{1,5},{5... | collective-permute-start | bytes 442376 | tf_op jit(solution)/shard_map/ppermute | solution.py:263
  28.3 5.3 %collective-permute-start.7 = (bf16[8,4096]{1,0:T(8,128)(2,1)S(1)}, bf16[8,4096]{1,0:T(8,128)(2,1)S(1)}, u32[]{:S(2)}, u32[]{:S(2)}) collective-permute-start(bf16[8,4096]{1,0:T(8,128)(2,1)S(1)} %probe_sides.1.refs_0_), channel_id=1, source_target_pairs={{0,24},{4,28},{8,16},{12,20},{16,8},{20,12},{24,0},{28,4},{1,25},{... | collective-permute-start | bytes 196616 | tf_op jit(solution)/shard_map/ppermute | solution.py:263
  31.3 4.3 %collective-permute-start.8 = (bf16[8,4096]{1,0:T(8,128)(2,1)S(1)}, bf16[8,4096]{1,0:T(8,128)(2,1)S(1)}, u32[]{:S(2)}, u32[]{:S(2)}) collective-permute-start(bf16[8,4096]{1,0:T(8,128)(2,1)S(1)} %probe_sides.1.refs_0_), channel_id=1, source_target_pairs={{0,16},{4,20},{8,24},{12,28},{16,0},{20,4},{24,8},{28,12},{1,17},{... | collective-permute-start | bytes 196616 | tf_op jit(solution)/shard_map/ppermute | solution.py:263
  31.8 4.3 %collective-permute-start.9 = (bf16[8,4096]{1,0:T(8,128)(2,1)S(1)}, bf16[8,4096]{1,0:T(8,128)(2,1)S(1)}, u32[]{:S(2)}, u32[]{:S(2)}) collective-permute-start(bf16[8,4096]{1,0:T(8,128)(2,1)S(1)} %probe_sides.1.refs_0_), channel_id=1, source_target_pairs={{0,8},{4,12},{8,0},{12,4},{16,24},{20,28},{24,16},{28,20},{1,9},{5... | collective-permute-start | bytes 196616 | tf_op jit(solution)/shard_map/ppermute | solution.py:263
  32.1 4.4 %collective-permute-start.11 = (f32[64,256]{1,0:T(8,128)S(1)}, f32[64,256]{1,0:T(8,128)S(1)}, u32[]{:S(2)}, u32[]{:S(2)}) collective-permute-start(f32[64,256]{1,0:T(8,128)S(1)} %get-tuple-element.57), channel_id=1, source_target_pairs={{0,4},{4,0},{8,12},{12,8},{16,20},{20,16},{24,28},{28,24},{1,5},{5... | collective-permute-start | bytes 196616 | tf_op jit(solution)/shard_map/ppermute | solution.py:263
  36.5 1.2 %collective-permute-start.10 = (f32[12,32]{1,0:T(8,128)S(1)}, f32[12,32]{1,0:T(8,128)S(1)}, u32[]{:S(2)}, u32[]{:S(2)}) collective-permute-start(f32[12,32]{1,0:T(8,128)S(1)} %get-tuple-element.55), channel_id=1, source_target_pairs={{0,4},{4,0},{8,12},{12,8},{16,20},{20,16},{24,28},{28,24},{1,5},{5... | collective-permute-start | bytes 4616 | tf_op jit(solution)/shard_map/ppermute | solution.py:263

commit v5 on v4

--- a/solution.py
+++ b/solution.py
@@ -42,26 +42,33 @@
     return me ^ (0, first, 6 - first, 6)[kind]
 
 
-def pack_kernel(
-    down_hbm, up_hbm, rank_down_hbm, rank_up_hbm, in_hbm, out_hbm,
-    extra_ref, own_ref, tail_ref, down_ref, up_ref, rank_down_ref, rank_up_ref, sems,
+def prepare_kernel(
+    n, seq, down_hbm, up_hbm, rank_down_hbm, rank_up_hbm, in_hbm, out_hbm,
+    c_x_hbm, c_m_hbm, c_len_hbm, p_x_hbm, p_m_hbm, p_len_hbm,
+    extra_ref, tail_ref, x_ref, m_ref, live_ref, c_send, p_send,
+    down_ref, up_ref, rank_down_ref, rank_up_ref, c_len, p_len, sems,
 ):
-    s_rows, o_rows = in_hbm.shape[0], out_hbm.shape[0]
-    tail = tail_ref.shape[0] - o_rows
+    o_rows, half = out_hbm.shape[0], c_x_hbm.shape[0]
+    s_rows, tail = in_hbm.shape[0], tail_ref.shape[0]
     moves = (
         (down_hbm, down_ref),
         (up_hbm, up_ref),
         (rank_down_hbm, rank_down_ref),
         (rank_up_hbm, rank_up_ref),
+        (c_len_hbm, c_len),
+        (p_len_hbm, p_len),
         (out_hbm, extra_ref.at[pl.ds(0, o_rows)]),
-        (out_hbm, tail_ref.at[pl.ds(tail, o_rows)]),
-        (in_hbm.at[pl.ds(s_rows - tail, tail)], tail_ref.at[pl.ds(0, tail)]),
-        (in_hbm, own_ref),
+        (in_hbm.at[pl.ds(s_rows - tail, tail)], tail_ref),
+    )
+    moves += tuple(
+        (source.at[pl.ds(e * seq, seq)], to.at[pl.ds(base + e * seq, seq)])
+        for source, to, base in ((c_m_hbm, m_ref, 0), (c_x_hbm, x_ref, 0), (p_m_hbm, m_ref, half), (p_x_hbm, x_ref, half))
+        for e in range(half // seq)
     )
     copies = [pltpu.make_async_copy(a, b, sems.at[i]) for i, (a, b) in enumerate(moves)]
     for copy in copies:
         copy.start()
-    for copy in copies[:4]:
+    for copy in copies[:6]:
         copy.wait()
     down_table = dot_last(rank_up_ref[...], down_ref[...]).astype(jnp.bfloat16)
     up_table = dot_last(rank_down_ref[...], up_ref[...]).astype(jnp.bfloat16)
@@ -74,97 +81,115 @@
     at = o_rows + blocks * ks
     extra_ref[at:, :] = jnp.zeros((ks, lanes), jnp.bfloat16)
     extra_ref[at:, :width] = up_table
-    for copy in copies[4:]:
+    lane = lax.broadcasted_iota(jnp.int32, live_ref.shape[1:], 1)
+    for side, lengths in enumerate((c_len, p_len)):
+        live = jnp.zeros(live_ref.shape[1:], jnp.bool_)
+        for e in range(half // seq):
+            live = live | ((lane >= e * seq) & (lane < e * seq + lengths[e]))
+        live_ref[side] = live.astype(jnp.float32).astype(live_ref.dtype)
+    other = 1 - lax.axis_index("fsdp") % 2
+    examples = half // seq
+    kd, ku = x_ref.shape[1] // n, m_ref.shape[1] // n
+    for copy in copies[6:8]:
         copy.wait()
-
-
-def load_kernel(
-    n, seq, c_x_hbm, c_m_hbm, c_len_hbm, p_x_hbm, p_m_hbm, p_len_hbm,
-    x_ref, m_ref, send_ref, c_len, p_len, sems,
-):
-    half = c_x_hbm.shape[0]
-    moves = (
-        (c_len_hbm, c_len), (p_len_hbm, p_len),
-        (c_m_hbm, m_ref.at[pl.ds(0, half)]), (p_m_hbm, m_ref.at[pl.ds(half, half)]),
-        (c_x_hbm, x_ref.at[pl.ds(0, half)]), (p_x_hbm, x_ref.at[pl.ds(half, half)]),
-    )
-    copies = [pltpu.make_async_copy(a, b, sems.at[i]) for i, (a, b) in enumerate(moves)]
-    for copy in copies:
-        copy.start()
-    for copy in copies:
-        copy.wait()
-    for side, lengths in enumerate((c_len, p_len)):
-        for e in range(half // seq):
-            rows = pl.ds(side * half + e * seq, seq)
-            for ref in (x_ref, m_ref):
-                dead = lax.broadcasted_iota(jnp.int32, (seq, ref.shape[1]), 0) >= lengths[e]
-                ref[rows, :] = jnp.where(dead, jnp.zeros((), ref.dtype), ref[rows, :])
-    other = 1 - lax.axis_index("fsdp") % 2
-    at = 0
-    for ref in (x_ref, m_ref):
-        wide = ref.shape[1] // n
-        for b in range(n // 2):
-            first = pl.multiple_of((2 * b + other) * wide, wide)
-            send_ref[:, at : at + wide] = ref[:, pl.ds(first, wide)]
-            at += wide
-
-
-def spans(n, x, m, xo, j, sketch, first, count):
+    for side, send_ref in enumerate((c_send, p_send)):
+        for ref, wide, base, turn in ((m_ref, ku, (n // 2) * kd, 0), (x_ref, kd, 0, 1)):
+            for e in range(examples):
+                copies[8 + (2 * side + turn) * examples + e].wait()
+                rows = pl.ds(e * seq, seq)
+                for b in range(n // 2):
+                    first = pl.multiple_of((2 * b + other) * wide, wide)
+                    at = base + b * wide
+                    send_ref[rows, at : at + wide] = ref[pl.ds(side * half + e * seq, seq), pl.ds(first, wide)]
+
+
+def spans(n, x, m, xo, block, sketch, first, count):
+    kind, core, whos = block
+    j = partner(lax.axis_index("fsdp") ^ core, kind, lax.axis_index("dp"))
     source, wide, base = ((x, x.shape[1] // n, 0), (m, m.shape[1] // n, (n // 2) * (x.shape[1] // n)))[sketch]
-    here = pl.ds(pl.multiple_of(j * wide + first, 128), count)
-    there = pl.ds(pl.multiple_of(base + (j // 2) * wide + first, 128), count)
-    return source[:, here], xo[:, there]
+    for who in whos:
+        if who == 0:
+            yield who, source[:, pl.ds(pl.multiple_of(j * wide + first, 128), count)]
+        else:
+            yield who, xo[:, pl.ds(pl.multiple_of(base + (j // 2) * wide + first, 128), count)]
 
 
 def small_sums(n, ks, places, x, m, xo, refs):
-    me, plane = lax.axis_index("fsdp"), lax.axis_index("dp")
     ku = m.shape[1] // n
     sums = [[0.0, 0.0], [0.0, 0.0]]
-    for r, at, kind in places:
-        j = partner(me, kind, plane)
+    for r, at, block in places:
         lanes = refs[r].shape[1]
         blocks = x.shape[1] // n // lanes
         up = refs[r][at + blocks * ks : at + (blocks + 1) * ks, :ku]
-        for who, rows in enumerate(spans(n, x, m, xo, j, 1, 0, ku)):
+        for who, rows in spans(n, x, m, xo, block, 1, 0, ku):
             sums[who][0] += dot_last(rows, up)
         table = jnp.concatenate([refs[r][at + b * ks : at + (b + 1) * ks, :] for b in range(blocks)], axis=1)
-        for who, rows in enumerate(spans(n, x, m, xo, j, 0, 0, blocks * lanes)):
+        for who, rows in spans(n, x, m, xo, block, 0, 0, blocks * lanes):
             sums[who][1] += dot_last(rows, table)
     return sums
 
 
 def products(n, places, x, m, xo, refs):
-    me, plane = lax.axis_index("fsdp"), lax.axis_index("dp")
     sums = [[0.0, 0.0], [0.0, 0.0]]
-    for ref, row, kind, sketch, first, count in places:
+    for ref, row, block, sketch, first, count in places:
         piece = refs[ref][row : row + count, :]
-        for who, rows in enumerate(spans(n, x, m, xo, partner(me, kind, plane), sketch, first, count)):
+        for who, rows in spans(n, x, m, xo, block, sketch, first, count):
             sums[who][sketch] += dot(rows, piece)
     return sums
 
 
-def early_kernel(n, ks, places, tables, x, m, xo, *refs):
+def own_kernel(n, ks, places, tables, in_hbm, extra, x, m, own, second, sums_ref, small_ref, sems):
+    extra_rows = extra.shape[0]
+    part = second.shape[0] - extra_rows
+    first = in_hbm.shape[0] * 3 // 8 // 128 * 128
+    copies = [
+        pltpu.make_async_copy(in_hbm, own, sems.at[0]),
+        pltpu.make_async_copy(in_hbm.at[pl.ds(first, part)], second.at[pl.ds(0, part)], sems.at[1]),
+    ]
+    for copy in copies:
+        copy.start()
+    second[part:, :] = extra[...]
+    half = x.shape[0] // 2
+    views = [(x.at[pl.ds(side * half, half)], m.at[pl.ds(side * half, half)], None) for side in range(2)]
+    for side in range(2):
+        small = small_sums(n, ks, tables, *views[side], (extra,))
+        for t in range(2):
+            small_ref[side, t] = small[0][t]
+    for copy in copies:
+        copy.wait()
+    for side in range(2):
+        sums = products(n, places, *views[side], (extra, own))
+        for t in range(2):
+            sums_ref[side, t] = sums[0][t]
+
+
+def early_kernel(n, ks, places, tables, x, m, c_xo, p_xo, own_sums, own_small, *refs):
     refs, (sums_ref, small_ref) = refs[:-2], refs[-2:]
-    sums = products(n, places, x, m, xo, refs)
-    small = small_sums(n, ks, tables, x, m, xo, refs)
-    for who in range(2):
+    half = c_xo.shape[0]
+    for side, xo in enumerate((c_xo, p_xo)):
+        rows = pl.ds(side * half, half)
+        views = x.at[rows], m.at[rows], xo
+        small = small_sums(n, ks, tables, *views, refs)
+        sums = products(n, places, *views, refs)
         for t in range(2):
-            sums_ref[who, t] = sums[who][t]
-            small_ref[who, t] = small[who][t]
-
-
-def late_kernel(n, ks, side, places, tables, x, m, xo, sums, early_small, *refs):
+            small_ref[side, 0, t] = small[0][t] + own_small[side, t]
+            small_ref[side, 1, t] = small[1][t]
+            sums_ref[side, 0, t] = sums[0][t] + own_sums[side, t]
+            sums_ref[side, 1, t] = sums[1][t]
+
+
+def late_kernel(n, ks, side, places, tables, x, m, xo, live, sums, early_small, *refs):
     refs, (keep, keep_small, send, wide, narrow) = refs[:-5], refs[-5:]
     core = lax.axis_index("fsdp") % 2
     half = x.shape[0] // 2
     rows = pl.ds(side * half, half)
-    views = x.at[rows], m.at[rows], xo.at[rows]
+    views = x.at[rows], m.at[rows], xo
     late = products(n, places, *views, refs)
     late_small = small_sums(n, ks, tables, *views, refs)
     for t in range(2):
         for who in range(2):
-            wide[t, who * half : (who + 1) * half, :] = late[who][t] + sums[who, t, rows, :]
-        both = [late_small[who][t] + early_small[who, t, rows, :] for who in range(2)]
+            wide[t, who * half : (who + 1) * half, :] = late[who][t] + sums[side, who, t]
+        both = [late_small[who][t] + early_small[side, who, t] for who in range(2)]
         narrow[t] = jnp.concatenate(both, axis=0).T
     keep[...] = wide[core]
     keep_small[...] = narrow[core]
@@ -174,12 +199,17 @@
     small = narrow[1 - core]
     high, low = split_two(jnp.concatenate([small[:, half:], small[:, :half]], axis=1))
     send[2 * half : 2 * half + ks, :] = high
-    send[2 * half + ks :, :] = low
-
-
-def gradients(seq, keep, keep_small, got):
+    send[2 * half + ks : 2 * half + 2 * ks, :] = low
+    send[2 * half + 2 * ks :, :half] = live[side]
+    send[2 * half + 2 * ks :, half:] = live[side]
+
+
+def gradients(seq, side, keep, keep_small, got, live):
     rows, ks = keep.shape[0], keep_small.shape[0]
-    small = keep_small[...] + got[rows : rows + ks, :].astype(jnp.float32) + got[rows + ks :, :].astype(jnp.float32)
+    high, low = (got[at : at + ks, :].astype(jnp.float32) for at in (rows, rows + ks))
+    there = got[rows + 2 * ks : rows + 2 * ks + 1, rows // 2 :]
+    lives = jnp.concatenate([live[side, :1, :].astype(jnp.float32), there.astype(jnp.float32)], axis=1)
+    small = jnp.where(lives > 0, keep_small[...] + high + low, 0.0)
     count = rows // seq
     tiled = jnp.concatenate([small] * count, axis=0)
     e_row = lax.broadcasted_iota(jnp.int32, tiled.shape, 0) // ks
@@ -200,12 +230,12 @@
             out[:, at : at + lanes] = scratch[b, rows, :].astype(out.dtype)
 
 
-def probe_kernel(seq, keep, keep_small, got, out, scratch):
-    flatten(gradients(seq, keep, keep_small, got), keep_small.shape[0], out, scratch)
-
-
-def candidate_kernel(seq, keep, keep_small, got, out, own, send, scratch):
-    grads = gradients(seq, keep, keep_small, got)
+def probe_kernel(seq, keep, keep_small, got, live, out, scratch):
+    flatten(gradients(seq, 1, keep, keep_small, got, live), keep_small.shape[0], out, scratch)
+
+
+def candidate_kernel(seq, keep, keep_small, got, live, out, own, send, scratch):
+    grads = gradients(seq, 0, keep, keep_small, got, live)
     flatten(grads, keep_small.shape[0], out, scratch)
     half = grads.shape[0] // 2
     own[...] = grads[:half]
@@ -294,69 +324,95 @@
             name=name,
         )(*operands)
 
-    beside = s_rows * 5 // 8 // 128 * 128
-    extra, own, tail = kernel(
-        pack_kernel,
-        "pack_weights",
-        (array(o_rows + t_rows, kp), array(s_rows, kp), array(s_rows - beside + o_rows, kp)),
-        in_hbm(down, up, rank_down.T, rank_up.T, sketch_in, sketch_out),
-        in_specs=[HBM] * 6,
+    flat = (examples * seq, model)
+    flat_m = (examples * seq, value)
+    rows = 2 * examples * seq
+    beside, part = s_rows * 3 // 8 // 128 * 128, s_rows // 2
+    tail = s_rows - beside - part
+    extra, last, x, m, live, c_cols, p_cols = kernel(
+        functools.partial(prepare_kernel, n, seq),
+        "prepare",
+        (
+            array(o_rows + t_rows, kp),
+            array(tail, kp),
+            array(rows, model),
+            array(rows, value),
+            array(2, 16, rows // 2),
+            array(rows // 2, (model + value) // 2),
+            array(rows // 2, (model + value) // 2),
+        ),
+        in_hbm(
+            down, up, rank_down.T, rank_up.T, sketch_in, sketch_out,
+            c_x.reshape(flat), c_m.reshape(flat_m), c_len, p_x.reshape(flat), p_m.reshape(flat_m), p_len,
+        ),
+        in_specs=[HBM] * 12,
         scratch=[
             pltpu.VMEM(down.shape, down.dtype),
             pltpu.VMEM(up.shape, up.dtype),
             pltpu.VMEM(rank_down.shape[::-1], rank_down.dtype),
             pltpu.VMEM(rank_up.shape[::-1], rank_up.dtype),
-            pltpu.SemaphoreType.DMA((8,)),
-        ],
-    )
-    flat = (examples * seq, model)
-    flat_m = (examples * seq, value)
-    rows = 2 * examples * seq
-    x, m, send = kernel(
-        functools.partial(load_kernel, n, seq),
-        "load_rows",
-        (array(rows, model), array(rows, value), array(rows, (model + value) // 2)),
-        in_hbm(c_x.reshape(flat), c_m.reshape(flat_m), c_len, p_x.reshape(flat), p_m.reshape(flat_m), p_len),
-        in_specs=[HBM] * 6,
-        scratch=[
             pltpu.SMEM(c_len.shape, c_len.dtype),
             pltpu.SMEM(p_len.shape, p_len.dtype),
-            pltpu.SemaphoreType.DMA((6,)),
+            pltpu.SemaphoreType.DMA((8 + 4 * examples,)),
         ],
     )
 
+    f32 = jnp.float32
+    here, there, both = (0,), (1,), (0, 1)
+    own, second, own_sums, own_small = kernel(
+        functools.partial(
+            own_kernel, n, ks,
+            ((0, 0, (0, 0, here), 1, 0, o_rows), (1, 0, (0, 0, here), 0, 0, s_rows)),
+            ((0, o_rows, (0, 0, here)),),
+        ),
+        "own_products",
+        (
+            array(s_rows, kp),
+            array(part + o_rows + t_rows, kp),
+            array(2, 2, rows // 2, kp, dtype=f32),
+            array(2, 2, rows // 2, ks, dtype=f32),
+        ),
+        (*in_hbm(sketch_in), extra, x, m),
+        in_specs=[HBM] + [VMEM] * 3,
+        scratch=[pltpu.SemaphoreType.DMA((2,))],
+    )
+
     first, first_extra = along(sketch_in, False), along(extra, False)
-    first, first_extra, x, m, send = lax.optimization_barrier((first, first_extra, x, m, send))
-
-    more = along(jnp.concatenate([first, first_extra, tail]), True)
-    rest = swap(jnp.concatenate([first[:beside], first_extra[o_rows:]]), 1, "dp", planes)
-    xo = sw(send, 1)
-
-    f32 = jnp.float32
+    second = along(second, True)
+    c_xo, p_xo = sw(c_cols, 1), sw(p_cols, 1)
+
+    more = along(jnp.concatenate([first, first_extra, last]), True)
+    rest = swap(first[:beside], 1, "dp", planes)
+    second_other = sw(second, 1)
+
+    t_at = part + o_rows
     early_places = (
-        (0, 0, 0, 0, 0, s_rows), (1, 0, 0, 1, 0, o_rows), (2, 0, 1, 0, 0, s_rows), (3, 0, 1, 1, 0, o_rows),
+        (0, 0, (0, 0, there), 1, 0, o_rows), (1, 0, (1, 0, both), 0, 0, s_rows), (2, 0, (1, 0, both), 1, 0, o_rows),
+        (3, 0, (2, 0, here), 0, beside, part), (3, part, (2, 0, here), 1, 0, o_rows),
+        (4, 0, (2, 1, here), 0, beside, part), (4, part, (2, 1, here), 1, 0, o_rows),
+        (5, 0, (0, 0, there), 0, 0, s_rows),
+    )
+    early_tables = (
+        (0, o_rows, (0, 0, there)), (2, o_rows, (1, 0, both)), (3, t_at, (2, 0, here)), (4, t_at, (2, 1, here)),
     )
     sums, small = kernel(
-        functools.partial(early_kernel, n, ks, early_places, ((1, o_rows, 0), (3, o_rows, 1))),
+        functools.partial(early_kernel, n, ks, early_places, early_tables),
         "early_products",
-        (array(2, 2, rows, kp, dtype=f32), array(2, 2, rows, ks, dtype=f32)),
-        (x, m, xo, own, extra, first, first_extra),
-    )
-    t_at = s_rows + o_rows
-    tail_at = t_at + t_rows
-    left_rows = s_rows - beside
+        (array(2, 2, 2, rows // 2, kp, dtype=f32), array(2, 2, 2, rows // 2, ks, dtype=f32)),
+        (x, m, c_xo, p_xo, own_sums, own_small, extra, first, first_extra, second, second_other, own),
+    )
     late_places = (
-        (0, 0, 3, 0, 0, s_rows), (0, s_rows, 3, 1, 0, o_rows),
-        (0, tail_at, 2, 0, beside, left_rows), (0, tail_at + left_rows, 2, 1, 0, o_rows),
-        (1, 0, 2, 0, 0, beside),
+        (0, 0, (3, 0, both), 0, 0, s_rows), (0, s_rows, (3, 0, both), 1, 0, o_rows),
+        (0, s_rows + o_rows + t_rows, (2, 0, both), 0, beside + part, tail),
+        (1, 0, (2, 0, both), 0, 0, beside),
     )
 
     def late(side, name):
         keep, keep_small, out = kernel(
-            functools.partial(late_kernel, n, ks, side, late_places, ((0, t_at, 3), (1, beside, 2))),
+            functools.partial(late_kernel, n, ks, side, late_places, ((0, s_rows + o_rows, (3, 0, both)),)),
             name,
-            (array(rows, kp, dtype=f32), array(ks, rows, dtype=f32), array(rows + 2 * ks, kp)),
-            (x, m, xo, sums, small, more, rest),
+            (array(rows, kp, dtype=f32), array(ks, rows, dtype=f32), array(rows + 2 * ks + 16, kp)),
+            (x, m, (c_xo, p_xo)[side], live, sums, small, more, rest),
             scratch=[pltpu.VMEM((2, rows, kp), f32), pltpu.VMEM((2, ks, rows), f32)],
         )
         return keep, keep_small, sw(out, 1)
@@ -368,14 +424,14 @@
         return [pltpu.VMEM((kp // 128, count, 128), f32)]
 
     p_side = kernel(
-        functools.partial(probe_kernel, seq), "probe_sides", side, late(1, "probe_products"), scratch=scratch(total)
+        functools.partial(probe_kernel, seq), "probe_sides", side, (*late(1, "probe_products"), live), scratch=scratch(total)
     )
     grads = array(total // 2, kp, dtype=f32)
     c_side, c_grads, c_send = kernel(
         functools.partial(candidate_kernel, seq),
         "candidate_sides",
         (side, grads, grads),
-        late(0, "candidate_products"),
+        (*late(0, "candidate_products"), live),
         scratch=scratch(total),
     )
     c_feat = kernel(

time: 38.4 us -> 37 us (0.964)
  waiting for transfers between devices: 15.5 us -> 11.6 us
  starting transfers between devices: 11.2 us -> 14.9 us
  Pallas kernels: 10.7 us -> 9.54 us
    ppermute x9 -> x11, waiting for transfers between devices: 11.9 us -> 7.75 us  [swap(): return lax.ppermute(x, axis, [(i, i ^ k) for i in range(size)])]
    ppermute x3 -> x4, starting transfers between devices: 5.2 us -> 7.75 us  [along(): return lax.ppermute(x, ('fsdp', 'dp'), pairs)]
    ppermute x9 -> x11, starting transfers between devices: 5.99 us -> 7.19 us  [swap(): return lax.ppermute(x, axis, [(i, i ^ k) for i in range(size)])]
    pallas_call x10, Pallas kernels: 10.7 us -> 9.54 us  [kernel(): pl.pallas_call(f, out_shape=outs, in_specs=in_specs or [VMEM] * len(opera...]
    ppermute x3 -> x4, waiting for transfers between devices: 3.66 us -> 3.84 us  [along(): return lax.ppermute(x, ('fsdp', 'dp'), pairs)]
  transfers between devices with their start and end apart: 12 -> 15, of which waited for: 8 -> 8; matrix products, arithmetic and copies ran while one was open for 0% -> 0% of each run, Pallas kernels for 24% -> 22%
where the time goes in v5:
time: 37 us; the launch traced here: 36.9 us
  starting transfers between devices  14.9 us (40%)
  waiting for transfers between devices  11.6 us (31%)
  Pallas kernels  9.54 us (26%)
  between operations  0.74 us (2%)
    pallas_call x10, Pallas kernels, kernel(): pl.pallas_call(f, out_shape=outs, in_specs=in_specs or [VMEM] * len(opera...  9.54 us
    ppermute x4, starting transfers between devices, along(): return lax.ppermute(x, ('fsdp', 'dp'), pairs)  7.75 us
    ppermute x11, waiting for transfers between devices, swap(): return lax.ppermute(x, axis, [(i, i ^ k) for i in range(size)])  7.75 us
    ppermute x11, starting transfers between devices, swap(): return lax.ppermute(x, axis, [(i, i ^ k) for i in range(size)])  7.19 us
    ppermute x4, waiting for transfers between devices, along(): return lax.ppermute(x, ('fsdp', 'dp'), pairs)  3.84 us
  transfers between devices with their start and end apart: 15, of which 8 were waited for; matrix products, arithmetic and copies ran while one was open for 0% of the time, Pallas kernels for 22%

profile of v5, /device:TPU:0, one launch (start us, length us, event | category | flops | bytes accessed | tf_op | source)
XLA Modules:
  0.0 36.9 jit_solution(13279928122289929503)
XLA Ops:
  0.6 3.0 %collective-permute-start.2 = (bf16[1024,256]{1,0:T(8,128)(2,1)}, bf16[1024,256]{1,0:T(8,128)(2,1)S(1)}, u32[]{:S(2)}, u32[]{:S(2)}) collective-permute-start(bf16[1024,256]{1,0:T(8,128)(2,1)} %in_hbm.3), channel_id=1, source_target_pairs={{0,8},{1,17},{2,10},{3,19},{4,20},{5,13},{6,22},{7,15},{8,0},{9,25... | collective-permute-start | bytes 1572872 | tf_op jit(solution)/shard_map/ppermute | solution.py:310
  3.6 2.8 %prepare.1 = (bf16[208,256]{1,0:T(8,128)(2,1)S(1)}, bf16[128,256]{1,0:T(8,128)(2,1)S(1)}, bf16[256,8192]{1,0:T(8,128)(2,1)S(1)}, bf16[256,1024]{1,0:T(8,128)(2,1...) custom-call(bf16[1024,128]{1,0:T(8,128)(2,1)} %down_hbm.1, ...), custom_call_target="tpu_custom_call" | custom-call | flops 1 | bytes 1 | tf_op jit(solution)/shard_map/prepare/pallas_call | solution.py:316
  6.4 0.1 collective-permute-start
  6.5 0.5 %collective-permute-start.1 = (bf16[128,4608]{1,0:T(8,128)(2,1)S(1)}, bf16[128,4608]{1,0:T(8,128)(2,1)S(1)}, u32[]{:S(2)}, u32[]{:S(2)}) collective-permute-start(bf16[128,4608]{1,0:T(8,128)(2,1)S(1)} %get-tuple-element.34), channel_id=1, source_target_pairs={{0,4},{4,0},{8,12},{12,8},{16,20},{20,16},{24,28},{28,24},{1,5},{5... | collective-permute-start | bytes 3538952 | tf_op jit(solution)/shard_map/ppermute | solution.py:293
  7.0 0.6 %collective-permute-start.3 = (bf16[208,256]{1,0:T(8,128)(2,1)S(1)}, bf16[208,256]{1,0:T(8,128)(2,1)S(1)}, u32[]{:S(2)}, u32[]{:S(2)}) collective-permute-start(bf16[208,256]{1,0:T(8,128)(2,1)S(1)} %get-tuple-element.35.extra.refs_0_), channel_id=1, source_target_pairs={{0,8},{1,17},{2,10},{3,19},{4,20},{5,13},{6,22},{7,15},{8,0},{9,25... | collective-permute-start | bytes 319496 | tf_op jit(solution)/shard_map/ppermute | solution.py:310
  7.6 1.5 %own_products.1 = (bf16[1024,256]{1,0:T(8,128)(2,1)S(1)}, bf16[720,256]{1,0:T(8,128)(2,1)S(1)}, f32[2,2,128,256]{3,2,1,0:T(8,128)S(1)}, f32[2,2,128,16]{3,2,1,0:T(8,128)S(1)}) custom-call(bf16[1024,256]{1,0:T(8,128)(2,1)} %in_hbm.3, bf16[208,256]{1,0:T(8,128)(2,1)S(1)} %get-tuple-element.35.extra.refs_0_, bf16[256,8192]{1,0:T(8,128)(2,1)S(1)} %get-tuple-element.30.x, ...), custom_call_target="tpu_custom_call" | custom-call | flops 1 | bytes 1 | tf_op jit(solution)/shard_map/own_products/pallas_call | solution.py:316
  9.1 1.5 %collective-permute-start.4 = (bf16[720,256]{1,0:T(8,128)(2,1)S(1)}, bf16[720,256]{1,0:T(8,128)(2,1)S(1)}, u32[]{:S(2)}, u32[]{:S(2)}) collective-permute-start(bf16[720,256]{1,0:T(8,128)(2,1)S(1)} %get-tuple-element.38), channel_id=1, source_target_pairs={{0,16},{1,9},{2,18},{3,11},{4,12},{5,21},{6,14},{7,23},{8,24},{9,1... | collective-permute-start | bytes 1105928 | tf_op jit(solution)/shard_map/ppermute | solution.py:310
  10.6 2.2 %collective-permute-done.3.refs_2_ = bf16[208,256]{1,0:T(8,128)(2,1)S(1)} collective-permute-done((bf16[208,256]{1,0:T(8,128)(2,1)S(1)}, bf16[208,256]{1,0:T(8,128)(2,1)S(1)}, u32[]{:S(2)}, u32[]{:S(2)}) %collective-permute-start.3) | collective-permute-done | bytes 106528 | tf_op jit(solution)/shard_map/ppermute | solution.py:310
  12.9 2.6 %collective-permute-start.6 = (bf16[1360,256]{1,0:T(8,128)(2,1)S(1)}, bf16[1360,256]{1,0:T(8,128)(2,1)S(1)}, u32[]{:S(2)}, u32[]{:S(2)}) collective-permute-start(bf16[1360,256]{1,0:T(8,128)(2,1)S(1)} %pad_maximum_fusion), channel_id=1, source_target_pairs={{0,16},{1,9},{2,18},{3,11},{4,12},{5,21},{6,14},{7,23},{8,24},{9,1... | collective-permute-start | bytes 2088968 | tf_op jit(solution)/shard_map/ppermute | solution.py:310
  15.5 1.2 %collective-permute-done.4.refs_3_ = bf16[720,256]{1,0:T(8,128)(2,1)S(1)} collective-permute-done((bf16[720,256]{1,0:T(8,128)(2,1)S(1)}, bf16[720,256]{1,0:T(8,128)(2,1)S(1)}, u32[]{:S(2)}, u32[]{:S(2)}) %collective-permute-start.4) | collective-permute-done | bytes 368672 | tf_op jit(solution)/shard_map/ppermute | solution.py:310
  16.7 1.7 %collective-permute-start.7 = (bf16[384,256]{1,0:T(8,128)(2,1)S(1)}, bf16[384,256]{1,0:T(8,128)(2,1)S(1)}, u32[]{:S(2)}, u32[]{:S(2)}) collective-permute-start(bf16[384,256]{1,0:T(8,128)(2,1)S(1)} %slice.4), channel_id=1, source_target_pairs={{0,1},{1,0},{2,3},{3,2},{4,5},{5,4},{6,7},{7,6},{8,9},{9,8},{10,11... | collective-permute-start | bytes 589832 | tf_op jit(solution)/shard_map/ppermute | solution.py:293
  18.4 0.0 collective-permute-done.c_xo.xo
  18.4 1.7 %early_products.1 = (f32[2,2,2,128,256]{4,3,2,1,0:T(8,128)S(1)}, f32[2,2,2,128,16]{4,3,2,1,0:T(8,128)S(1)}) custom-call(bf16[256,8192]{1,0:T(8,128)(2,1)S(1)} %get-tuple-element.30.x, bf16[256,1024]{1,0:T(8,128)(2,1)S(1)} %get-tuple-element.31.m, bf16[128,4608]{1,0:T(8,128)(2,1)S(1)} %collective-permute-done.c_xo.xo, ...), custom_call_target="tpu_custom_call" | custom-call | flops 1 | bytes 1 | tf_op jit(solution)/shard_map/early_products/pallas_call | solution.py:316
  20.1 4.0 %collective-permute-done.7.refs_1_ = bf16[384,256]{1,0:T(8,128)(2,1)S(1)} collective-permute-done((bf16[384,256]{1,0:T(8,128)(2,1)S(1)}, bf16[384,256]{1,0:T(8,128)(2,1)S(1)}, u32[]{:S(2)}, u32[]{:S(2)}) %collective-permute-start.7) | collective-permute-done | bytes 196640 | tf_op jit(solution)/shard_map/ppermute | solution.py:293
  24.1 0.4 %collective-permute-done.6.refs_0_ = bf16[1360,256]{1,0:T(8,128)(2,1)S(1)} collective-permute-done((bf16[1360,256]{1,0:T(8,128)(2,1)S(1)}, bf16[1360,256]{1,0:T(8,128)(2,1)S(1)}, u32[]{:S(2)}, u32[]{:S(2)}) %collective-permute-start.6) | collective-permute-done | bytes 696352 | tf_op jit(solution)/shard_map/ppermute | solution.py:310
  24.5 0.7 %probe_products.1 = (f32[256,256]{1,0:T(8,128)S(1)}, f32[16,256]{1,0:T(8,128)S(1)}, bf16[304,256]{1,0:T(8,128)(2,1)S(1)}) custom-call(bf16[256,8192]{1,0:T(8,128)(2,1)S(1)} %get-tuple-element.30.x, bf16[256,1024]{1,0:T(8,128)(2,1)S(1)} %get-tuple-element.31.m, bf16[128,4608]{1,0:T(8,128)(2,1)S(1)} %collective-permute-done.1.p_xo.xo, ...), custom_call_target="tpu_custom_call" | custom-call | flops 1 | bytes 1 | tf_op jit(solution)/shard_map/probe_products/pallas_call | solution.py:316
  25.2 0.1 collective-permute-start.9
  25.3 0.7 %candidate_products.1 = (f32[256,256]{1,0:T(8,128)S(1)}, f32[16,256]{1,0:T(8,128)S(1)}, bf16[304,256]{1,0:T(8,128)(2,1)S(1)}) custom-call(bf16[256,8192]{1,0:T(8,128)(2,1)S(1)} %get-tuple-element.30.x, bf16[256,1024]{1,0:T(8,128)(2,1)S(1)} %get-tuple-element.31.m, bf16[128,4608]{1,0:T(8,128)(2,1)S(1)} %collective-permute-done.c_xo.xo, ...), custom_call_target="tpu_custom_call" | custom-call | flops 1 | bytes 1 | tf_op jit(solution)/shard_map/candidate_products/pallas_call | solution.py:316
  26.0 0.6 %collective-permute-start.8 = (bf16[304,256]{1,0:T(8,128)(2,1)S(1)}, bf16[304,256]{1,0:T(8,128)(2,1)S(1)}, u32[]{:S(2)}, u32[]{:S(2)}) collective-permute-start(bf16[304,256]{1,0:T(8,128)(2,1)S(1)} %get-tuple-element.45), channel_id=1, source_target_pairs={{0,4},{4,0},{8,12},{12,8},{16,20},{20,16},{24,28},{28,24},{1,5},{5... | collective-permute-start | bytes 466952 | tf_op jit(solution)/shard_map/ppermute | solution.py:293
  26.6 0.1 collective-permute-done.9.got
  26.7 0.2 probe_sides.1.refs_0_
  26.9 3.5 %collective-permute-start.10 = (bf16[8,4096]{1,0:T(8,128)(2,1)S(1)}, bf16[8,4096]{1,0:T(8,128)(2,1)S(1)}, u32[]{:S(2)}, u32[]{:S(2)}) collective-permute-start(bf16[8,4096]{1,0:T(8,128)(2,1)S(1)} %probe_sides.1.refs_0_), channel_id=1, source_target_pairs={{0,24},{4,28},{8,16},{12,20},{16,8},{20,12},{24,0},{28,4},{1,25},{... | collective-permute-start | bytes 196616 | tf_op jit(solution)/shard_map/ppermute | solution.py:293
  30.4 0.6 %collective-permute-start.12 = (bf16[8,4096]{1,0:T(8,128)(2,1)S(1)}, bf16[8,4096]{1,0:T(8,128)(2,1)S(1)}, u32[]{:S(2)}, u32[]{:S(2)}) collective-permute-start(bf16[8,4096]{1,0:T(8,128)(2,1)S(1)} %probe_sides.1.refs_0_), channel_id=1, source_target_pairs={{0,8},{4,12},{8,0},{12,4},{16,24},{20,28},{24,16},{28,20},{1,9},{5... | collective-permute-start | bytes 196616 | tf_op jit(solution)/shard_map/ppermute | solution.py:293
  31.0 0.2 candidate_sides.1
  31.3 0.1 collective-permute-start.14
  31.3 1.4 %collective-permute-done.10.refs_1_ = bf16[8,4096]{1,0:T(8,128)(2,1)S(1)} collective-permute-done((bf16[8,4096]{1,0:T(8,128)(2,1)S(1)}, bf16[8,4096]{1,0:T(8,128)(2,1)S(1)}, u32[]{:S(2)}, u32[]{:S(2)}) %collective-permute-start.10) | collective-permute-done | bytes 65568 | tf_op jit(solution)/shard_map/ppermute | solution.py:293
  32.8 1.9 %collective-permute-done.11.refs_2_ = bf16[8,4096]{1,0:T(8,128)(2,1)S(1)} collective-permute-done((bf16[8,4096]{1,0:T(8,128)(2,1)S(1)}, bf16[8,4096]{1,0:T(8,128)(2,1)S(1)}, u32[]{:S(2)}, u32[]{:S(2)}) %collective-permute-start.11) | collective-permute-done | bytes 65568 | tf_op jit(solution)/shard_map/ppermute | solution.py:293
  34.7 0.4 %score_shares.1 = (f32[12,32]{1,0:T(8,128)S(1)}, f32[12,32]{1,0:T(8,128)S(1)}) custom-call(bf16[8,4096]{1,0:T(8,128)(2,1)S(1)} %get-tuple-element.50.c_ref, bf16[8,4096]{1,0:T(8,128)(2,1)S(1)} %probe_sides.1.refs_0_, bf16[8,4096]{1,0:T(8,128)(2,1)S(1)} %collective-permute-done.10.refs_1_, bf16[8,4096]{1,0:T(8,128)(2,1)S(1)} %collective-permute-done.11.refs_2_, ...), custom_call_target="tpu_custom_call" | custom-call | flops 1 | bytes 1 | tf_op jit(solution)/shard_map/score_shares/pallas_call | solution.py:316
  35.1 0.1 collective-permute-start.13
  35.1 0.8 %candidate_features.1 = bf16[4,8192]{1,0:T(4,128)(2,1)} custom-call(f32[64,256]{1,0:T(8,128)S(1)} %get-tuple-element.56.own, f32[64,256]{1,0:T(8,128)S(1)} %collective-permute-done.14.got), custom_call_target="tpu_custom_call" | custom-call | flops 1 | bytes 1 | tf_op jit(solution)/shard_map/candidate_features/pallas_call | solution.py:316
  35.9 0.3 collective-permute-done.13.got
  36.3 0.6 %scores.1 = f32[4,32]{1,0:T(4,128)} custom-call(f32[12,32]{1,0:T(8,128)S(1)} %get-tuple-element.54.own, f32[12,32]{1,0:T(8,128)S(1)} %collective-permute-done.13.got), custom_call_target="tpu_custom_call" | custom-call | flops 1 | bytes 1 | tf_op jit(solution)/shard_map/scores/pallas_call | solution.py:316
  (10 shorter events, 0.1 us)
Async XLA Ops:
  0.6 12.2 %collective-permute-start.2 = (bf16[1024,256]{1,0:T(8,128)(2,1)}, bf16[1024,256]{1,0:T(8,128)(2,1)S(1)}, u32[]{:S(2)}, u32[]{:S(2)}) collective-permute-start(bf16[1024,256]{1,0:T(8,128)(2,1)} %in_hbm.3), channel_id=1, source_target_pairs={{0,8},{1,17},{2,10},{3,19},{4,20},{5,13},{6,22},{7,15},{8,0},{9,25... | collective-permute-start | bytes 1572872 | tf_op jit(solution)/shard_map/ppermute | solution.py:310
  6.4 12.0 %collective-permute-start = (bf16[128,4608]{1,0:T(8,128)(2,1)S(1)}, bf16[128,4608]{1,0:T(8,128)(2,1)S(1)}, u32[]{:S(2)}, u32[]{:S(2)}) collective-permute-start(bf16[128,4608]{1,0:T(8,128)(2,1)S(1)} %get-tuple-element.32), channel_id=1, source_target_pairs={{0,4},{4,0},{8,12},{12,8},{16,20},{20,16},{24,28},{28,24},{1,5},{5... | collective-permute-start | bytes 3538952 | tf_op jit(solution)/shard_map/ppermute | solution.py:293
  6.5 11.9 %collective-permute-start.1 = (bf16[128,4608]{1,0:T(8,128)(2,1)S(1)}, bf16[128,4608]{1,0:T(8,128)(2,1)S(1)}, u32[]{:S(2)}, u32[]{:S(2)}) collective-permute-start(bf16[128,4608]{1,0:T(8,128)(2,1)S(1)} %get-tuple-element.34), channel_id=1, source_target_pairs={{0,4},{4,0},{8,12},{12,8},{16,20},{20,16},{24,28},{28,24},{1,5},{5... | collective-permute-start | bytes 3538952 | tf_op jit(solution)/shard_map/ppermute | solution.py:293
  7.0 5.8 %collective-permute-start.3 = (bf16[208,256]{1,0:T(8,128)(2,1)S(1)}, bf16[208,256]{1,0:T(8,128)(2,1)S(1)}, u32[]{:S(2)}, u32[]{:S(2)}) collective-permute-start(bf16[208,256]{1,0:T(8,128)(2,1)S(1)} %get-tuple-element.35.extra.refs_0_), channel_id=1, source_target_pairs={{0,8},{1,17},{2,10},{3,19},{4,20},{5,13},{6,22},{7,15},{8,0},{9,25... | collective-permute-start | bytes 319496 | tf_op jit(solution)/shard_map/ppermute | solution.py:310
  9.1 7.6 %collective-permute-start.4 = (bf16[720,256]{1,0:T(8,128)(2,1)S(1)}, bf16[720,256]{1,0:T(8,128)(2,1)S(1)}, u32[]{:S(2)}, u32[]{:S(2)}) collective-permute-start(bf16[720,256]{1,0:T(8,128)(2,1)S(1)} %get-tuple-element.38), channel_id=1, source_target_pairs={{0,16},{1,9},{2,18},{3,11},{4,12},{5,21},{6,14},{7,23},{8,24},{9,1... | collective-permute-start | bytes 1105928 | tf_op jit(solution)/shard_map/ppermute | solution.py:310
  12.9 11.6 %collective-permute-start.6 = (bf16[1360,256]{1,0:T(8,128)(2,1)S(1)}, bf16[1360,256]{1,0:T(8,128)(2,1)S(1)}, u32[]{:S(2)}, u32[]{:S(2)}) collective-permute-start(bf16[1360,256]{1,0:T(8,128)(2,1)S(1)} %pad_maximum_fusion), channel_id=1, source_target_pairs={{0,16},{1,9},{2,18},{3,11},{4,12},{5,21},{6,14},{7,23},{8,24},{9,1... | collective-permute-start | bytes 2088968 | tf_op jit(solution)/shard_map/ppermute | solution.py:310
  16.7 1.7 %collective-permute-start.5 = (bf16[720,256]{1,0:T(8,128)(2,1)S(1)}, bf16[720,256]{1,0:T(8,128)(2,1)S(1)}, u32[]{:S(2)}, u32[]{:S(2)}) collective-permute-start(bf16[720,256]{1,0:T(8,128)(2,1)S(1)} %collective-permute-done.4.refs_3_), channel_id=1, source_target_pairs={{0,4},{4,0},{8,12},{12,8},{16,20},{20,16},{24,28},{28,24},{1,5},{5... | collective-permute-start | bytes 1105928 | tf_op jit(solution)/shard_map/ppermute | solution.py:293
  16.7 7.4 %collective-permute-start.7 = (bf16[384,256]{1,0:T(8,128)(2,1)S(1)}, bf16[384,256]{1,0:T(8,128)(2,1)S(1)}, u32[]{:S(2)}, u32[]{:S(2)}) collective-permute-start(bf16[384,256]{1,0:T(8,128)(2,1)S(1)} %slice.4), channel_id=1, source_target_pairs={{0,1},{1,0},{2,3},{3,2},{4,5},{5,4},{6,7},{7,6},{8,9},{9,8},{10,11... | collective-permute-start | bytes 589832 | tf_op jit(solution)/shard_map/ppermute | solution.py:293
  25.2 1.4 %collective-permute-start.9 = (bf16[304,256]{1,0:T(8,128)(2,1)S(1)}, bf16[304,256]{1,0:T(8,128)(2,1)S(1)}, u32[]{:S(2)}, u32[]{:S(2)}) collective-permute-start(bf16[304,256]{1,0:T(8,128)(2,1)S(1)} %get-tuple-element.49), channel_id=1, source_target_pairs={{0,4},{4,0},{8,12},{12,8},{16,20},{20,16},{24,28},{28,24},{1,5},{5... | collective-permute-start | bytes 466952 | tf_op jit(solution)/shard_map/ppermute | solution.py:293
  26.0 5.0 %collective-permute-start.8 = (bf16[304,256]{1,0:T(8,128)(2,1)S(1)}, bf16[304,256]{1,0:T(8,128)(2,1)S(1)}, u32[]{:S(2)}, u32[]{:S(2)}) collective-permute-start(bf16[304,256]{1,0:T(8,128)(2,1)S(1)} %get-tuple-element.45), channel_id=1, source_target_pairs={{0,4},{4,0},{8,12},{12,8},{16,20},{20,16},{24,28},{28,24},{1,5},{5... | collective-permute-start | bytes 466952 | tf_op jit(solution)/shard_map/ppermute | solution.py:293
  26.9 5.9 %collective-permute-start.10 = (bf16[8,4096]{1,0:T(8,128)(2,1)S(1)}, bf16[8,4096]{1,0:T(8,128)(2,1)S(1)}, u32[]{:S(2)}, u32[]{:S(2)}) collective-permute-start(bf16[8,4096]{1,0:T(8,128)(2,1)S(1)} %probe_sides.1.refs_0_), channel_id=1, source_target_pairs={{0,24},{4,28},{8,16},{12,20},{16,8},{20,12},{24,0},{28,4},{1,25},{... | collective-permute-start | bytes 196616 | tf_op jit(solution)/shard_map/ppermute | solution.py:293
  30.4 4.3 %collective-permute-start.11 = (bf16[8,4096]{1,0:T(8,128)(2,1)S(1)}, bf16[8,4096]{1,0:T(8,128)(2,1)S(1)}, u32[]{:S(2)}, u32[]{:S(2)}) collective-permute-start(bf16[8,4096]{1,0:T(8,128)(2,1)S(1)} %probe_sides.1.refs_0_), channel_id=1, source_target_pairs={{0,16},{4,20},{8,24},{12,28},{16,0},{20,4},{24,8},{28,12},{1,17},{... | collective-permute-start | bytes 196616 | tf_op jit(solution)/shard_map/ppermute | solution.py:293
  30.4 4.3 %collective-permute-start.12 = (bf16[8,4096]{1,0:T(8,128)(2,1)S(1)}, bf16[8,4096]{1,0:T(8,128)(2,1)S(1)}, u32[]{:S(2)}, u32[]{:S(2)}) collective-permute-start(bf16[8,4096]{1,0:T(8,128)(2,1)S(1)} %probe_sides.1.refs_0_), channel_id=1, source_target_pairs={{0,8},{4,12},{8,0},{12,4},{16,24},{20,28},{24,16},{28,20},{1,9},{5... | collective-permute-start | bytes 196616 | tf_op jit(solution)/shard_map/ppermute | solution.py:293
  31.3 3.9 %collective-permute-start.14 = (f32[64,256]{1,0:T(8,128)S(1)}, f32[64,256]{1,0:T(8,128)S(1)}, u32[]{:S(2)}, u32[]{:S(2)}) collective-permute-start(f32[64,256]{1,0:T(8,128)S(1)} %get-tuple-element.57), channel_id=1, source_target_pairs={{0,4},{4,0},{8,12},{12,8},{16,20},{20,16},{24,28},{28,24},{1,5},{5... | collective-permute-start | bytes 196616 | tf_op jit(solution)/shard_map/ppermute | solution.py:293
  35.1 1.2 %collective-permute-start.13 = (f32[12,32]{1,0:T(8,128)S(1)}, f32[12,32]{1,0:T(8,128)S(1)}, u32[]{:S(2)}, u32[]{:S(2)}) collective-permute-start(f32[12,32]{1,0:T(8,128)S(1)} %get-tuple-element.55), channel_id=1, source_target_pairs={{0,4},{4,0},{8,12},{12,8},{16,20},{20,16},{24,28},{28,24},{1,5},{5... | collective-permute-start | bytes 4616 | tf_op jit(solution)/shard_map/ppermute | solution.py:293

commit v6 on v5

--- a/solution.py
+++ b/solution.py
@@ -42,14 +42,17 @@
     return me ^ (0, first, 6 - first, 6)[kind]
 
 
+def there_at(kd, ku):
+    return (0, kd, None, 2 * kd), tuple(3 * kd + kind * ku for kind in range(4))
+
+
 def prepare_kernel(
-    n, seq, down_hbm, up_hbm, rank_down_hbm, rank_up_hbm, in_hbm, out_hbm,
+    n, seq, down_hbm, up_hbm, rank_down_hbm, rank_up_hbm, out_hbm,
     c_x_hbm, c_m_hbm, c_len_hbm, p_x_hbm, p_m_hbm, p_len_hbm,
-    extra_ref, tail_ref, x_ref, m_ref, live_ref, c_send, p_send,
+    extra_ref, x_ref, m_ref, live_ref, c_send, p_send,
     down_ref, up_ref, rank_down_ref, rank_up_ref, c_len, p_len, sems,
 ):
     o_rows, half = out_hbm.shape[0], c_x_hbm.shape[0]
-    s_rows, tail = in_hbm.shape[0], tail_ref.shape[0]
     moves = (
         (down_hbm, down_ref),
         (up_hbm, up_ref),
@@ -58,7 +61,6 @@
         (c_len_hbm, c_len),
         (p_len_hbm, p_len),
         (out_hbm, extra_ref.at[pl.ds(0, o_rows)]),
-        (in_hbm.at[pl.ds(s_rows - tail, tail)], tail_ref),
     )
     moves += tuple(
         (source.at[pl.ds(e * seq, seq)], to.at[pl.ds(base + e * seq, seq)])
@@ -87,31 +89,32 @@
         for e in range(half // seq):
             live = live | ((lane >= e * seq) & (lane < e * seq + lengths[e]))
         live_ref[side] = live.astype(jnp.float32).astype(live_ref.dtype)
-    other = 1 - lax.axis_index("fsdp") % 2
+    other, plane = lax.axis_index("fsdp") ^ 1, lax.axis_index("dp")
     examples = half // seq
     kd, ku = x_ref.shape[1] // n, m_ref.shape[1] // n
-    for copy in copies[6:8]:
-        copy.wait()
+    copies[6].wait()
     for side, send_ref in enumerate((c_send, p_send)):
-        for ref, wide, base, turn in ((m_ref, ku, (n // 2) * kd, 0), (x_ref, kd, 0, 1)):
+        for sketch, ref, wide in ((1, m_ref, ku), (0, x_ref, kd)):
             for e in range(examples):
-                copies[8 + (2 * side + turn) * examples + e].wait()
+                copies[7 + (2 * side + 1 - sketch) * examples + e].wait()
                 rows = pl.ds(e * seq, seq)
-                for b in range(n // 2):
-                    first = pl.multiple_of((2 * b + other) * wide, wide)
-                    at = base + b * wide
-                    send_ref[rows, at : at + wide] = ref[pl.ds(side * half + e * seq, seq), pl.ds(first, wide)]
+                for kind, at in enumerate(there_at(kd, ku)[sketch]):
+                    if at is not None:
+                        first = pl.multiple_of(partner(other, kind, plane) * wide, wide)
+                        send_ref[rows, at : at + wide] = ref[pl.ds(side * half + e * seq, seq), pl.ds(first, wide)]
 
 
 def spans(n, x, m, xo, block, sketch, first, count):
     kind, core, whos = block
     j = partner(lax.axis_index("fsdp") ^ core, kind, lax.axis_index("dp"))
-    source, wide, base = ((x, x.shape[1] // n, 0), (m, m.shape[1] // n, (n // 2) * (x.shape[1] // n)))[sketch]
+    kd, ku = x.shape[1] // n, m.shape[1] // n
+    source, wide = ((x, kd), (m, ku))[sketch]
     for who in whos:
         if who == 0:
             yield who, source[:, pl.ds(pl.multiple_of(j * wide + first, 128), count)]
         else:
-            yield who, xo[:, pl.ds(pl.multiple_of(base + (j // 2) * wide + first, 128), count)]
+            at = there_at(kd, ku)[sketch][kind] + first
+            yield who, xo[:, at : at + count]
 
 
 def small_sums(n, ks, places, x, m, xo, refs):
@@ -139,16 +142,16 @@
 
 
 def own_kernel(n, ks, places, tables, in_hbm, extra, x, m, own, second, sums_ref, small_ref, sems):
-    extra_rows = extra.shape[0]
-    part = second.shape[0] - extra_rows
-    first = in_hbm.shape[0] * 3 // 8 // 128 * 128
+    part = first = in_hbm.shape[0] // 2
+    o_rows = m.shape[1] // n
     copies = [
         pltpu.make_async_copy(in_hbm, own, sems.at[0]),
         pltpu.make_async_copy(in_hbm.at[pl.ds(first, part)], second.at[pl.ds(0, part)], sems.at[1]),
     ]
     for copy in copies:
         copy.start()
-    second[part:, :] = extra[...]
+    second[part : second.shape[0] - o_rows, :] = extra[o_rows:, :]
+    second[second.shape[0] - o_rows :, :] = extra[:o_rows, :]
     half = x.shape[0] // 2
     views = [(x.at[pl.ds(side * half, half)], m.at[pl.ds(side * half, half)], None) for side in range(2)]
     for side in range(2):
@@ -327,25 +330,23 @@
     flat = (examples * seq, model)
     flat_m = (examples * seq, value)
     rows = 2 * examples * seq
-    beside, part = s_rows * 3 // 8 // 128 * 128, s_rows // 2
-    tail = s_rows - beside - part
-    extra, last, x, m, live, c_cols, p_cols = kernel(
+    beside = part = s_rows // 2
+    extra, x, m, live, c_cols, p_cols = kernel(
         functools.partial(prepare_kernel, n, seq),
         "prepare",
         (
             array(o_rows + t_rows, kp),
-            array(tail, kp),
             array(rows, model),
             array(rows, value),
             array(2, 16, rows // 2),
-            array(rows // 2, (model + value) // 2),
-            array(rows // 2, (model + value) // 2),
+            array(rows // 2, 3 * s_rows + 4 * o_rows),
+            array(rows // 2, 3 * s_rows + 4 * o_rows),
         ),
         in_hbm(
-            down, up, rank_down.T, rank_up.T, sketch_in, sketch_out,
+            down, up, rank_down.T, rank_up.T, sketch_out,
             c_x.reshape(flat), c_m.reshape(flat_m), c_len, p_x.reshape(flat), p_m.reshape(flat_m), p_len,
         ),
-        in_specs=[HBM] * 12,
+        in_specs=[HBM] * 11,
         scratch=[
             pltpu.VMEM(down.shape, down.dtype),
             pltpu.VMEM(up.shape, up.dtype),
@@ -353,7 +354,7 @@
             pltpu.VMEM(rank_up.shape[::-1], rank_up.dtype),
             pltpu.SMEM(c_len.shape, c_len.dtype),
             pltpu.SMEM(p_len.shape, p_len.dtype),
-            pltpu.SemaphoreType.DMA((8 + 4 * examples,)),
+            pltpu.SemaphoreType.DMA((7 + 4 * examples,)),
         ],
     )
 
@@ -381,19 +382,18 @@
     second = along(second, True)
     c_xo, p_xo = sw(c_cols, 1), sw(p_cols, 1)
 
-    more = along(jnp.concatenate([first, first_extra, last]), True)
+    more = along(jnp.concatenate([first, first_extra]), True)
     rest = swap(first[:beside], 1, "dp", planes)
-    second_other = sw(second, 1)
-
-    t_at = part + o_rows
+    second_other, rest_other = sw(second[: part + t_rows], 1), sw(rest, 1)
+
+    o_at = part + t_rows
     early_places = (
         (0, 0, (0, 0, there), 1, 0, o_rows), (1, 0, (1, 0, both), 0, 0, s_rows), (2, 0, (1, 0, both), 1, 0, o_rows),
-        (3, 0, (2, 0, here), 0, beside, part), (3, part, (2, 0, here), 1, 0, o_rows),
-        (4, 0, (2, 1, here), 0, beside, part), (4, part, (2, 1, here), 1, 0, o_rows),
-        (5, 0, (0, 0, there), 0, 0, s_rows),
+        (3, 0, (2, 0, here), 0, beside, part), (4, 0, (2, 1, here), 0, beside, part),
+        (3, o_at, (2, 0, both), 1, 0, o_rows), (5, 0, (0, 0, there), 0, 0, s_rows),
     )
     early_tables = (
-        (0, o_rows, (0, 0, there)), (2, o_rows, (1, 0, both)), (3, t_at, (2, 0, here)), (4, t_at, (2, 1, here)),
+        (0, o_rows, (0, 0, there)), (2, o_rows, (1, 0, both)), (3, part, (2, 0, here)), (4, part, (2, 1, here)),
     )
     sums, small = kernel(
         functools.partial(early_kernel, n, ks, early_places, early_tables),
@@ -403,8 +403,7 @@
     )
     late_places = (
         (0, 0, (3, 0, both), 0, 0, s_rows), (0, s_rows, (3, 0, both), 1, 0, o_rows),
-        (0, s_rows + o_rows + t_rows, (2, 0, both), 0, beside + part, tail),
-        (1, 0, (2, 0, both), 0, 0, beside),
+        (1, 0, (2, 0, here), 0, 0, beside), (2, 0, (2, 1, here), 0, 0, beside),
     )
 
     def late(side, name):
@@ -412,7 +411,7 @@
             functools.partial(late_kernel, n, ks, side, late_places, ((0, s_rows + o_rows, (3, 0, both)),)),
             name,
             (array(rows, kp, dtype=f32), array(ks, rows, dtype=f32), array(rows + 2 * ks + 16, kp)),
-            (x, m, (c_xo, p_xo)[side], live, sums, small, more, rest),
+            (x, m, (c_xo, p_xo)[side], live, sums, small, more, rest, rest_other),
             scratch=[pltpu.VMEM((2, rows, kp), f32), pltpu.VMEM((2, ks, rows), f32)],
         )
         return keep, keep_small, sw(out, 1)

time: 37 us -> 36.1 us (0.976)
  starting transfers between devices: 14.9 us -> 14.1 us
    ppermute x4, waiting for transfers between devices: 3.84 us -> 2.44 us  [along(): return lax.ppermute(x, ('fsdp', 'dp'), pairs)]
    ppermute x11 -> x12, waiting for transfers between devices: 7.75 us -> 9.06 us  [swap(): return lax.ppermute(x, axis, [(i, i ^ k) for i in range(size)])]
    ppermute x11 -> x12, starting transfers between devices: 7.19 us -> 6.59 us  [swap(): return lax.ppermute(x, axis, [(i, i ^ k) for i in range(size)])]
  transfers between devices with their start and end apart: 15 -> 16, of which waited for: 8 -> 8; matrix products, arithmetic and copies ran while one was open for 0% -> 0% of each run, Pallas kernels for 22% -> 23%
where the time goes in v6:
time: 36.1 us; the launch traced here: 36 us
  starting transfers between devices  14.1 us (39%)
  waiting for transfers between devices  11.5 us (32%)
  Pallas kernels  9.51 us (26%)
  between operations  0.76 us (2%)
    pallas_call x10, Pallas kernels, kernel(): pl.pallas_call(f, out_shape=outs, in_specs=in_specs or [VMEM] * len(opera...  9.51 us
    ppermute x12, waiting for transfers between devices, swap(): return lax.ppermute(x, axis, [(i, i ^ k) for i in range(size)])  9.06 us
    ppermute x4, starting transfers between devices, along(): return lax.ppermute(x, ('fsdp', 'dp'), pairs)  7.52 us
    ppermute x12, starting transfers between devices, swap(): return lax.ppermute(x, axis, [(i, i ^ k) for i in range(size)])  6.59 us
    ppermute x4, waiting for transfers between devices, along(): return lax.ppermute(x, ('fsdp', 'dp'), pairs)  2.44 us
  transfers between devices with their start and end apart: 16, of which 8 were waited for; matrix products, arithmetic and copies ran while one was open for 0% of the time, Pallas kernels for 23%

profile of v6, /device:TPU:0, one launch (start us, length us, event | category | flops | bytes accessed | tf_op | source)
XLA Modules:
  0.0 36.0 jit_solution(16164936223791084617)
XLA Ops:
  0.6 3.0 %collective-permute-start.2 = (bf16[1024,256]{1,0:T(8,128)(2,1)}, bf16[1024,256]{1,0:T(8,128)(2,1)S(1)}, u32[]{:S(2)}, u32[]{:S(2)}) collective-permute-start(bf16[1024,256]{1,0:T(8,128)(2,1)} %in_hbm.1), channel_id=1, source_target_pairs={{0,8},{1,17},{2,10},{3,19},{4,20},{5,13},{6,22},{7,15},{8,0},{9,25... | collective-permute-start | bytes 1572872 | tf_op jit(solution)/shard_map/ppermute | solution.py:313
  3.6 2.7 %prepare.1 = (bf16[208,256]{1,0:T(8,128)(2,1)S(1)}, bf16[256,8192]{1,0:T(8,128)(2,1)S(1)}, bf16[256,1024]{1,0:T(8,128)(2,1)S(1)}, bf16[2,16,128]{2,1,0:T(8,128)(...) custom-call(bf16[1024,128]{1,0:T(8,128)(2,1)} %down_hbm.1, bf16[128,128]{1,0:T(8,128)(2,1)} %up_hbm.1, ...), custom_call_target="tpu_custom_call" | custom-call | flops 1 | bytes 1 | tf_op jit(solution)/shard_map/prepare/pallas_call | solution.py:319
  6.4 0.1 collective-permute-start.3
  6.5 0.5 %collective-permute-start.1 = (bf16[128,3584]{1,0:T(8,128)(2,1)S(1)}, bf16[128,3584]{1,0:T(8,128)(2,1)S(1)}, u32[]{:S(2)}, u32[]{:S(2)}) collective-permute-start(bf16[128,3584]{1,0:T(8,128)(2,1)S(1)} %get-tuple-element.33), channel_id=1, source_target_pairs={{0,4},{4,0},{8,12},{12,8},{16,20},{20,16},{24,28},{28,24},{1,5},{5... | collective-permute-start | bytes 2752520 | tf_op jit(solution)/shard_map/ppermute | solution.py:296
  7.0 1.5 %own_products.1 = (bf16[1024,256]{1,0:T(8,128)(2,1)S(1)}, bf16[720,256]{1,0:T(8,128)(2,1)S(1)}, f32[2,2,128,256]{3,2,1,0:T(8,128)S(1)}, f32[2,2,128,16]{3,2,1,0:T(8,128)S(1)}) custom-call(bf16[1024,256]{1,0:T(8,128)(2,1)} %in_hbm.1, bf16[208,256]{1,0:T(8,128)(2,1)S(1)} %get-tuple-element.34.extra.refs_0_, bf16[256,8192]{1,0:T(8,128)(2,1)S(1)} %get-tuple-element.29.x, ...), custom_call_target="tpu_custom_call" | custom-call | flops 1 | bytes 1 | tf_op jit(solution)/shard_map/own_products/pallas_call | solution.py:319
  8.5 2.0 %collective-permute-start.4 = (bf16[720,256]{1,0:T(8,128)(2,1)S(1)}, bf16[720,256]{1,0:T(8,128)(2,1)S(1)}, u32[]{:S(2)}, u32[]{:S(2)}) collective-permute-start(bf16[720,256]{1,0:T(8,128)(2,1)S(1)} %get-tuple-element.37), channel_id=1, source_target_pairs={{0,16},{1,9},{2,18},{3,11},{4,12},{5,21},{6,14},{7,23},{8,24},{9,1... | collective-permute-start | bytes 1105928 | tf_op jit(solution)/shard_map/ppermute | solution.py:313
  10.5 2.3 %collective-permute-done.3.refs_2_ = bf16[208,256]{1,0:T(8,128)(2,1)S(1)} collective-permute-done((bf16[208,256]{1,0:T(8,128)(2,1)S(1)}, bf16[208,256]{1,0:T(8,128)(2,1)S(1)}, u32[]{:S(2)}, u32[]{:S(2)}) %collective-permute-start.3) | collective-permute-done | bytes 106528 | tf_op jit(solution)/shard_map/ppermute | solution.py:313
  12.9 2.4 %collective-permute-start.6 = (bf16[1232,256]{1,0:T(8,128)(2,1)S(1)}, bf16[1232,256]{1,0:T(8,128)(2,1)S(1)}, u32[]{:S(2)}, u32[]{:S(2)}) collective-permute-start(bf16[1232,256]{1,0:T(8,128)(2,1)S(1)} %pad_maximum_fusion), channel_id=1, source_target_pairs={{0,16},{1,9},{2,18},{3,11},{4,12},{5,21},{6,14},{7,23},{8,24},{9,1... | collective-permute-start | bytes 1892360 | tf_op jit(solution)/shard_map/ppermute | solution.py:313
  15.3 1.6 %collective-permute-start.7 = (bf16[512,256]{1,0:T(8,128)(2,1)S(1)}, bf16[512,256]{1,0:T(8,128)(2,1)S(1)}, u32[]{:S(2)}, u32[]{:S(2)}) collective-permute-start(bf16[512,256]{1,0:T(8,128)(2,1)S(1)} %slice.9), channel_id=1, source_target_pairs={{0,1},{1,0},{2,3},{3,2},{4,5},{5,4},{6,7},{7,6},{8,9},{9,8},{10,11... | collective-permute-start | bytes 786440 | tf_op jit(solution)/shard_map/ppermute | solution.py:296
  17.0 0.1 collective-permute-start.5
  17.0 4.7 %collective-permute-done.7.refs_1_ = bf16[512,256]{1,0:T(8,128)(2,1)S(1)} collective-permute-done((bf16[512,256]{1,0:T(8,128)(2,1)S(1)}, bf16[512,256]{1,0:T(8,128)(2,1)S(1)}, u32[]{:S(2)}, u32[]{:S(2)}) %collective-permute-start.7) | collective-permute-done | bytes 262176 | tf_op jit(solution)/shard_map/ppermute | solution.py:296
  21.8 1.7 %early_products.1 = (f32[2,2,2,128,256]{4,3,2,1,0:T(8,128)S(1)}, f32[2,2,2,128,16]{4,3,2,1,0:T(8,128)S(1)}) custom-call(bf16[256,8192]{1,0:T(8,128)(2,1)S(1)} %get-tuple-element.29.x, bf16[256,1024]{1,0:T(8,128)(2,1)S(1)} %get-tuple-element.30.m, bf16[128,3584]{1,0:T(8,128)(2,1)S(1)} %collective-permute-done.c_xo.xo, ...), custom_call_target="tpu_custom_call" | custom-call | flops 1 | bytes 1 | tf_op jit(solution)/shard_map/early_products/pallas_call | solution.py:319
  23.5 0.1 collective-permute-done.6.refs_0_
  23.6 0.7 %probe_products.1 = (f32[256,256]{1,0:T(8,128)S(1)}, f32[16,256]{1,0:T(8,128)S(1)}, bf16[304,256]{1,0:T(8,128)(2,1)S(1)}) custom-call(bf16[256,8192]{1,0:T(8,128)(2,1)S(1)} %get-tuple-element.29.x, bf16[256,1024]{1,0:T(8,128)(2,1)S(1)} %get-tuple-element.30.m, bf16[128,3584]{1,0:T(8,128)(2,1)S(1)} %collective-permute-done.1.p_xo.xo, ...), custom_call_target="tpu_custom_call" | custom-call | flops 1 | bytes 1 | tf_op jit(solution)/shard_map/probe_products/pallas_call | solution.py:319
  24.3 0.4 %collective-permute-start.10 = (bf16[304,256]{1,0:T(8,128)(2,1)S(1)}, bf16[304,256]{1,0:T(8,128)(2,1)S(1)}, u32[]{:S(2)}, u32[]{:S(2)}) collective-permute-start(bf16[304,256]{1,0:T(8,128)(2,1)S(1)} %get-tuple-element.47), channel_id=1, source_target_pairs={{0,4},{4,0},{8,12},{12,8},{16,20},{20,16},{24,28},{28,24},{1,5},{5... | collective-permute-start | bytes 466952 | tf_op jit(solution)/shard_map/ppermute | solution.py:296
  24.7 0.7 %candidate_products.1 = (f32[256,256]{1,0:T(8,128)S(1)}, f32[16,256]{1,0:T(8,128)S(1)}, bf16[304,256]{1,0:T(8,128)(2,1)S(1)}) custom-call(bf16[256,8192]{1,0:T(8,128)(2,1)S(1)} %get-tuple-element.29.x, bf16[256,1024]{1,0:T(8,128)(2,1)S(1)} %get-tuple-element.30.m, bf16[128,3584]{1,0:T(8,128)(2,1)S(1)} %collective-permute-done.c_xo.xo, ...), custom_call_target="tpu_custom_call" | custom-call | flops 1 | bytes 1 | tf_op jit(solution)/shard_map/candidate_products/pallas_call | solution.py:319
  25.4 0.1 collective-permute-start.9
  25.6 0.2 collective-permute-done.10.got
  25.8 0.2 probe_sides.1.refs_0_
  26.0 3.0 %collective-permute-start.11 = (bf16[8,4096]{1,0:T(8,128)(2,1)S(1)}, bf16[8,4096]{1,0:T(8,128)(2,1)S(1)}, u32[]{:S(2)}, u32[]{:S(2)}) collective-permute-start(bf16[8,4096]{1,0:T(8,128)(2,1)S(1)} %probe_sides.1.refs_0_), channel_id=1, source_target_pairs={{0,24},{4,28},{8,16},{12,20},{16,8},{20,12},{24,0},{28,4},{1,25},{... | collective-permute-start | bytes 196616 | tf_op jit(solution)/shard_map/ppermute | solution.py:296
  29.0 0.5 %collective-permute-start.12 = (bf16[8,4096]{1,0:T(8,128)(2,1)S(1)}, bf16[8,4096]{1,0:T(8,128)(2,1)S(1)}, u32[]{:S(2)}, u32[]{:S(2)}) collective-permute-start(bf16[8,4096]{1,0:T(8,128)(2,1)S(1)} %probe_sides.1.refs_0_), channel_id=1, source_target_pairs={{0,16},{4,20},{8,24},{12,28},{16,0},{20,4},{24,8},{28,12},{1,17},{... | collective-permute-start | bytes 196616 | tf_op jit(solution)/shard_map/ppermute | solution.py:296
  29.5 0.1 collective-permute-start.13
  29.6 0.2 candidate_sides.1
  29.8 0.1 collective-permute-start.15
  29.9 1.4 %collective-permute-done.11.refs_1_ = bf16[8,4096]{1,0:T(8,128)(2,1)S(1)} collective-permute-done((bf16[8,4096]{1,0:T(8,128)(2,1)S(1)}, bf16[8,4096]{1,0:T(8,128)(2,1)S(1)}, u32[]{:S(2)}, u32[]{:S(2)}) %collective-permute-start.11) | collective-permute-done | bytes 65568 | tf_op jit(solution)/shard_map/ppermute | solution.py:296
  31.4 1.9 %collective-permute-done.12.refs_2_ = bf16[8,4096]{1,0:T(8,128)(2,1)S(1)} collective-permute-done((bf16[8,4096]{1,0:T(8,128)(2,1)S(1)}, bf16[8,4096]{1,0:T(8,128)(2,1)S(1)}, u32[]{:S(2)}, u32[]{:S(2)}) %collective-permute-start.12) | collective-permute-done | bytes 65568 | tf_op jit(solution)/shard_map/ppermute | solution.py:296
  33.2 0.5 %collective-permute-done.13.refs_3_ = bf16[8,4096]{1,0:T(8,128)(2,1)S(1)} collective-permute-done((bf16[8,4096]{1,0:T(8,128)(2,1)S(1)}, bf16[8,4096]{1,0:T(8,128)(2,1)S(1)}, u32[]{:S(2)}, u32[]{:S(2)}) %collective-permute-start.13) | collective-permute-done | bytes 65568 | tf_op jit(solution)/shard_map/ppermute | solution.py:296
  33.7 0.4 %score_shares.1 = (f32[12,32]{1,0:T(8,128)S(1)}, f32[12,32]{1,0:T(8,128)S(1)}) custom-call(bf16[8,4096]{1,0:T(8,128)(2,1)S(1)} %get-tuple-element.48.c_ref, bf16[8,4096]{1,0:T(8,128)(2,1)S(1)} %probe_sides.1.refs_0_, bf16[8,4096]{1,0:T(8,128)(2,1)S(1)} %collective-permute-done.11.refs_1_, bf16[8,4096]{1,0:T(8,128)(2,1)S(1)} %collective-permute-done.12.refs_2_, ...), custom_call_target="tpu_custom_call" | custom-call | flops 1 | bytes 1 | tf_op jit(solution)/shard_map/score_shares/pallas_call | solution.py:319
  34.1 0.1 collective-permute-start.14
  34.2 0.8 %candidate_features.1 = bf16[4,8192]{1,0:T(4,128)(2,1)} custom-call(f32[64,256]{1,0:T(8,128)S(1)} %get-tuple-element.54.own, f32[64,256]{1,0:T(8,128)S(1)} %collective-permute-done.15.got), custom_call_target="tpu_custom_call" | custom-call | flops 1 | bytes 1 | tf_op jit(solution)/shard_map/candidate_features/pallas_call | solution.py:319
  35.0 0.3 collective-permute-done.14.got
  35.4 0.6 %scores.1 = f32[4,32]{1,0:T(4,128)} custom-call(f32[12,32]{1,0:T(8,128)S(1)} %get-tuple-element.52.own, f32[12,32]{1,0:T(8,128)S(1)} %collective-permute-done.14.got), custom_call_target="tpu_custom_call" | custom-call | flops 1 | bytes 1 | tf_op jit(solution)/shard_map/scores/pallas_call | solution.py:319
  (13 shorter events, 0.2 us)
Async XLA Ops:
  0.6 12.2 %collective-permute-start.2 = (bf16[1024,256]{1,0:T(8,128)(2,1)}, bf16[1024,256]{1,0:T(8,128)(2,1)S(1)}, u32[]{:S(2)}, u32[]{:S(2)}) collective-permute-start(bf16[1024,256]{1,0:T(8,128)(2,1)} %in_hbm.1), channel_id=1, source_target_pairs={{0,8},{1,17},{2,10},{3,19},{4,20},{5,13},{6,22},{7,15},{8,0},{9,25... | collective-permute-start | bytes 1572872 | tf_op jit(solution)/shard_map/ppermute | solution.py:313
  6.4 6.5 %collective-permute-start.3 = (bf16[208,256]{1,0:T(8,128)(2,1)S(1)}, bf16[208,256]{1,0:T(8,128)(2,1)S(1)}, u32[]{:S(2)}, u32[]{:S(2)}) collective-permute-start(bf16[208,256]{1,0:T(8,128)(2,1)S(1)} %get-tuple-element.34.extra.refs_0_), channel_id=1, source_target_pairs={{0,8},{1,17},{2,10},{3,19},{4,20},{5,13},{6,22},{7,15},{8,0},{9,25... | collective-permute-start | bytes 319496 | tf_op jit(solution)/shard_map/ppermute | solution.py:313
  6.5 15.3 %collective-permute-start = (bf16[128,3584]{1,0:T(8,128)(2,1)S(1)}, bf16[128,3584]{1,0:T(8,128)(2,1)S(1)}, u32[]{:S(2)}, u32[]{:S(2)}) collective-permute-start(bf16[128,3584]{1,0:T(8,128)(2,1)S(1)} %get-tuple-element.31), channel_id=1, source_target_pairs={{0,4},{4,0},{8,12},{12,8},{16,20},{20,16},{24,28},{28,24},{1,5},{5... | collective-permute-start | bytes 2752520 | tf_op jit(solution)/shard_map/ppermute | solution.py:296
  6.5 15.3 %collective-permute-start.1 = (bf16[128,3584]{1,0:T(8,128)(2,1)S(1)}, bf16[128,3584]{1,0:T(8,128)(2,1)S(1)}, u32[]{:S(2)}, u32[]{:S(2)}) collective-permute-start(bf16[128,3584]{1,0:T(8,128)(2,1)S(1)} %get-tuple-element.33), channel_id=1, source_target_pairs={{0,4},{4,0},{8,12},{12,8},{16,20},{20,16},{24,28},{28,24},{1,5},{5... | collective-permute-start | bytes 2752520 | tf_op jit(solution)/shard_map/ppermute | solution.py:296
  8.5 8.4 %collective-permute-start.4 = (bf16[720,256]{1,0:T(8,128)(2,1)S(1)}, bf16[720,256]{1,0:T(8,128)(2,1)S(1)}, u32[]{:S(2)}, u32[]{:S(2)}) collective-permute-start(bf16[720,256]{1,0:T(8,128)(2,1)S(1)} %get-tuple-element.37), channel_id=1, source_target_pairs={{0,16},{1,9},{2,18},{3,11},{4,12},{5,21},{6,14},{7,23},{8,24},{9,1... | collective-permute-start | bytes 1105928 | tf_op jit(solution)/shard_map/ppermute | solution.py:313
  12.9 10.7 %collective-permute-start.6 = (bf16[1232,256]{1,0:T(8,128)(2,1)S(1)}, bf16[1232,256]{1,0:T(8,128)(2,1)S(1)}, u32[]{:S(2)}, u32[]{:S(2)}) collective-permute-start(bf16[1232,256]{1,0:T(8,128)(2,1)S(1)} %pad_maximum_fusion), channel_id=1, source_target_pairs={{0,16},{1,9},{2,18},{3,11},{4,12},{5,21},{6,14},{7,23},{8,24},{9,1... | collective-permute-start | bytes 1892360 | tf_op jit(solution)/shard_map/ppermute | solution.py:313
  15.3 6.4 %collective-permute-start.7 = (bf16[512,256]{1,0:T(8,128)(2,1)S(1)}, bf16[512,256]{1,0:T(8,128)(2,1)S(1)}, u32[]{:S(2)}, u32[]{:S(2)}) collective-permute-start(bf16[512,256]{1,0:T(8,128)(2,1)S(1)} %slice.9), channel_id=1, source_target_pairs={{0,1},{1,0},{2,3},{3,2},{4,5},{5,4},{6,7},{7,6},{8,9},{9,8},{10,11... | collective-permute-start | bytes 786440 | tf_op jit(solution)/shard_map/ppermute | solution.py:296
  17.0 4.8 %collective-permute-start.5 = (bf16[592,256]{1,0:T(8,128)(2,1)S(1)}, bf16[592,256]{1,0:T(8,128)(2,1)S(1)}, u32[]{:S(2)}, u32[]{:S(2)}) collective-permute-start(bf16[592,256]{1,0:T(8,128)(2,1)S(1)} %slice.8), channel_id=1, source_target_pairs={{0,4},{4,0},{8,12},{12,8},{16,20},{20,16},{24,28},{28,24},{1,5},{5... | collective-permute-start | bytes 909320 | tf_op jit(solution)/shard_map/ppermute | solution.py:296
  21.8 1.7 %collective-permute-start.8 = (bf16[512,256]{1,0:T(8,128)(2,1)S(1)}, bf16[512,256]{1,0:T(8,128)(2,1)S(1)}, u32[]{:S(2)}, u32[]{:S(2)}) collective-permute-start(bf16[512,256]{1,0:T(8,128)(2,1)S(1)} %collective-permute-done.7.refs_1_), channel_id=1, source_target_pairs={{0,4},{4,0},{8,12},{12,8},{16,20},{20,16},{24,28},{28,24},{1,5},{5... | collective-permute-start | bytes 786440 | tf_op jit(solution)/shard_map/ppermute | solution.py:296
  24.3 1.5 %collective-permute-start.10 = (bf16[304,256]{1,0:T(8,128)(2,1)S(1)}, bf16[304,256]{1,0:T(8,128)(2,1)S(1)}, u32[]{:S(2)}, u32[]{:S(2)}) collective-permute-start(bf16[304,256]{1,0:T(8,128)(2,1)S(1)} %get-tuple-element.47), channel_id=1, source_target_pairs={{0,4},{4,0},{8,12},{12,8},{16,20},{20,16},{24,28},{28,24},{1,5},{5... | collective-permute-start | bytes 466952 | tf_op jit(solution)/shard_map/ppermute | solution.py:296
  25.4 4.2 %collective-permute-start.9 = (bf16[304,256]{1,0:T(8,128)(2,1)S(1)}, bf16[304,256]{1,0:T(8,128)(2,1)S(1)}, u32[]{:S(2)}, u32[]{:S(2)}) collective-permute-start(bf16[304,256]{1,0:T(8,128)(2,1)S(1)} %get-tuple-element.43), channel_id=1, source_target_pairs={{0,4},{4,0},{8,12},{12,8},{16,20},{20,16},{24,28},{28,24},{1,5},{5... | collective-permute-start | bytes 466952 | tf_op jit(solution)/shard_map/ppermute | solution.py:296
  26.0 5.4 %collective-permute-start.11 = (bf16[8,4096]{1,0:T(8,128)(2,1)S(1)}, bf16[8,4096]{1,0:T(8,128)(2,1)S(1)}, u32[]{:S(2)}, u32[]{:S(2)}) collective-permute-start(bf16[8,4096]{1,0:T(8,128)(2,1)S(1)} %probe_sides.1.refs_0_), channel_id=1, source_target_pairs={{0,24},{4,28},{8,16},{12,20},{16,8},{20,12},{24,0},{28,4},{1,25},{... | collective-permute-start | bytes 196616 | tf_op jit(solution)/shard_map/ppermute | solution.py:296
  29.0 4.3 %collective-permute-start.12 = (bf16[8,4096]{1,0:T(8,128)(2,1)S(1)}, bf16[8,4096]{1,0:T(8,128)(2,1)S(1)}, u32[]{:S(2)}, u32[]{:S(2)}) collective-permute-start(bf16[8,4096]{1,0:T(8,128)(2,1)S(1)} %probe_sides.1.refs_0_), channel_id=1, source_target_pairs={{0,16},{4,20},{8,24},{12,28},{16,0},{20,4},{24,8},{28,12},{1,17},{... | collective-permute-start | bytes 196616 | tf_op jit(solution)/shard_map/ppermute | solution.py:296
  29.5 4.3 %collective-permute-start.13 = (bf16[8,4096]{1,0:T(8,128)(2,1)S(1)}, bf16[8,4096]{1,0:T(8,128)(2,1)S(1)}, u32[]{:S(2)}, u32[]{:S(2)}) collective-permute-start(bf16[8,4096]{1,0:T(8,128)(2,1)S(1)} %probe_sides.1.refs_0_), channel_id=1, source_target_pairs={{0,8},{4,12},{8,0},{12,4},{16,24},{20,28},{24,16},{28,20},{1,9},{5... | collective-permute-start | bytes 196616 | tf_op jit(solution)/shard_map/ppermute | solution.py:296
  29.8 4.4 %collective-permute-start.15 = (f32[64,256]{1,0:T(8,128)S(1)}, f32[64,256]{1,0:T(8,128)S(1)}, u32[]{:S(2)}, u32[]{:S(2)}) collective-permute-start(f32[64,256]{1,0:T(8,128)S(1)} %get-tuple-element.55), channel_id=1, source_target_pairs={{0,4},{4,0},{8,12},{12,8},{16,20},{20,16},{24,28},{28,24},{1,5},{5... | collective-permute-start | bytes 196616 | tf_op jit(solution)/shard_map/ppermute | solution.py:296
  34.1 1.2 %collective-permute-start.14 = (f32[12,32]{1,0:T(8,128)S(1)}, f32[12,32]{1,0:T(8,128)S(1)}, u32[]{:S(2)}, u32[]{:S(2)}) collective-permute-start(f32[12,32]{1,0:T(8,128)S(1)} %get-tuple-element.53), channel_id=1, source_target_pairs={{0,4},{4,0},{8,12},{12,8},{16,20},{20,16},{24,28},{28,24},{1,5},{5... | collective-permute-start | bytes 4616 | tf_op jit(solution)/shard_map/ppermute | solution.py:296

commit v7 on v6

--- a/solution.py
+++ b/solution.py
@@ -144,26 +144,24 @@
 def own_kernel(n, ks, places, tables, in_hbm, extra, x, m, own, second, sums_ref, small_ref, sems):
     part = first = in_hbm.shape[0] // 2
     o_rows = m.shape[1] // n
-    copies = [
-        pltpu.make_async_copy(in_hbm, own, sems.at[0]),
-        pltpu.make_async_copy(in_hbm.at[pl.ds(first, part)], second.at[pl.ds(0, part)], sems.at[1]),
-    ]
-    for copy in copies:
-        copy.start()
-    second[part : second.shape[0] - o_rows, :] = extra[o_rows:, :]
-    second[second.shape[0] - o_rows :, :] = extra[:o_rows, :]
+    load = pltpu.make_async_copy(in_hbm, own, sems.at[0])
+    load.start()
     half = x.shape[0] // 2
     views = [(x.at[pl.ds(side * half, half)], m.at[pl.ds(side * half, half)], None) for side in range(2)]
     for side in range(2):
         small = small_sums(n, ks, tables, *views[side], (extra,))
         for t in range(2):
             small_ref[side, t] = small[0][t]
-    for copy in copies:
-        copy.wait()
+    load.wait()
     for side in range(2):
         sums = products(n, places, *views[side], (extra, own))
         for t in range(2):
             sums_ref[side, t] = sums[0][t]
+    fill = pltpu.make_async_copy(in_hbm.at[pl.ds(first, part)], second.at[pl.ds(0, part)], sems.at[1])
+    fill.start()
+    second[part : second.shape[0] - o_rows, :] = extra[o_rows:, :]
+    second[second.shape[0] - o_rows :, :] = extra[:o_rows, :]
+    fill.wait()
 
 
 def early_kernel(n, ks, places, tables, x, m, c_xo, p_xo, own_sums, own_small, *refs):
@@ -225,7 +223,7 @@
 def flatten(grads, ks, out, scratch, base=0):
     cols, lanes = grads.shape[1], scratch.shape[2]
     for b in range(cols // lanes):
-        scratch[b] = grads[:, b * lanes : (b + 1) * lanes]
+        scratch[b, : grads.shape[0], :] = grads[:, b * lanes : (b + 1) * lanes]
     for k in range(ks):
         for b in range(cols // lanes):
             at = base + k * cols + b * lanes
@@ -259,7 +257,7 @@
 
 def score_kernel(kinds, c_ref, *refs):
     probes, (own_ref, send_ref) = refs[:-2], refs[-2:]
-    me = lax.axis_index("fsdp")
+    me, plane = lax.axis_index("fsdp"), lax.axis_index("dp")
     cands = c_ref[...]
     per = cands.shape[0] // 2
     held = jnp.concatenate([ref[...] for ref in probes], axis=0)
@@ -277,7 +275,7 @@
     placed = jnp.zeros(rows.shape, jnp.float32)
     for g in range(width // per):
         block = jnp.concatenate([rows[:, g * per : (g + 1) * per]] * (width // per), axis=1)
-        placed = jnp.where(group == (me ^ kinds[g // 2] ^ (g % 2)), block, placed)
+        placed = jnp.where(group == (partner(me, kinds[g // 2], plane) ^ (g % 2)), block, placed)
     squares = jnp.broadcast_to(diagonal(dot_last(cands, cands), 1), (2 * per, width))
     for i, ref in enumerate((own_ref, send_ref)):
         ref[:per, :] = placed[i * per : (i + 1) * per]
@@ -420,7 +418,7 @@
     side = array(2 * examples, ks * kp)
 
     def scratch(count):
-        return [pltpu.VMEM((kp // 128, count, 128), f32)]
+        return [pltpu.VMEM((kp // 128, count + ks, 128), f32)]
 
     p_side = kernel(
         functools.partial(probe_kernel, seq), "probe_sides", side, (*late(1, "probe_products"), live), scratch=scratch(total)
@@ -441,8 +439,8 @@
         scratch=scratch(total // 2),
     )
 
-    kinds = (0, 6, 4, 2)
-    got = [sw(p_side, k) for k in kinds[1:]]
+    kinds = (0, 3, 2, 1)
+    got = [sw(p_side, 6), along(p_side, True), along(p_side, False)]
     c_side, *got = lax.optimization_barrier((c_side, *got))
     part = array(3 * examples, n * examples, dtype=f32)
     scores, to_other = kernel(
@@ -503,7 +501,10 @@
     in_specs = (cube, cube, line, cube, cube, line, shard, shard, shard, shard, P(), P())
 
     def body(*args):
-        if n == 1 << 3 and planes % 2 == 0:
+        sketch_in, sketch_out = args[8:10]
+        s_rows, (o_rows, kp) = sketch_in.shape[0], sketch_out.shape
+        whole = s_rows % 256 == 0 and s_rows % kp == 0 and o_rows % 128 == 0 and o_rows <= kp and kp % 128 == 0
+        if n == 1 << 3 and planes % 2 == 0 and whole:
             return fast_body(n, planes, *args)
         return plain_body(*args)
 

time: 36.1 us -> 36.1 us (level)
  waiting for transfers between devices: 11.5 us -> 10.7 us
  Pallas kernels: 9.51 us -> 10.2 us
    ppermute x12 -> x10, waiting for transfers between devices: 9.06 us -> 6.29 us  [swap(): return lax.ppermute(x, axis, [(i, i ^ k) for i in range(size)])]
    ppermute x4 -> x6, waiting for transfers between devices: 2.44 us -> 4.44 us  [along(): return lax.ppermute(x, ('fsdp', 'dp'), pairs)]
    pallas_call x10, Pallas kernels: 9.51 us -> 10.2 us  [kernel(): pl.pallas_call(f, out_shape=outs, in_specs=in_specs or [VMEM] * len(opera...]
    ppermute x12 -> x10, starting transfers between devices: 6.59 us -> 5.92 us  [swap(): return lax.ppermute(x, axis, [(i, i ^ k) for i in range(size)])]
    ppermute x4 -> x6, starting transfers between devices: 7.52 us -> 8.14 us  [along(): return lax.ppermute(x, ('fsdp', 'dp'), pairs)]
  transfers between devices with their start and end apart: 16 -> 16, of which waited for: 8 -> 9; matrix products, arithmetic and copies ran while one was open for 0% -> 0% of each run, Pallas kernels for 23% -> 25%
where the time goes in v7:
time: 36.1 us; the launch traced here: 35.9 us
  starting transfers between devices  14.1 us (39%)
  waiting for transfers between devices  10.7 us (30%)
  Pallas kernels  10.2 us (28%)
  between operations  0.77 us (2%)
    pallas_call x10, Pallas kernels, kernel(): pl.pallas_call(f, out_shape=outs, in_specs=in_specs or [VMEM] * len(opera...  10.2 us
    ppermute x6, starting transfers between devices, along(): return lax.ppermute(x, ('fsdp', 'dp'), pairs)  8.14 us
    ppermute x10, waiting for transfers between devices, swap(): return lax.ppermute(x, axis, [(i, i ^ k) for i in range(size)])  6.29 us
    ppermute x10, starting transfers between devices, swap(): return lax.ppermute(x, axis, [(i, i ^ k) for i in range(size)])  5.92 us
    ppermute x6, waiting for transfers between devices, along(): return lax.ppermute(x, ('fsdp', 'dp'), pairs)  4.44 us
  transfers between devices with their start and end apart: 16, of which 9 were waited for; matrix products, arithmetic and copies ran while one was open for 0% of the time, Pallas kernels for 25%

profile of v7, /device:TPU:0, one launch (start us, length us, event | category | flops | bytes accessed | tf_op | source)
XLA Modules:
  0.0 35.9 jit_solution(11449710500921792669)
XLA Ops:
  0.6 3.0 %collective-permute-start.2 = (bf16[1024,256]{1,0:T(8,128)(2,1)}, bf16[1024,256]{1,0:T(8,128)(2,1)S(1)}, u32[]{:S(2)}, u32[]{:S(2)}) collective-permute-start(bf16[1024,256]{1,0:T(8,128)(2,1)} %in_hbm.1), channel_id=1, source_target_pairs={{0,8},{1,17},{2,10},{3,19},{4,20},{5,13},{6,22},{7,15},{8,0},{9,25... | collective-permute-start | bytes 1572872 | tf_op jit(solution)/shard_map/ppermute | solution.py:311
  3.6 2.7 %prepare.1 = (bf16[208,256]{1,0:T(8,128)(2,1)S(1)}, bf16[256,8192]{1,0:T(8,128)(2,1)S(1)}, bf16[256,1024]{1,0:T(8,128)(2,1)S(1)}, bf16[2,16,128]{2,1,0:T(8,128)(...) custom-call(bf16[1024,128]{1,0:T(8,128)(2,1)} %down_hbm.1, bf16[128,128]{1,0:T(8,128)(2,1)} %up_hbm.1, ...), custom_call_target="tpu_custom_call" | custom-call | flops 1 | bytes 1 | tf_op jit(solution)/shard_map/prepare/pallas_call | solution.py:317
  6.4 0.1 collective-permute-start.3
  6.5 0.5 %collective-permute-start.1 = (bf16[128,3584]{1,0:T(8,128)(2,1)S(1)}, bf16[128,3584]{1,0:T(8,128)(2,1)S(1)}, u32[]{:S(2)}, u32[]{:S(2)}) collective-permute-start(bf16[128,3584]{1,0:T(8,128)(2,1)S(1)} %get-tuple-element.33), channel_id=1, source_target_pairs={{0,4},{4,0},{8,12},{12,8},{16,20},{20,16},{24,28},{28,24},{1,5},{5... | collective-permute-start | bytes 2752520 | tf_op jit(solution)/shard_map/ppermute | solution.py:294
  7.0 2.2 %own_products.1 = (bf16[1024,256]{1,0:T(8,128)(2,1)S(1)}, bf16[720,256]{1,0:T(8,128)(2,1)S(1)}, f32[2,2,128,256]{3,2,1,0:T(8,128)S(1)}, f32[2,2,128,16]{3,2,1,0:T(8,128)S(1)}) custom-call(bf16[1024,256]{1,0:T(8,128)(2,1)} %in_hbm.1, bf16[208,256]{1,0:T(8,128)(2,1)S(1)} %get-tuple-element.34.extra.refs_0_, bf16[256,8192]{1,0:T(8,128)(2,1)S(1)} %get-tuple-element.29.x, ...), custom_call_target="tpu_custom_call" | custom-call | flops 1 | bytes 1 | tf_op jit(solution)/shard_map/own_products/pallas_call | solution.py:317
  9.2 2.0 %collective-permute-start.4 = (bf16[720,256]{1,0:T(8,128)(2,1)S(1)}, bf16[720,256]{1,0:T(8,128)(2,1)S(1)}, u32[]{:S(2)}, u32[]{:S(2)}) collective-permute-start(bf16[720,256]{1,0:T(8,128)(2,1)S(1)} %get-tuple-element.37), channel_id=1, source_target_pairs={{0,16},{1,9},{2,18},{3,11},{4,12},{5,21},{6,14},{7,23},{8,24},{9,1... | collective-permute-start | bytes 1105928 | tf_op jit(solution)/shard_map/ppermute | solution.py:311
  11.3 0.9 %collective-permute-done.3.refs_2_ = bf16[208,256]{1,0:T(8,128)(2,1)S(1)} collective-permute-done((bf16[208,256]{1,0:T(8,128)(2,1)S(1)}, bf16[208,256]{1,0:T(8,128)(2,1)S(1)}, u32[]{:S(2)}, u32[]{:S(2)}) %collective-permute-start.3) | collective-permute-done | bytes 106528 | tf_op jit(solution)/shard_map/ppermute | solution.py:311
  12.2 2.4 %collective-permute-start.6 = (bf16[1232,256]{1,0:T(8,128)(2,1)S(1)}, bf16[1232,256]{1,0:T(8,128)(2,1)S(1)}, u32[]{:S(2)}, u32[]{:S(2)}) collective-permute-start(bf16[1232,256]{1,0:T(8,128)(2,1)S(1)} %pad_maximum_fusion), channel_id=1, source_target_pairs={{0,16},{1,9},{2,18},{3,11},{4,12},{5,21},{6,14},{7,23},{8,24},{9,1... | collective-permute-start | bytes 1892360 | tf_op jit(solution)/shard_map/ppermute | solution.py:311
  14.6 1.6 %collective-permute-start.7 = (bf16[512,256]{1,0:T(8,128)(2,1)S(1)}, bf16[512,256]{1,0:T(8,128)(2,1)S(1)}, u32[]{:S(2)}, u32[]{:S(2)}) collective-permute-start(bf16[512,256]{1,0:T(8,128)(2,1)S(1)} %slice.9), channel_id=1, source_target_pairs={{0,1},{1,0},{2,3},{3,2},{4,5},{5,4},{6,7},{7,6},{8,9},{9,8},{10,11... | collective-permute-start | bytes 786440 | tf_op jit(solution)/shard_map/ppermute | solution.py:294
  16.2 0.6 %collective-permute-done.4.refs_3_ = bf16[720,256]{1,0:T(8,128)(2,1)S(1)} collective-permute-done((bf16[720,256]{1,0:T(8,128)(2,1)S(1)}, bf16[720,256]{1,0:T(8,128)(2,1)S(1)}, u32[]{:S(2)}, u32[]{:S(2)}) %collective-permute-start.4) | collective-permute-done | bytes 368672 | tf_op jit(solution)/shard_map/ppermute | solution.py:311
  16.8 0.1 collective-permute-start.5
  16.9 4.4 %collective-permute-done.7.refs_1_ = bf16[512,256]{1,0:T(8,128)(2,1)S(1)} collective-permute-done((bf16[512,256]{1,0:T(8,128)(2,1)S(1)}, bf16[512,256]{1,0:T(8,128)(2,1)S(1)}, u32[]{:S(2)}, u32[]{:S(2)}) %collective-permute-start.7) | collective-permute-done | bytes 262176 | tf_op jit(solution)/shard_map/ppermute | solution.py:294
  21.3 1.7 %early_products.1 = (f32[2,2,2,128,256]{4,3,2,1,0:T(8,128)S(1)}, f32[2,2,2,128,16]{4,3,2,1,0:T(8,128)S(1)}) custom-call(bf16[256,8192]{1,0:T(8,128)(2,1)S(1)} %get-tuple-element.29.x, bf16[256,1024]{1,0:T(8,128)(2,1)S(1)} %get-tuple-element.30.m, bf16[128,3584]{1,0:T(8,128)(2,1)S(1)} %collective-permute-done.c_xo.xo, ...), custom_call_target="tpu_custom_call" | custom-call | flops 1 | bytes 1 | tf_op jit(solution)/shard_map/early_products/pallas_call | solution.py:317
  23.0 0.6 %collective-permute-done.6.refs_0_ = bf16[1232,256]{1,0:T(8,128)(2,1)S(1)} collective-permute-done((bf16[1232,256]{1,0:T(8,128)(2,1)S(1)}, bf16[1232,256]{1,0:T(8,128)(2,1)S(1)}, u32[]{:S(2)}, u32[]{:S(2)}) %collective-permute-start.6) | collective-permute-done | bytes 630816 | tf_op jit(solution)/shard_map/ppermute | solution.py:311
  23.6 0.7 %probe_products.1 = (f32[256,256]{1,0:T(8,128)S(1)}, f32[16,256]{1,0:T(8,128)S(1)}, bf16[304,256]{1,0:T(8,128)(2,1)S(1)}) custom-call(bf16[256,8192]{1,0:T(8,128)(2,1)S(1)} %get-tuple-element.29.x, bf16[256,1024]{1,0:T(8,128)(2,1)S(1)} %get-tuple-element.30.m, bf16[128,3584]{1,0:T(8,128)(2,1)S(1)} %collective-permute-done.1.p_xo.xo, ...), custom_call_target="tpu_custom_call" | custom-call | flops 1 | bytes 1 | tf_op jit(solution)/shard_map/probe_products/pallas_call | solution.py:317
  24.3 0.7 %candidate_products.1 = (f32[256,256]{1,0:T(8,128)S(1)}, f32[16,256]{1,0:T(8,128)S(1)}, bf16[304,256]{1,0:T(8,128)(2,1)S(1)}) custom-call(bf16[256,8192]{1,0:T(8,128)(2,1)S(1)} %get-tuple-element.29.x, bf16[256,1024]{1,0:T(8,128)(2,1)S(1)} %get-tuple-element.30.m, bf16[128,3584]{1,0:T(8,128)(2,1)S(1)} %collective-permute-done.c_xo.xo, ...), custom_call_target="tpu_custom_call" | custom-call | flops 1 | bytes 1 | tf_op jit(solution)/shard_map/candidate_products/pallas_call | solution.py:317
  25.0 0.5 %collective-permute-start.9 = (bf16[304,256]{1,0:T(8,128)(2,1)S(1)}, bf16[304,256]{1,0:T(8,128)(2,1)S(1)}, u32[]{:S(2)}, u32[]{:S(2)}) collective-permute-start(bf16[304,256]{1,0:T(8,128)(2,1)S(1)} %get-tuple-element.43), channel_id=1, source_target_pairs={{0,4},{4,0},{8,12},{12,8},{16,20},{20,16},{24,28},{28,24},{1,5},{5... | collective-permute-start | bytes 466952 | tf_op jit(solution)/shard_map/ppermute | solution.py:294
  25.6 0.1 collective-permute-done.10.got
  25.7 0.2 probe_sides.1.refs_0_
  25.9 3.0 %collective-permute-start.11 = (bf16[8,4096]{1,0:T(8,128)(2,1)S(1)}, bf16[8,4096]{1,0:T(8,128)(2,1)S(1)}, u32[]{:S(2)}, u32[]{:S(2)}) collective-permute-start(bf16[8,4096]{1,0:T(8,128)(2,1)S(1)} %probe_sides.1.refs_0_), channel_id=1, source_target_pairs={{0,24},{4,28},{8,16},{12,20},{16,8},{20,12},{24,0},{28,4},{1,25},{... | collective-permute-start | bytes 196616 | tf_op jit(solution)/shard_map/ppermute | solution.py:294
  28.9 0.5 %collective-permute-start.12 = (bf16[8,4096]{1,0:T(8,128)(2,1)S(1)}, bf16[8,4096]{1,0:T(8,128)(2,1)S(1)}, u32[]{:S(2)}, u32[]{:S(2)}) collective-permute-start(bf16[8,4096]{1,0:T(8,128)(2,1)S(1)} %probe_sides.1.refs_0_), channel_id=1, source_target_pairs={{0,16},{1,9},{2,18},{3,11},{4,12},{5,21},{6,14},{7,23},{8,24},{9,1... | collective-permute-start | bytes 196616 | tf_op jit(solution)/shard_map/ppermute | solution.py:311
  29.4 0.1 collective-permute-start.13
  29.5 0.2 candidate_sides.1
  29.8 0.1 collective-permute-start.15
  29.8 1.4 %collective-permute-done.11.refs_1_ = bf16[8,4096]{1,0:T(8,128)(2,1)S(1)} collective-permute-done((bf16[8,4096]{1,0:T(8,128)(2,1)S(1)}, bf16[8,4096]{1,0:T(8,128)(2,1)S(1)}, u32[]{:S(2)}, u32[]{:S(2)}) %collective-permute-start.11) | collective-permute-done | bytes 65568 | tf_op jit(solution)/shard_map/ppermute | solution.py:294
  31.3 1.9 %collective-permute-done.12.refs_2_ = bf16[8,4096]{1,0:T(8,128)(2,1)S(1)} collective-permute-done((bf16[8,4096]{1,0:T(8,128)(2,1)S(1)}, bf16[8,4096]{1,0:T(8,128)(2,1)S(1)}, u32[]{:S(2)}, u32[]{:S(2)}) %collective-permute-start.12) | collective-permute-done | bytes 65568 | tf_op jit(solution)/shard_map/ppermute | solution.py:311
  33.2 0.5 %collective-permute-done.13.refs_3_ = bf16[8,4096]{1,0:T(8,128)(2,1)S(1)} collective-permute-done((bf16[8,4096]{1,0:T(8,128)(2,1)S(1)}, bf16[8,4096]{1,0:T(8,128)(2,1)S(1)}, u32[]{:S(2)}, u32[]{:S(2)}) %collective-permute-start.13) | collective-permute-done | bytes 65568 | tf_op jit(solution)/shard_map/ppermute | solution.py:311
  33.7 0.4 %score_shares.1 = (f32[12,32]{1,0:T(8,128)S(1)}, f32[12,32]{1,0:T(8,128)S(1)}) custom-call(bf16[8,4096]{1,0:T(8,128)(2,1)S(1)} %get-tuple-element.48.c_ref, bf16[8,4096]{1,0:T(8,128)(2,1)S(1)} %probe_sides.1.refs_0_, bf16[8,4096]{1,0:T(8,128)(2,1)S(1)} %collective-permute-done.11.refs_1_, bf16[8,4096]{1,0:T(8,128)(2,1)S(1)} %collective-permute-done.12.refs_2_, ...), custom_call_target="tpu_custom_call" | custom-call | flops 1 | bytes 1 | tf_op jit(solution)/shard_map/score_shares/pallas_call | solution.py:317
  34.1 0.1 collective-permute-start.14
  34.1 0.8 %candidate_features.1 = bf16[4,8192]{1,0:T(4,128)(2,1)} custom-call(f32[64,256]{1,0:T(8,128)S(1)} %get-tuple-element.54.own, f32[64,256]{1,0:T(8,128)S(1)} %collective-permute-done.15.got), custom_call_target="tpu_custom_call" | custom-call | flops 1 | bytes 1 | tf_op jit(solution)/shard_map/candidate_features/pallas_call | solution.py:317
  35.0 0.3 collective-permute-done.14.got
  35.3 0.6 %scores.1 = f32[4,32]{1,0:T(4,128)} custom-call(f32[12,32]{1,0:T(8,128)S(1)} %get-tuple-element.52.own, f32[12,32]{1,0:T(8,128)S(1)} %collective-permute-done.14.got), custom_call_target="tpu_custom_call" | custom-call | flops 1 | bytes 1 | tf_op jit(solution)/shard_map/scores/pallas_call | solution.py:317
  (13 shorter events, 0.2 us)
Async XLA Ops:
  0.6 11.5 %collective-permute-start.2 = (bf16[1024,256]{1,0:T(8,128)(2,1)}, bf16[1024,256]{1,0:T(8,128)(2,1)S(1)}, u32[]{:S(2)}, u32[]{:S(2)}) collective-permute-start(bf16[1024,256]{1,0:T(8,128)(2,1)} %in_hbm.1), channel_id=1, source_target_pairs={{0,8},{1,17},{2,10},{3,19},{4,20},{5,13},{6,22},{7,15},{8,0},{9,25... | collective-permute-start | bytes 1572872 | tf_op jit(solution)/shard_map/ppermute | solution.py:311
  6.4 5.8 %collective-permute-start.3 = (bf16[208,256]{1,0:T(8,128)(2,1)S(1)}, bf16[208,256]{1,0:T(8,128)(2,1)S(1)}, u32[]{:S(2)}, u32[]{:S(2)}) collective-permute-start(bf16[208,256]{1,0:T(8,128)(2,1)S(1)} %get-tuple-element.34.extra.refs_0_), channel_id=1, source_target_pairs={{0,8},{1,17},{2,10},{3,19},{4,20},{5,13},{6,22},{7,15},{8,0},{9,25... | collective-permute-start | bytes 319496 | tf_op jit(solution)/shard_map/ppermute | solution.py:311
  6.5 14.8 %collective-permute-start = (bf16[128,3584]{1,0:T(8,128)(2,1)S(1)}, bf16[128,3584]{1,0:T(8,128)(2,1)S(1)}, u32[]{:S(2)}, u32[]{:S(2)}) collective-permute-start(bf16[128,3584]{1,0:T(8,128)(2,1)S(1)} %get-tuple-element.31), channel_id=1, source_target_pairs={{0,4},{4,0},{8,12},{12,8},{16,20},{20,16},{24,28},{28,24},{1,5},{5... | collective-permute-start | bytes 2752520 | tf_op jit(solution)/shard_map/ppermute | solution.py:294
  6.5 14.8 %collective-permute-start.1 = (bf16[128,3584]{1,0:T(8,128)(2,1)S(1)}, bf16[128,3584]{1,0:T(8,128)(2,1)S(1)}, u32[]{:S(2)}, u32[]{:S(2)}) collective-permute-start(bf16[128,3584]{1,0:T(8,128)(2,1)S(1)} %get-tuple-element.33), channel_id=1, source_target_pairs={{0,4},{4,0},{8,12},{12,8},{16,20},{20,16},{24,28},{28,24},{1,5},{5... | collective-permute-start | bytes 2752520 | tf_op jit(solution)/shard_map/ppermute | solution.py:294
  9.2 7.6 %collective-permute-start.4 = (bf16[720,256]{1,0:T(8,128)(2,1)S(1)}, bf16[720,256]{1,0:T(8,128)(2,1)S(1)}, u32[]{:S(2)}, u32[]{:S(2)}) collective-permute-start(bf16[720,256]{1,0:T(8,128)(2,1)S(1)} %get-tuple-element.37), channel_id=1, source_target_pairs={{0,16},{1,9},{2,18},{3,11},{4,12},{5,21},{6,14},{7,23},{8,24},{9,1... | collective-permute-start | bytes 1105928 | tf_op jit(solution)/shard_map/ppermute | solution.py:311
  12.2 11.4 %collective-permute-start.6 = (bf16[1232,256]{1,0:T(8,128)(2,1)S(1)}, bf16[1232,256]{1,0:T(8,128)(2,1)S(1)}, u32[]{:S(2)}, u32[]{:S(2)}) collective-permute-start(bf16[1232,256]{1,0:T(8,128)(2,1)S(1)} %pad_maximum_fusion), channel_id=1, source_target_pairs={{0,16},{1,9},{2,18},{3,11},{4,12},{5,21},{6,14},{7,23},{8,24},{9,1... | collective-permute-start | bytes 1892360 | tf_op jit(solution)/shard_map/ppermute | solution.py:311
  14.6 6.7 %collective-permute-start.7 = (bf16[512,256]{1,0:T(8,128)(2,1)S(1)}, bf16[512,256]{1,0:T(8,128)(2,1)S(1)}, u32[]{:S(2)}, u32[]{:S(2)}) collective-permute-start(bf16[512,256]{1,0:T(8,128)(2,1)S(1)} %slice.9), channel_id=1, source_target_pairs={{0,1},{1,0},{2,3},{3,2},{4,5},{5,4},{6,7},{7,6},{8,9},{9,8},{10,11... | collective-permute-start | bytes 786440 | tf_op jit(solution)/shard_map/ppermute | solution.py:294
  16.8 4.4 %collective-permute-start.5 = (bf16[592,256]{1,0:T(8,128)(2,1)S(1)}, bf16[592,256]{1,0:T(8,128)(2,1)S(1)}, u32[]{:S(2)}, u32[]{:S(2)}) collective-permute-start(bf16[592,256]{1,0:T(8,128)(2,1)S(1)} %slice.8), channel_id=1, source_target_pairs={{0,4},{4,0},{8,12},{12,8},{16,20},{20,16},{24,28},{28,24},{1,5},{5... | collective-permute-start | bytes 909320 | tf_op jit(solution)/shard_map/ppermute | solution.py:294
  21.3 1.7 %collective-permute-start.8 = (bf16[512,256]{1,0:T(8,128)(2,1)S(1)}, bf16[512,256]{1,0:T(8,128)(2,1)S(1)}, u32[]{:S(2)}, u32[]{:S(2)}) collective-permute-start(bf16[512,256]{1,0:T(8,128)(2,1)S(1)} %collective-permute-done.7.refs_1_), channel_id=1, source_target_pairs={{0,4},{4,0},{8,12},{12,8},{16,20},{20,16},{24,28},{28,24},{1,5},{5... | collective-permute-start | bytes 786440 | tf_op jit(solution)/shard_map/ppermute | solution.py:294
  24.3 1.4 %collective-permute-start.10 = (bf16[304,256]{1,0:T(8,128)(2,1)S(1)}, bf16[304,256]{1,0:T(8,128)(2,1)S(1)}, u32[]{:S(2)}, u32[]{:S(2)}) collective-permute-start(bf16[304,256]{1,0:T(8,128)(2,1)S(1)} %get-tuple-element.47), channel_id=1, source_target_pairs={{0,4},{4,0},{8,12},{12,8},{16,20},{20,16},{24,28},{28,24},{1,5},{5... | collective-permute-start | bytes 466952 | tf_op jit(solution)/shard_map/ppermute | solution.py:294
  25.0 4.5 %collective-permute-start.9 = (bf16[304,256]{1,0:T(8,128)(2,1)S(1)}, bf16[304,256]{1,0:T(8,128)(2,1)S(1)}, u32[]{:S(2)}, u32[]{:S(2)}) collective-permute-start(bf16[304,256]{1,0:T(8,128)(2,1)S(1)} %get-tuple-element.43), channel_id=1, source_target_pairs={{0,4},{4,0},{8,12},{12,8},{16,20},{20,16},{24,28},{28,24},{1,5},{5... | collective-permute-start | bytes 466952 | tf_op jit(solution)/shard_map/ppermute | solution.py:294
  25.9 5.4 %collective-permute-start.11 = (bf16[8,4096]{1,0:T(8,128)(2,1)S(1)}, bf16[8,4096]{1,0:T(8,128)(2,1)S(1)}, u32[]{:S(2)}, u32[]{:S(2)}) collective-permute-start(bf16[8,4096]{1,0:T(8,128)(2,1)S(1)} %probe_sides.1.refs_0_), channel_id=1, source_target_pairs={{0,24},{4,28},{8,16},{12,20},{16,8},{20,12},{24,0},{28,4},{1,25},{... | collective-permute-start | bytes 196616 | tf_op jit(solution)/shard_map/ppermute | solution.py:294
  28.9 4.3 %collective-permute-start.12 = (bf16[8,4096]{1,0:T(8,128)(2,1)S(1)}, bf16[8,4096]{1,0:T(8,128)(2,1)S(1)}, u32[]{:S(2)}, u32[]{:S(2)}) collective-permute-start(bf16[8,4096]{1,0:T(8,128)(2,1)S(1)} %probe_sides.1.refs_0_), channel_id=1, source_target_pairs={{0,16},{1,9},{2,18},{3,11},{4,12},{5,21},{6,14},{7,23},{8,24},{9,1... | collective-permute-start | bytes 196616 | tf_op jit(solution)/shard_map/ppermute | solution.py:311
  29.4 4.3 %collective-permute-start.13 = (bf16[8,4096]{1,0:T(8,128)(2,1)S(1)}, bf16[8,4096]{1,0:T(8,128)(2,1)S(1)}, u32[]{:S(2)}, u32[]{:S(2)}) collective-permute-start(bf16[8,4096]{1,0:T(8,128)(2,1)S(1)} %probe_sides.1.refs_0_), channel_id=1, source_target_pairs={{0,8},{1,17},{2,10},{3,19},{4,20},{5,13},{6,22},{7,15},{8,0},{9,25... | collective-permute-start | bytes 196616 | tf_op jit(solution)/shard_map/ppermute | solution.py:311
  29.8 4.4 %collective-permute-start.15 = (f32[64,256]{1,0:T(8,128)S(1)}, f32[64,256]{1,0:T(8,128)S(1)}, u32[]{:S(2)}, u32[]{:S(2)}) collective-permute-start(f32[64,256]{1,0:T(8,128)S(1)} %get-tuple-element.55), channel_id=1, source_target_pairs={{0,4},{4,0},{8,12},{12,8},{16,20},{20,16},{24,28},{28,24},{1,5},{5... | collective-permute-start | bytes 196616 | tf_op jit(solution)/shard_map/ppermute | solution.py:294
  34.1 1.2 %collective-permute-start.14 = (f32[12,32]{1,0:T(8,128)S(1)}, f32[12,32]{1,0:T(8,128)S(1)}, u32[]{:S(2)}, u32[]{:S(2)}) collective-permute-start(f32[12,32]{1,0:T(8,128)S(1)} %get-tuple-element.53), channel_id=1, source_target_pairs={{0,4},{4,0},{8,12},{12,8},{16,20},{20,16},{24,28},{28,24},{1,5},{5... | collective-permute-start | bytes 4616 | tf_op jit(solution)/shard_map/ppermute | solution.py:294

commit v8 on v7

--- a/solution.py
+++ b/solution.py
@@ -114,7 +114,7 @@
             yield who, source[:, pl.ds(pl.multiple_of(j * wide + first, 128), count)]
         else:
             at = there_at(kd, ku)[sketch][kind] + first
-            yield who, xo[:, at : at + count]
+            yield who, jnp.concatenate([ref[:, at : at + count] for ref in xo], axis=0)
 
 
 def small_sums(n, ks, places, x, m, xo, refs):
@@ -134,10 +134,13 @@
 
 def products(n, places, x, m, xo, refs):
     sums = [[0.0, 0.0], [0.0, 0.0]]
+    height = x.shape[0]
     for ref, row, block, sketch, first, count in places:
         piece = refs[ref][row : row + count, :]
-        for who, rows in spans(n, x, m, xo, block, sketch, first, count):
-            sums[who][sketch] += dot(rows, piece)
+        whos, rows = zip(*spans(n, x, m, xo, block, sketch, first, count))
+        total = dot(jnp.concatenate(rows, axis=0), piece)
+        for i, who in enumerate(whos):
+            sums[who][sketch] += total[i * height : (i + 1) * height]
     return sums
 
 
@@ -167,16 +170,16 @@
 def early_kernel(n, ks, places, tables, x, m, c_xo, p_xo, own_sums, own_small, *refs):
     refs, (sums_ref, small_ref) = refs[:-2], refs[-2:]
     half = c_xo.shape[0]
-    for side, xo in enumerate((c_xo, p_xo)):
-        rows = pl.ds(side * half, half)
-        views = x.at[rows], m.at[rows], xo
-        small = small_sums(n, ks, tables, *views, refs)
-        sums = products(n, places, *views, refs)
+    views = x, m, (c_xo, p_xo)
+    small = small_sums(n, ks, tables, *views, refs)
+    sums = products(n, places, *views, refs)
+    for side in range(2):
+        rows = slice(side * half, (side + 1) * half)
         for t in range(2):
-            small_ref[side, 0, t] = small[0][t] + own_small[side, t]
-            small_ref[side, 1, t] = small[1][t]
-            sums_ref[side, 0, t] = sums[0][t] + own_sums[side, t]
-            sums_ref[side, 1, t] = sums[1][t]
+            small_ref[side, 0, t] = small[0][t][rows] + own_small[side, t]
+            small_ref[side, 1, t] = small[1][t][rows]
+            sums_ref[side, 0, t] = sums[0][t][rows] + own_sums[side, t]
+            sums_ref[side, 1, t] = sums[1][t][rows]
 
 
 def late_kernel(n, ks, side, places, tables, x, m, xo, live, sums, early_small, *refs):
@@ -184,7 +187,7 @@
     core = lax.axis_index("fsdp") % 2
     half = x.shape[0] // 2
     rows = pl.ds(side * half, half)
-    views = x.at[rows], m.at[rows], xo
+    views = x.at[rows], m.at[rows], (xo,)
     late = products(n, places, *views, refs)
     late_small = small_sums(n, ks, tables, *views, refs)
     for t in range(2):

time: 36.1 us -> 36 us (level)
  no operation moved by 1% of the time
where the time goes in v8:
time: 36 us; the launch traced here: 35.8 us
  starting transfers between devices  14.1 us (39%)
  waiting for transfers between devices  10.8 us (30%)
  Pallas kernels  10 us (28%)
  between operations  0.77 us (2%)
    pallas_call x10, Pallas kernels, kernel(): pl.pallas_call(f, out_shape=outs, in_specs=in_specs or [VMEM] * len(opera...  10 us
    ppermute x6, starting transfers between devices, along(): return lax.ppermute(x, ('fsdp', 'dp'), pairs)  8.14 us
    ppermute x10, waiting for transfers between devices, swap(): return lax.ppermute(x, axis, [(i, i ^ k) for i in range(size)])  6.36 us
    ppermute x10, starting transfers between devices, swap(): return lax.ppermute(x, axis, [(i, i ^ k) for i in range(size)])  5.97 us
    ppermute x6, waiting for transfers between devices, along(): return lax.ppermute(x, ('fsdp', 'dp'), pairs)  4.49 us
  transfers between devices with their start and end apart: 16, of which 9 were waited for; matrix products, arithmetic and copies ran while one was open for 0% of the time, Pallas kernels for 25%

profile of v8, /device:TPU:0, one launch (start us, length us, event | category | flops | bytes accessed | tf_op | source)
XLA Modules:
  0.0 35.8 jit_solution(10337053797950973921)
XLA Ops:
  0.6 3.0 %collective-permute-start.2 = (bf16[1024,256]{1,0:T(8,128)(2,1)}, bf16[1024,256]{1,0:T(8,128)(2,1)S(1)}, u32[]{:S(2)}, u32[]{:S(2)}) collective-permute-start(bf16[1024,256]{1,0:T(8,128)(2,1)} %in_hbm.1), channel_id=1, source_target_pairs={{0,8},{1,17},{2,10},{3,19},{4,20},{5,13},{6,22},{7,15},{8,0},{9,25... | collective-permute-start | bytes 1572872 | tf_op jit(solution)/shard_map/ppermute | solution.py:314
  3.6 2.7 %prepare.1 = (bf16[208,256]{1,0:T(8,128)(2,1)S(1)}, bf16[256,8192]{1,0:T(8,128)(2,1)S(1)}, bf16[256,1024]{1,0:T(8,128)(2,1)S(1)}, bf16[2,16,128]{2,1,0:T(8,128)(...) custom-call(bf16[1024,128]{1,0:T(8,128)(2,1)} %down_hbm.1, bf16[128,128]{1,0:T(8,128)(2,1)} %up_hbm.1, ...), custom_call_target="tpu_custom_call" | custom-call | flops 1 | bytes 1 | tf_op jit(solution)/shard_map/prepare/pallas_call | solution.py:320
  6.4 0.1 collective-permute-start.3
  6.5 0.5 %collective-permute-start.1 = (bf16[128,3584]{1,0:T(8,128)(2,1)S(1)}, bf16[128,3584]{1,0:T(8,128)(2,1)S(1)}, u32[]{:S(2)}, u32[]{:S(2)}) collective-permute-start(bf16[128,3584]{1,0:T(8,128)(2,1)S(1)} %get-tuple-element.33), channel_id=1, source_target_pairs={{0,4},{4,0},{8,12},{12,8},{16,20},{20,16},{24,28},{28,24},{1,5},{5... | collective-permute-start | bytes 2752520 | tf_op jit(solution)/shard_map/ppermute | solution.py:297
  7.0 2.2 %own_products.1 = (bf16[1024,256]{1,0:T(8,128)(2,1)S(1)}, bf16[720,256]{1,0:T(8,128)(2,1)S(1)}, f32[2,2,128,256]{3,2,1,0:T(8,128)S(1)}, f32[2,2,128,16]{3,2,1,0:T(8,128)S(1)}) custom-call(bf16[1024,256]{1,0:T(8,128)(2,1)} %in_hbm.1, bf16[208,256]{1,0:T(8,128)(2,1)S(1)} %get-tuple-element.34.extra.refs_0_, bf16[256,8192]{1,0:T(8,128)(2,1)S(1)} %get-tuple-element.29.x, ...), custom_call_target="tpu_custom_call" | custom-call | flops 1 | bytes 1 | tf_op jit(solution)/shard_map/own_products/pallas_call | solution.py:320
  9.2 2.0 %collective-permute-start.4 = (bf16[720,256]{1,0:T(8,128)(2,1)S(1)}, bf16[720,256]{1,0:T(8,128)(2,1)S(1)}, u32[]{:S(2)}, u32[]{:S(2)}) collective-permute-start(bf16[720,256]{1,0:T(8,128)(2,1)S(1)} %get-tuple-element.37), channel_id=1, source_target_pairs={{0,16},{1,9},{2,18},{3,11},{4,12},{5,21},{6,14},{7,23},{8,24},{9,1... | collective-permute-start | bytes 1105928 | tf_op jit(solution)/shard_map/ppermute | solution.py:314
  11.3 0.9 %collective-permute-done.3.refs_2_ = bf16[208,256]{1,0:T(8,128)(2,1)S(1)} collective-permute-done((bf16[208,256]{1,0:T(8,128)(2,1)S(1)}, bf16[208,256]{1,0:T(8,128)(2,1)S(1)}, u32[]{:S(2)}, u32[]{:S(2)}) %collective-permute-start.3) | collective-permute-done | bytes 106528 | tf_op jit(solution)/shard_map/ppermute | solution.py:314
  12.2 2.4 %collective-permute-start.6 = (bf16[1232,256]{1,0:T(8,128)(2,1)S(1)}, bf16[1232,256]{1,0:T(8,128)(2,1)S(1)}, u32[]{:S(2)}, u32[]{:S(2)}) collective-permute-start(bf16[1232,256]{1,0:T(8,128)(2,1)S(1)} %pad_maximum_fusion), channel_id=1, source_target_pairs={{0,16},{1,9},{2,18},{3,11},{4,12},{5,21},{6,14},{7,23},{8,24},{9,1... | collective-permute-start | bytes 1892360 | tf_op jit(solution)/shard_map/ppermute | solution.py:314
  14.6 1.6 %collective-permute-start.7 = (bf16[512,256]{1,0:T(8,128)(2,1)S(1)}, bf16[512,256]{1,0:T(8,128)(2,1)S(1)}, u32[]{:S(2)}, u32[]{:S(2)}) collective-permute-start(bf16[512,256]{1,0:T(8,128)(2,1)S(1)} %slice.9), channel_id=1, source_target_pairs={{0,1},{1,0},{2,3},{3,2},{4,5},{5,4},{6,7},{7,6},{8,9},{9,8},{10,11... | collective-permute-start | bytes 786440 | tf_op jit(solution)/shard_map/ppermute | solution.py:297
  16.2 0.6 %collective-permute-done.4.refs_3_ = bf16[720,256]{1,0:T(8,128)(2,1)S(1)} collective-permute-done((bf16[720,256]{1,0:T(8,128)(2,1)S(1)}, bf16[720,256]{1,0:T(8,128)(2,1)S(1)}, u32[]{:S(2)}, u32[]{:S(2)}) %collective-permute-start.4) | collective-permute-done | bytes 368672 | tf_op jit(solution)/shard_map/ppermute | solution.py:314
  16.8 0.1 collective-permute-start.5
  16.9 4.4 %collective-permute-done.7.refs_1_ = bf16[512,256]{1,0:T(8,128)(2,1)S(1)} collective-permute-done((bf16[512,256]{1,0:T(8,128)(2,1)S(1)}, bf16[512,256]{1,0:T(8,128)(2,1)S(1)}, u32[]{:S(2)}, u32[]{:S(2)}) %collective-permute-start.7) | collective-permute-done | bytes 262176 | tf_op jit(solution)/shard_map/ppermute | solution.py:297
  21.3 1.6 %early_products.1 = (f32[2,2,2,128,256]{4,3,2,1,0:T(8,128)S(1)}, f32[2,2,2,128,16]{4,3,2,1,0:T(8,128)S(1)}) custom-call(bf16[256,8192]{1,0:T(8,128)(2,1)S(1)} %get-tuple-element.29.x, bf16[256,1024]{1,0:T(8,128)(2,1)S(1)} %get-tuple-element.30.m, bf16[128,3584]{1,0:T(8,128)(2,1)S(1)} %collective-permute-done.c_xo.xo, ...), custom_call_target="tpu_custom_call" | custom-call | flops 1 | bytes 1 | tf_op jit(solution)/shard_map/early_products/pallas_call | solution.py:320
  23.0 0.6 %collective-permute-done.6.refs_0_ = bf16[1232,256]{1,0:T(8,128)(2,1)S(1)} collective-permute-done((bf16[1232,256]{1,0:T(8,128)(2,1)S(1)}, bf16[1232,256]{1,0:T(8,128)(2,1)S(1)}, u32[]{:S(2)}, u32[]{:S(2)}) %collective-permute-start.6) | collective-permute-done | bytes 630816 | tf_op jit(solution)/shard_map/ppermute | solution.py:314
  23.6 0.6 %probe_products.1 = (f32[256,256]{1,0:T(8,128)S(1)}, f32[16,256]{1,0:T(8,128)S(1)}, bf16[304,256]{1,0:T(8,128)(2,1)S(1)}) custom-call(bf16[256,8192]{1,0:T(8,128)(2,1)S(1)} %get-tuple-element.29.x, bf16[256,1024]{1,0:T(8,128)(2,1)S(1)} %get-tuple-element.30.m, bf16[128,3584]{1,0:T(8,128)(2,1)S(1)} %collective-permute-done.1.p_xo.xo, ...), custom_call_target="tpu_custom_call" | custom-call | flops 1 | bytes 1 | tf_op jit(solution)/shard_map/probe_products/pallas_call | solution.py:320
  24.3 0.6 %candidate_products.1 = (f32[256,256]{1,0:T(8,128)S(1)}, f32[16,256]{1,0:T(8,128)S(1)}, bf16[304,256]{1,0:T(8,128)(2,1)S(1)}) custom-call(bf16[256,8192]{1,0:T(8,128)(2,1)S(1)} %get-tuple-element.29.x, bf16[256,1024]{1,0:T(8,128)(2,1)S(1)} %get-tuple-element.30.m, bf16[128,3584]{1,0:T(8,128)(2,1)S(1)} %collective-permute-done.c_xo.xo, ...), custom_call_target="tpu_custom_call" | custom-call | flops 1 | bytes 1 | tf_op jit(solution)/shard_map/candidate_products/pallas_call | solution.py:320
  24.9 0.6 %collective-permute-start.9 = (bf16[304,256]{1,0:T(8,128)(2,1)S(1)}, bf16[304,256]{1,0:T(8,128)(2,1)S(1)}, u32[]{:S(2)}, u32[]{:S(2)}) collective-permute-start(bf16[304,256]{1,0:T(8,128)(2,1)S(1)} %get-tuple-element.43), channel_id=1, source_target_pairs={{0,4},{4,0},{8,12},{12,8},{16,20},{20,16},{24,28},{28,24},{1,5},{5... | collective-permute-start | bytes 466952 | tf_op jit(solution)/shard_map/ppermute | solution.py:297
  25.4 0.2 collective-permute-done.10.got
  25.6 0.2 probe_sides.1.refs_0_
  25.9 3.0 %collective-permute-start.11 = (bf16[8,4096]{1,0:T(8,128)(2,1)S(1)}, bf16[8,4096]{1,0:T(8,128)(2,1)S(1)}, u32[]{:S(2)}, u32[]{:S(2)}) collective-permute-start(bf16[8,4096]{1,0:T(8,128)(2,1)S(1)} %probe_sides.1.refs_0_), channel_id=1, source_target_pairs={{0,24},{4,28},{8,16},{12,20},{16,8},{20,12},{24,0},{28,4},{1,25},{... | collective-permute-start | bytes 196616 | tf_op jit(solution)/shard_map/ppermute | solution.py:297
  28.8 0.5 %collective-permute-start.12 = (bf16[8,4096]{1,0:T(8,128)(2,1)S(1)}, bf16[8,4096]{1,0:T(8,128)(2,1)S(1)}, u32[]{:S(2)}, u32[]{:S(2)}) collective-permute-start(bf16[8,4096]{1,0:T(8,128)(2,1)S(1)} %probe_sides.1.refs_0_), channel_id=1, source_target_pairs={{0,16},{1,9},{2,18},{3,11},{4,12},{5,21},{6,14},{7,23},{8,24},{9,1... | collective-permute-start | bytes 196616 | tf_op jit(solution)/shard_map/ppermute | solution.py:314
  29.3 0.1 collective-permute-start.13
  29.5 0.2 candidate_sides.1
  29.7 0.1 collective-permute-start.15
  29.8 1.4 %collective-permute-done.11.refs_1_ = bf16[8,4096]{1,0:T(8,128)(2,1)S(1)} collective-permute-done((bf16[8,4096]{1,0:T(8,128)(2,1)S(1)}, bf16[8,4096]{1,0:T(8,128)(2,1)S(1)}, u32[]{:S(2)}, u32[]{:S(2)}) %collective-permute-start.11) | collective-permute-done | bytes 65568 | tf_op jit(solution)/shard_map/ppermute | solution.py:297
  31.2 1.9 %collective-permute-done.12.refs_2_ = bf16[8,4096]{1,0:T(8,128)(2,1)S(1)} collective-permute-done((bf16[8,4096]{1,0:T(8,128)(2,1)S(1)}, bf16[8,4096]{1,0:T(8,128)(2,1)S(1)}, u32[]{:S(2)}, u32[]{:S(2)}) %collective-permute-start.12) | collective-permute-done | bytes 65568 | tf_op jit(solution)/shard_map/ppermute | solution.py:314
  33.1 0.5 %collective-permute-done.13.refs_3_ = bf16[8,4096]{1,0:T(8,128)(2,1)S(1)} collective-permute-done((bf16[8,4096]{1,0:T(8,128)(2,1)S(1)}, bf16[8,4096]{1,0:T(8,128)(2,1)S(1)}, u32[]{:S(2)}, u32[]{:S(2)}) %collective-permute-start.13) | collective-permute-done | bytes 65568 | tf_op jit(solution)/shard_map/ppermute | solution.py:314
  33.6 0.4 %score_shares.1 = (f32[12,32]{1,0:T(8,128)S(1)}, f32[12,32]{1,0:T(8,128)S(1)}) custom-call(bf16[8,4096]{1,0:T(8,128)(2,1)S(1)} %get-tuple-element.48.c_ref, bf16[8,4096]{1,0:T(8,128)(2,1)S(1)} %probe_sides.1.refs_0_, bf16[8,4096]{1,0:T(8,128)(2,1)S(1)} %collective-permute-done.11.refs_1_, bf16[8,4096]{1,0:T(8,128)(2,1)S(1)} %collective-permute-done.12.refs_2_, ...), custom_call_target="tpu_custom_call" | custom-call | flops 1 | bytes 1 | tf_op jit(solution)/shard_map/score_shares/pallas_call | solution.py:320
  34.0 0.1 collective-permute-start.14
  34.1 0.8 %candidate_features.1 = bf16[4,8192]{1,0:T(4,128)(2,1)} custom-call(f32[64,256]{1,0:T(8,128)S(1)} %get-tuple-element.54.own, f32[64,256]{1,0:T(8,128)S(1)} %collective-permute-done.15.got), custom_call_target="tpu_custom_call" | custom-call | flops 1 | bytes 1 | tf_op jit(solution)/shard_map/candidate_features/pallas_call | solution.py:320
  34.9 0.3 collective-permute-done.14.got
  35.2 0.6 %scores.1 = f32[4,32]{1,0:T(4,128)} custom-call(f32[12,32]{1,0:T(8,128)S(1)} %get-tuple-element.52.own, f32[12,32]{1,0:T(8,128)S(1)} %collective-permute-done.14.got), custom_call_target="tpu_custom_call" | custom-call | flops 1 | bytes 1 | tf_op jit(solution)/shard_map/scores/pallas_call | solution.py:320
  (13 shorter events, 0.2 us)
Async XLA Ops:
  0.6 11.5 %collective-permute-start.2 = (bf16[1024,256]{1,0:T(8,128)(2,1)}, bf16[1024,256]{1,0:T(8,128)(2,1)S(1)}, u32[]{:S(2)}, u32[]{:S(2)}) collective-permute-start(bf16[1024,256]{1,0:T(8,128)(2,1)} %in_hbm.1), channel_id=1, source_target_pairs={{0,8},{1,17},{2,10},{3,19},{4,20},{5,13},{6,22},{7,15},{8,0},{9,25... | collective-permute-start | bytes 1572872 | tf_op jit(solution)/shard_map/ppermute | solution.py:314
  6.4 5.8 %collective-permute-start.3 = (bf16[208,256]{1,0:T(8,128)(2,1)S(1)}, bf16[208,256]{1,0:T(8,128)(2,1)S(1)}, u32[]{:S(2)}, u32[]{:S(2)}) collective-permute-start(bf16[208,256]{1,0:T(8,128)(2,1)S(1)} %get-tuple-element.34.extra.refs_0_), channel_id=1, source_target_pairs={{0,8},{1,17},{2,10},{3,19},{4,20},{5,13},{6,22},{7,15},{8,0},{9,25... | collective-permute-start | bytes 319496 | tf_op jit(solution)/shard_map/ppermute | solution.py:314
  6.5 14.8 %collective-permute-start = (bf16[128,3584]{1,0:T(8,128)(2,1)S(1)}, bf16[128,3584]{1,0:T(8,128)(2,1)S(1)}, u32[]{:S(2)}, u32[]{:S(2)}) collective-permute-start(bf16[128,3584]{1,0:T(8,128)(2,1)S(1)} %get-tuple-element.31), channel_id=1, source_target_pairs={{0,4},{4,0},{8,12},{12,8},{16,20},{20,16},{24,28},{28,24},{1,5},{5... | collective-permute-start | bytes 2752520 | tf_op jit(solution)/shard_map/ppermute | solution.py:297
  6.5 14.8 %collective-permute-start.1 = (bf16[128,3584]{1,0:T(8,128)(2,1)S(1)}, bf16[128,3584]{1,0:T(8,128)(2,1)S(1)}, u32[]{:S(2)}, u32[]{:S(2)}) collective-permute-start(bf16[128,3584]{1,0:T(8,128)(2,1)S(1)} %get-tuple-element.33), channel_id=1, source_target_pairs={{0,4},{4,0},{8,12},{12,8},{16,20},{20,16},{24,28},{28,24},{1,5},{5... | collective-permute-start | bytes 2752520 | tf_op jit(solution)/shard_map/ppermute | solution.py:297
  9.2 7.6 %collective-permute-start.4 = (bf16[720,256]{1,0:T(8,128)(2,1)S(1)}, bf16[720,256]{1,0:T(8,128)(2,1)S(1)}, u32[]{:S(2)}, u32[]{:S(2)}) collective-permute-start(bf16[720,256]{1,0:T(8,128)(2,1)S(1)} %get-tuple-element.37), channel_id=1, source_target_pairs={{0,16},{1,9},{2,18},{3,11},{4,12},{5,21},{6,14},{7,23},{8,24},{9,1... | collective-permute-start | bytes 1105928 | tf_op jit(solution)/shard_map/ppermute | solution.py:314
  12.2 11.4 %collective-permute-start.6 = (bf16[1232,256]{1,0:T(8,128)(2,1)S(1)}, bf16[1232,256]{1,0:T(8,128)(2,1)S(1)}, u32[]{:S(2)}, u32[]{:S(2)}) collective-permute-start(bf16[1232,256]{1,0:T(8,128)(2,1)S(1)} %pad_maximum_fusion), channel_id=1, source_target_pairs={{0,16},{1,9},{2,18},{3,11},{4,12},{5,21},{6,14},{7,23},{8,24},{9,1... | collective-permute-start | bytes 1892360 | tf_op jit(solution)/shard_map/ppermute | solution.py:314
  14.6 6.7 %collective-permute-start.7 = (bf16[512,256]{1,0:T(8,128)(2,1)S(1)}, bf16[512,256]{1,0:T(8,128)(2,1)S(1)}, u32[]{:S(2)}, u32[]{:S(2)}) collective-permute-start(bf16[512,256]{1,0:T(8,128)(2,1)S(1)} %slice.9), channel_id=1, source_target_pairs={{0,1},{1,0},{2,3},{3,2},{4,5},{5,4},{6,7},{7,6},{8,9},{9,8},{10,11... | collective-permute-start | bytes 786440 | tf_op jit(solution)/shard_map/ppermute | solution.py:297
  16.8 4.4 %collective-permute-start.5 = (bf16[592,256]{1,0:T(8,128)(2,1)S(1)}, bf16[592,256]{1,0:T(8,128)(2,1)S(1)}, u32[]{:S(2)}, u32[]{:S(2)}) collective-permute-start(bf16[592,256]{1,0:T(8,128)(2,1)S(1)} %slice.8), channel_id=1, source_target_pairs={{0,4},{4,0},{8,12},{12,8},{16,20},{20,16},{24,28},{28,24},{1,5},{5... | collective-permute-start | bytes 909320 | tf_op jit(solution)/shard_map/ppermute | solution.py:297
  21.3 1.7 %collective-permute-start.8 = (bf16[512,256]{1,0:T(8,128)(2,1)S(1)}, bf16[512,256]{1,0:T(8,128)(2,1)S(1)}, u32[]{:S(2)}, u32[]{:S(2)}) collective-permute-start(bf16[512,256]{1,0:T(8,128)(2,1)S(1)} %collective-permute-done.7.refs_1_), channel_id=1, source_target_pairs={{0,4},{4,0},{8,12},{12,8},{16,20},{20,16},{24,28},{28,24},{1,5},{5... | collective-permute-start | bytes 786440 | tf_op jit(solution)/shard_map/ppermute | solution.py:297
  24.2 1.4 %collective-permute-start.10 = (bf16[304,256]{1,0:T(8,128)(2,1)S(1)}, bf16[304,256]{1,0:T(8,128)(2,1)S(1)}, u32[]{:S(2)}, u32[]{:S(2)}) collective-permute-start(bf16[304,256]{1,0:T(8,128)(2,1)S(1)} %get-tuple-element.47), channel_id=1, source_target_pairs={{0,4},{4,0},{8,12},{12,8},{16,20},{20,16},{24,28},{28,24},{1,5},{5... | collective-permute-start | bytes 466952 | tf_op jit(solution)/shard_map/ppermute | solution.py:297
  24.9 4.6 %collective-permute-start.9 = (bf16[304,256]{1,0:T(8,128)(2,1)S(1)}, bf16[304,256]{1,0:T(8,128)(2,1)S(1)}, u32[]{:S(2)}, u32[]{:S(2)}) collective-permute-start(bf16[304,256]{1,0:T(8,128)(2,1)S(1)} %get-tuple-element.43), channel_id=1, source_target_pairs={{0,4},{4,0},{8,12},{12,8},{16,20},{20,16},{24,28},{28,24},{1,5},{5... | collective-permute-start | bytes 466952 | tf_op jit(solution)/shard_map/ppermute | solution.py:297
  25.9 5.4 %collective-permute-start.11 = (bf16[8,4096]{1,0:T(8,128)(2,1)S(1)}, bf16[8,4096]{1,0:T(8,128)(2,1)S(1)}, u32[]{:S(2)}, u32[]{:S(2)}) collective-permute-start(bf16[8,4096]{1,0:T(8,128)(2,1)S(1)} %probe_sides.1.refs_0_), channel_id=1, source_target_pairs={{0,24},{4,28},{8,16},{12,20},{16,8},{20,12},{24,0},{28,4},{1,25},{... | collective-permute-start | bytes 196616 | tf_op jit(solution)/shard_map/ppermute | solution.py:297
  28.8 4.3 %collective-permute-start.12 = (bf16[8,4096]{1,0:T(8,128)(2,1)S(1)}, bf16[8,4096]{1,0:T(8,128)(2,1)S(1)}, u32[]{:S(2)}, u32[]{:S(2)}) collective-permute-start(bf16[8,4096]{1,0:T(8,128)(2,1)S(1)} %probe_sides.1.refs_0_), channel_id=1, source_target_pairs={{0,16},{1,9},{2,18},{3,11},{4,12},{5,21},{6,14},{7,23},{8,24},{9,1... | collective-permute-start | bytes 196616 | tf_op jit(solution)/shard_map/ppermute | solution.py:314
  29.3 4.3 %collective-permute-start.13 = (bf16[8,4096]{1,0:T(8,128)(2,1)S(1)}, bf16[8,4096]{1,0:T(8,128)(2,1)S(1)}, u32[]{:S(2)}, u32[]{:S(2)}) collective-permute-start(bf16[8,4096]{1,0:T(8,128)(2,1)S(1)} %probe_sides.1.refs_0_), channel_id=1, source_target_pairs={{0,8},{1,17},{2,10},{3,19},{4,20},{5,13},{6,22},{7,15},{8,0},{9,25... | collective-permute-start | bytes 196616 | tf_op jit(solution)/shard_map/ppermute | solution.py:314
  29.7 4.4 %collective-permute-start.15 = (f32[64,256]{1,0:T(8,128)S(1)}, f32[64,256]{1,0:T(8,128)S(1)}, u32[]{:S(2)}, u32[]{:S(2)}) collective-permute-start(f32[64,256]{1,0:T(8,128)S(1)} %get-tuple-element.55), channel_id=1, source_target_pairs={{0,4},{4,0},{8,12},{12,8},{16,20},{20,16},{24,28},{28,24},{1,5},{5... | collective-permute-start | bytes 196616 | tf_op jit(solution)/shard_map/ppermute | solution.py:297
  34.0 1.2 %collective-permute-start.14 = (f32[12,32]{1,0:T(8,128)S(1)}, f32[12,32]{1,0:T(8,128)S(1)}, u32[]{:S(2)}, u32[]{:S(2)}) collective-permute-start(f32[12,32]{1,0:T(8,128)S(1)} %get-tuple-element.53), channel_id=1, source_target_pairs={{0,4},{4,0},{8,12},{12,8},{16,20},{20,16},{24,28},{28,24},{1,5},{5... | collective-permute-start | bytes 4616 | tf_op jit(solution)/shard_map/ppermute | solution.py:297

commit v9 on v8

--- a/solution.py
+++ b/solution.py
@@ -259,10 +259,10 @@
 
 
 def score_kernel(kinds, c_ref, *refs):
-    probes, (own_ref, send_ref) = refs[:-2], refs[-2:]
+    probes, before, (own_ref, send_ref) = refs[: len(kinds)], refs[len(kinds) : -2], refs[-2:]
     me, plane = lax.axis_index("fsdp"), lax.axis_index("dp")
     cands = c_ref[...]
-    per = cands.shape[0] // 2
+    per, total = cands.shape[0] // 2, own_ref.shape[1]
     held = jnp.concatenate([ref[...] for ref in probes], axis=0)
     width = held.shape[0]
     mixed = dot_last(jnp.concatenate([cands, held], axis=0), held)
@@ -274,12 +274,18 @@
         return jnp.sum(jnp.where(rows == cols, square, 0.0), axis=axis, keepdims=True)
 
     rows = jnp.concatenate([scores, jnp.broadcast_to(diagonal(gram, 0), scores.shape)], axis=0)
-    group = lax.broadcasted_iota(jnp.int32, rows.shape, 1) // per
-    placed = jnp.zeros(rows.shape, jnp.float32)
+    group = lax.broadcasted_iota(jnp.int32, (rows.shape[0], total), 1) // per
+    placed = jnp.zeros(group.shape, jnp.float32)
     for g in range(width // per):
-        block = jnp.concatenate([rows[:, g * per : (g + 1) * per]] * (width // per), axis=1)
+        block = jnp.concatenate([rows[:, g * per : (g + 1) * per]] * (total // per), axis=1)
         placed = jnp.where(group == (partner(me, kinds[g // 2], plane) ^ (g % 2)), block, placed)
-    squares = jnp.broadcast_to(diagonal(dot_last(cands, cands), 1), (2 * per, width))
+    if before:
+        for i, (ref, held_ref) in enumerate(zip((own_ref, send_ref), before)):
+            ref[:per, :] = held_ref[:per, :] + placed[i * per : (i + 1) * per]
+            ref[per : 2 * per, :] = held_ref[per : 2 * per, :] + placed[2 * per : 3 * per]
+            ref[2 * per :, :] = held_ref[2 * per :, :]
+        return
+    squares = jnp.broadcast_to(diagonal(dot_last(cands, cands), 1), (2 * per, total))
     for i, ref in enumerate((own_ref, send_ref)):
         ref[:per, :] = placed[i * per : (i + 1) * per]
         ref[per : 2 * per, :] = placed[2 * per : 3 * per]
@@ -442,12 +448,17 @@
         scratch=scratch(total // 2),
     )
 
-    kinds = (0, 3, 2, 1)
-    got = [sw(p_side, 6), along(p_side, True), along(p_side, False)]
-    c_side, *got = lax.optimization_barrier((c_side, *got))
+    across, second_side, first_side = sw(p_side, 6), along(p_side, True), along(p_side, False)
     part = array(3 * examples, n * examples, dtype=f32)
+    shares = kernel(
+        functools.partial(score_kernel, (0, 3)), "first_shares", (part, part), (c_side, p_side, across)
+    )
+    *shares, second_side, first_side = lax.optimization_barrier((*shares, second_side, first_side))
     scores, to_other = kernel(
-        functools.partial(score_kernel, kinds), "score_shares", (part, part), (c_side, p_side, *got)
+        functools.partial(score_kernel, (2, 1)),
+        "score_shares",
+        (part, part),
+        (c_side, second_side, first_side, *shares),
     )
     scores = kernel(
         functools.partial(final_kernel, 2 * ks * kp),

time: 36 us -> 35.9 us (level)
    pallas_call x10 -> x11, Pallas kernels: 10 us -> 10.3 us  [kernel(): pl.pallas_call(f, out_shape=outs, in_specs=in_specs or [VMEM] * len(opera...]
where the time goes in v9:
time: 35.9 us; the launch traced here: 35.7 us
  starting transfers between devices  14.1 us (39%)
  waiting for transfers between devices  10.5 us (29%)
  Pallas kernels  10.3 us (29%)
  between operations  0.77 us (2%)
    pallas_call x11, Pallas kernels, kernel(): pl.pallas_call(f, out_shape=outs, in_specs=in_specs or [VMEM] * len(opera...  10.3 us
    ppermute x6, starting transfers between devices, along(): return lax.ppermute(x, ('fsdp', 'dp'), pairs)  8.14 us
    ppermute x10, waiting for transfers between devices, swap(): return lax.ppermute(x, axis, [(i, i ^ k) for i in range(size)])  6.36 us
    ppermute x10, starting transfers between devices, swap(): return lax.ppermute(x, axis, [(i, i ^ k) for i in range(size)])  5.97 us
    ppermute x6, waiting for transfers between devices, along(): return lax.ppermute(x, ('fsdp', 'dp'), pairs)  4.13 us
  transfers between devices with their start and end apart: 16, of which 9 were waited for; matrix products, arithmetic and copies ran while one was open for 0% of the time, Pallas kernels for 25%

profile of v9, /device:TPU:0, one launch (start us, length us, event | category | flops | bytes accessed | tf_op | source)
XLA Modules:
  0.0 35.7 jit_solution(3108972252009237392)
XLA Ops:
  0.6 3.0 %collective-permute-start.2 = (bf16[1024,256]{1,0:T(8,128)(2,1)}, bf16[1024,256]{1,0:T(8,128)(2,1)S(1)}, u32[]{:S(2)}, u32[]{:S(2)}) collective-permute-start(bf16[1024,256]{1,0:T(8,128)(2,1)} %in_hbm.1), channel_id=1, source_target_pairs={{0,8},{1,17},{2,10},{3,19},{4,20},{5,13},{6,22},{7,15},{8,0},{9,25... | collective-permute-start | bytes 1572872 | tf_op jit(solution)/shard_map/ppermute | solution.py:320
  3.6 2.7 %prepare.1 = (bf16[208,256]{1,0:T(8,128)(2,1)S(1)}, bf16[256,8192]{1,0:T(8,128)(2,1)S(1)}, bf16[256,1024]{1,0:T(8,128)(2,1)S(1)}, bf16[2,16,128]{2,1,0:T(8,128)(...) custom-call(bf16[1024,128]{1,0:T(8,128)(2,1)} %down_hbm.1, bf16[128,128]{1,0:T(8,128)(2,1)} %up_hbm.1, ...), custom_call_target="tpu_custom_call" | custom-call | flops 1 | bytes 1 | tf_op jit(solution)/shard_map/prepare/pallas_call | solution.py:326
  6.4 0.1 collective-permute-start.3
  6.5 0.5 %collective-permute-start.1 = (bf16[128,3584]{1,0:T(8,128)(2,1)S(1)}, bf16[128,3584]{1,0:T(8,128)(2,1)S(1)}, u32[]{:S(2)}, u32[]{:S(2)}) collective-permute-start(bf16[128,3584]{1,0:T(8,128)(2,1)S(1)} %get-tuple-element.35), channel_id=1, source_target_pairs={{0,4},{4,0},{8,12},{12,8},{16,20},{20,16},{24,28},{28,24},{1,5},{5... | collective-permute-start | bytes 2752520 | tf_op jit(solution)/shard_map/ppermute | solution.py:303
  7.0 2.2 %own_products.1 = (bf16[1024,256]{1,0:T(8,128)(2,1)S(1)}, bf16[720,256]{1,0:T(8,128)(2,1)S(1)}, f32[2,2,128,256]{3,2,1,0:T(8,128)S(1)}, f32[2,2,128,16]{3,2,1,0:T(8,128)S(1)}) custom-call(bf16[1024,256]{1,0:T(8,128)(2,1)} %in_hbm.1, bf16[208,256]{1,0:T(8,128)(2,1)S(1)} %get-tuple-element.36.extra.refs_0_, bf16[256,8192]{1,0:T(8,128)(2,1)S(1)} %get-tuple-element.31.x, ...), custom_call_target="tpu_custom_call" | custom-call | flops 1 | bytes 1 | tf_op jit(solution)/shard_map/own_products/pallas_call | solution.py:326
  9.2 2.0 %collective-permute-start.4 = (bf16[720,256]{1,0:T(8,128)(2,1)S(1)}, bf16[720,256]{1,0:T(8,128)(2,1)S(1)}, u32[]{:S(2)}, u32[]{:S(2)}) collective-permute-start(bf16[720,256]{1,0:T(8,128)(2,1)S(1)} %get-tuple-element.39), channel_id=1, source_target_pairs={{0,16},{1,9},{2,18},{3,11},{4,12},{5,21},{6,14},{7,23},{8,24},{9,1... | collective-permute-start | bytes 1105928 | tf_op jit(solution)/shard_map/ppermute | solution.py:320
  11.3 0.9 %collective-permute-done.3.refs_2_ = bf16[208,256]{1,0:T(8,128)(2,1)S(1)} collective-permute-done((bf16[208,256]{1,0:T(8,128)(2,1)S(1)}, bf16[208,256]{1,0:T(8,128)(2,1)S(1)}, u32[]{:S(2)}, u32[]{:S(2)}) %collective-permute-start.3) | collective-permute-done | bytes 106528 | tf_op jit(solution)/shard_map/ppermute | solution.py:320
  12.2 2.4 %collective-permute-start.6 = (bf16[1232,256]{1,0:T(8,128)(2,1)S(1)}, bf16[1232,256]{1,0:T(8,128)(2,1)S(1)}, u32[]{:S(2)}, u32[]{:S(2)}) collective-permute-start(bf16[1232,256]{1,0:T(8,128)(2,1)S(1)} %pad_maximum_fusion), channel_id=1, source_target_pairs={{0,16},{1,9},{2,18},{3,11},{4,12},{5,21},{6,14},{7,23},{8,24},{9,1... | collective-permute-start | bytes 1892360 | tf_op jit(solution)/shard_map/ppermute | solution.py:320
  14.6 1.6 %collective-permute-start.7 = (bf16[512,256]{1,0:T(8,128)(2,1)S(1)}, bf16[512,256]{1,0:T(8,128)(2,1)S(1)}, u32[]{:S(2)}, u32[]{:S(2)}) collective-permute-start(bf16[512,256]{1,0:T(8,128)(2,1)S(1)} %slice.9), channel_id=1, source_target_pairs={{0,1},{1,0},{2,3},{3,2},{4,5},{5,4},{6,7},{7,6},{8,9},{9,8},{10,11... | collective-permute-start | bytes 786440 | tf_op jit(solution)/shard_map/ppermute | solution.py:303
  16.2 0.6 %collective-permute-done.4.refs_3_ = bf16[720,256]{1,0:T(8,128)(2,1)S(1)} collective-permute-done((bf16[720,256]{1,0:T(8,128)(2,1)S(1)}, bf16[720,256]{1,0:T(8,128)(2,1)S(1)}, u32[]{:S(2)}, u32[]{:S(2)}) %collective-permute-start.4) | collective-permute-done | bytes 368672 | tf_op jit(solution)/shard_map/ppermute | solution.py:320
  16.8 0.1 collective-permute-start.5
  16.9 4.4 %collective-permute-done.7.refs_1_ = bf16[512,256]{1,0:T(8,128)(2,1)S(1)} collective-permute-done((bf16[512,256]{1,0:T(8,128)(2,1)S(1)}, bf16[512,256]{1,0:T(8,128)(2,1)S(1)}, u32[]{:S(2)}, u32[]{:S(2)}) %collective-permute-start.7) | collective-permute-done | bytes 262176 | tf_op jit(solution)/shard_map/ppermute | solution.py:303
  21.3 1.6 %early_products.1 = (f32[2,2,2,128,256]{4,3,2,1,0:T(8,128)S(1)}, f32[2,2,2,128,16]{4,3,2,1,0:T(8,128)S(1)}) custom-call(bf16[256,8192]{1,0:T(8,128)(2,1)S(1)} %get-tuple-element.31.x, bf16[256,1024]{1,0:T(8,128)(2,1)S(1)} %get-tuple-element.32.m, bf16[128,3584]{1,0:T(8,128)(2,1)S(1)} %collective-permute-done.c_xo.xo, ...), custom_call_target="tpu_custom_call" | custom-call | flops 1 | bytes 1 | tf_op jit(solution)/shard_map/early_products/pallas_call | solution.py:326
  23.0 0.6 %collective-permute-done.6.refs_0_ = bf16[1232,256]{1,0:T(8,128)(2,1)S(1)} collective-permute-done((bf16[1232,256]{1,0:T(8,128)(2,1)S(1)}, bf16[1232,256]{1,0:T(8,128)(2,1)S(1)}, u32[]{:S(2)}, u32[]{:S(2)}) %collective-permute-start.6) | collective-permute-done | bytes 630816 | tf_op jit(solution)/shard_map/ppermute | solution.py:320
  23.6 0.6 %probe_products.1 = (f32[256,256]{1,0:T(8,128)S(1)}, f32[16,256]{1,0:T(8,128)S(1)}, bf16[304,256]{1,0:T(8,128)(2,1)S(1)}) custom-call(bf16[256,8192]{1,0:T(8,128)(2,1)S(1)} %get-tuple-element.31.x, bf16[256,1024]{1,0:T(8,128)(2,1)S(1)} %get-tuple-element.32.m, bf16[128,3584]{1,0:T(8,128)(2,1)S(1)} %collective-permute-done.1.p_xo.xo, ...), custom_call_target="tpu_custom_call" | custom-call | flops 1 | bytes 1 | tf_op jit(solution)/shard_map/probe_products/pallas_call | solution.py:326
  24.3 0.6 %candidate_products.1 = (f32[256,256]{1,0:T(8,128)S(1)}, f32[16,256]{1,0:T(8,128)S(1)}, bf16[304,256]{1,0:T(8,128)(2,1)S(1)}) custom-call(bf16[256,8192]{1,0:T(8,128)(2,1)S(1)} %get-tuple-element.31.x, bf16[256,1024]{1,0:T(8,128)(2,1)S(1)} %get-tuple-element.32.m, bf16[128,3584]{1,0:T(8,128)(2,1)S(1)} %collective-permute-done.c_xo.xo, ...), custom_call_target="tpu_custom_call" | custom-call | flops 1 | bytes 1 | tf_op jit(solution)/shard_map/candidate_products/pallas_call | solution.py:326
  24.9 0.6 %collective-permute-start.9 = (bf16[304,256]{1,0:T(8,128)(2,1)S(1)}, bf16[304,256]{1,0:T(8,128)(2,1)S(1)}, u32[]{:S(2)}, u32[]{:S(2)}) collective-permute-start(bf16[304,256]{1,0:T(8,128)(2,1)S(1)} %get-tuple-element.45), channel_id=1, source_target_pairs={{0,4},{4,0},{8,12},{12,8},{16,20},{20,16},{24,28},{28,24},{1,5},{5... | collective-permute-start | bytes 466952 | tf_op jit(solution)/shard_map/ppermute | solution.py:303
  25.4 0.2 collective-permute-done.10.got
  25.6 0.2 probe_sides.1.refs_0_
  25.9 3.0 %collective-permute-start.11 = (bf16[8,4096]{1,0:T(8,128)(2,1)S(1)}, bf16[8,4096]{1,0:T(8,128)(2,1)S(1)}, u32[]{:S(2)}, u32[]{:S(2)}) collective-permute-start(bf16[8,4096]{1,0:T(8,128)(2,1)S(1)} %probe_sides.1.refs_0_), channel_id=1, source_target_pairs={{0,24},{4,28},{8,16},{12,20},{16,8},{20,12},{24,0},{28,4},{1,25},{... | collective-permute-start | bytes 196616 | tf_op jit(solution)/shard_map/ppermute | solution.py:303
  28.8 0.5 %collective-permute-start.12 = (bf16[8,4096]{1,0:T(8,128)(2,1)S(1)}, bf16[8,4096]{1,0:T(8,128)(2,1)S(1)}, u32[]{:S(2)}, u32[]{:S(2)}) collective-permute-start(bf16[8,4096]{1,0:T(8,128)(2,1)S(1)} %probe_sides.1.refs_0_), channel_id=1, source_target_pairs={{0,16},{1,9},{2,18},{3,11},{4,12},{5,21},{6,14},{7,23},{8,24},{9,1... | collective-permute-start | bytes 196616 | tf_op jit(solution)/shard_map/ppermute | solution.py:320
  29.3 0.1 collective-permute-start.13
  29.5 0.2 candidate_sides.1
  29.7 0.1 collective-permute-start.15
  29.8 1.4 %collective-permute-done.11.refs_1_ = bf16[8,4096]{1,0:T(8,128)(2,1)S(1)} collective-permute-done((bf16[8,4096]{1,0:T(8,128)(2,1)S(1)}, bf16[8,4096]{1,0:T(8,128)(2,1)S(1)}, u32[]{:S(2)}, u32[]{:S(2)}) %collective-permute-start.11) | collective-permute-done | bytes 65568 | tf_op jit(solution)/shard_map/ppermute | solution.py:303
  31.2 0.4 first_shares.1
  31.6 1.5 %collective-permute-done.12.refs_0_ = bf16[8,4096]{1,0:T(8,128)(2,1)S(1)} collective-permute-done((bf16[8,4096]{1,0:T(8,128)(2,1)S(1)}, bf16[8,4096]{1,0:T(8,128)(2,1)S(1)}, u32[]{:S(2)}, u32[]{:S(2)}) %collective-permute-start.12) | collective-permute-done | bytes 65568 | tf_op jit(solution)/shard_map/ppermute | solution.py:320
  33.1 0.5 %collective-permute-done.13.refs_1_ = bf16[8,4096]{1,0:T(8,128)(2,1)S(1)} collective-permute-done((bf16[8,4096]{1,0:T(8,128)(2,1)S(1)}, bf16[8,4096]{1,0:T(8,128)(2,1)S(1)}, u32[]{:S(2)}, u32[]{:S(2)}) %collective-permute-start.13) | collective-permute-done | bytes 65568 | tf_op jit(solution)/shard_map/ppermute | solution.py:320
  33.6 0.3 score_shares.1
  34.0 0.8 %candidate_features.1 = bf16[4,8192]{1,0:T(4,128)(2,1)} custom-call(f32[64,256]{1,0:T(8,128)S(1)} %get-tuple-element.58.own, f32[64,256]{1,0:T(8,128)S(1)} %collective-permute-done.15.got), custom_call_target="tpu_custom_call" | custom-call | flops 1 | bytes 1 | tf_op jit(solution)/shard_map/candidate_features/pallas_call | solution.py:326
  34.8 0.3 collective-permute-done.14.got
  35.1 0.6 %scores.1 = f32[4,32]{1,0:T(4,128)} custom-call(f32[12,32]{1,0:T(8,128)S(1)} %get-tuple-element.56.own, f32[12,32]{1,0:T(8,128)S(1)} %collective-permute-done.14.got), custom_call_target="tpu_custom_call" | custom-call | flops 1 | bytes 1 | tf_op jit(solution)/shard_map/scores/pallas_call | solution.py:326
  (14 shorter events, 0.3 us)
Async XLA Ops:
  0.6 11.5 %collective-permute-start.2 = (bf16[1024,256]{1,0:T(8,128)(2,1)}, bf16[1024,256]{1,0:T(8,128)(2,1)S(1)}, u32[]{:S(2)}, u32[]{:S(2)}) collective-permute-start(bf16[1024,256]{1,0:T(8,128)(2,1)} %in_hbm.1), channel_id=1, source_target_pairs={{0,8},{1,17},{2,10},{3,19},{4,20},{5,13},{6,22},{7,15},{8,0},{9,25... | collective-permute-start | bytes 1572872 | tf_op jit(solution)/shard_map/ppermute | solution.py:320
  6.4 5.8 %collective-permute-start.3 = (bf16[208,256]{1,0:T(8,128)(2,1)S(1)}, bf16[208,256]{1,0:T(8,128)(2,1)S(1)}, u32[]{:S(2)}, u32[]{:S(2)}) collective-permute-start(bf16[208,256]{1,0:T(8,128)(2,1)S(1)} %get-tuple-element.36.extra.refs_0_), channel_id=1, source_target_pairs={{0,8},{1,17},{2,10},{3,19},{4,20},{5,13},{6,22},{7,15},{8,0},{9,25... | collective-permute-start | bytes 319496 | tf_op jit(solution)/shard_map/ppermute | solution.py:320
  6.5 14.8 %collective-permute-start = (bf16[128,3584]{1,0:T(8,128)(2,1)S(1)}, bf16[128,3584]{1,0:T(8,128)(2,1)S(1)}, u32[]{:S(2)}, u32[]{:S(2)}) collective-permute-start(bf16[128,3584]{1,0:T(8,128)(2,1)S(1)} %get-tuple-element.33), channel_id=1, source_target_pairs={{0,4},{4,0},{8,12},{12,8},{16,20},{20,16},{24,28},{28,24},{1,5},{5... | collective-permute-start | bytes 2752520 | tf_op jit(solution)/shard_map/ppermute | solution.py:303
  6.5 14.8 %collective-permute-start.1 = (bf16[128,3584]{1,0:T(8,128)(2,1)S(1)}, bf16[128,3584]{1,0:T(8,128)(2,1)S(1)}, u32[]{:S(2)}, u32[]{:S(2)}) collective-permute-start(bf16[128,3584]{1,0:T(8,128)(2,1)S(1)} %get-tuple-element.35), channel_id=1, source_target_pairs={{0,4},{4,0},{8,12},{12,8},{16,20},{20,16},{24,28},{28,24},{1,5},{5... | collective-permute-start | bytes 2752520 | tf_op jit(solution)/shard_map/ppermute | solution.py:303
  9.2 7.6 %collective-permute-start.4 = (bf16[720,256]{1,0:T(8,128)(2,1)S(1)}, bf16[720,256]{1,0:T(8,128)(2,1)S(1)}, u32[]{:S(2)}, u32[]{:S(2)}) collective-permute-start(bf16[720,256]{1,0:T(8,128)(2,1)S(1)} %get-tuple-element.39), channel_id=1, source_target_pairs={{0,16},{1,9},{2,18},{3,11},{4,12},{5,21},{6,14},{7,23},{8,24},{9,1... | collective-permute-start | bytes 1105928 | tf_op jit(solution)/shard_map/ppermute | solution.py:320
  12.2 11.4 %collective-permute-start.6 = (bf16[1232,256]{1,0:T(8,128)(2,1)S(1)}, bf16[1232,256]{1,0:T(8,128)(2,1)S(1)}, u32[]{:S(2)}, u32[]{:S(2)}) collective-permute-start(bf16[1232,256]{1,0:T(8,128)(2,1)S(1)} %pad_maximum_fusion), channel_id=1, source_target_pairs={{0,16},{1,9},{2,18},{3,11},{4,12},{5,21},{6,14},{7,23},{8,24},{9,1... | collective-permute-start | bytes 1892360 | tf_op jit(solution)/shard_map/ppermute | solution.py:320
  14.6 6.7 %collective-permute-start.7 = (bf16[512,256]{1,0:T(8,128)(2,1)S(1)}, bf16[512,256]{1,0:T(8,128)(2,1)S(1)}, u32[]{:S(2)}, u32[]{:S(2)}) collective-permute-start(bf16[512,256]{1,0:T(8,128)(2,1)S(1)} %slice.9), channel_id=1, source_target_pairs={{0,1},{1,0},{2,3},{3,2},{4,5},{5,4},{6,7},{7,6},{8,9},{9,8},{10,11... | collective-permute-start | bytes 786440 | tf_op jit(solution)/shard_map/ppermute | solution.py:303
  16.8 4.4 %collective-permute-start.5 = (bf16[592,256]{1,0:T(8,128)(2,1)S(1)}, bf16[592,256]{1,0:T(8,128)(2,1)S(1)}, u32[]{:S(2)}, u32[]{:S(2)}) collective-permute-start(bf16[592,256]{1,0:T(8,128)(2,1)S(1)} %slice.8), channel_id=1, source_target_pairs={{0,4},{4,0},{8,12},{12,8},{16,20},{20,16},{24,28},{28,24},{1,5},{5... | collective-permute-start | bytes 909320 | tf_op jit(solution)/shard_map/ppermute | solution.py:303
  21.3 1.7 %collective-permute-start.8 = (bf16[512,256]{1,0:T(8,128)(2,1)S(1)}, bf16[512,256]{1,0:T(8,128)(2,1)S(1)}, u32[]{:S(2)}, u32[]{:S(2)}) collective-permute-start(bf16[512,256]{1,0:T(8,128)(2,1)S(1)} %collective-permute-done.7.refs_1_), channel_id=1, source_target_pairs={{0,4},{4,0},{8,12},{12,8},{16,20},{20,16},{24,28},{28,24},{1,5},{5... | collective-permute-start | bytes 786440 | tf_op jit(solution)/shard_map/ppermute | solution.py:303
  24.2 1.4 %collective-permute-start.10 = (bf16[304,256]{1,0:T(8,128)(2,1)S(1)}, bf16[304,256]{1,0:T(8,128)(2,1)S(1)}, u32[]{:S(2)}, u32[]{:S(2)}) collective-permute-start(bf16[304,256]{1,0:T(8,128)(2,1)S(1)} %get-tuple-element.49), channel_id=1, source_target_pairs={{0,4},{4,0},{8,12},{12,8},{16,20},{20,16},{24,28},{28,24},{1,5},{5... | collective-permute-start | bytes 466952 | tf_op jit(solution)/shard_map/ppermute | solution.py:303
  24.9 4.6 %collective-permute-start.9 = (bf16[304,256]{1,0:T(8,128)(2,1)S(1)}, bf16[304,256]{1,0:T(8,128)(2,1)S(1)}, u32[]{:S(2)}, u32[]{:S(2)}) collective-permute-start(bf16[304,256]{1,0:T(8,128)(2,1)S(1)} %get-tuple-element.45), channel_id=1, source_target_pairs={{0,4},{4,0},{8,12},{12,8},{16,20},{20,16},{24,28},{28,24},{1,5},{5... | collective-permute-start | bytes 466952 | tf_op jit(solution)/shard_map/ppermute | solution.py:303
  25.9 5.4 %collective-permute-start.11 = (bf16[8,4096]{1,0:T(8,128)(2,1)S(1)}, bf16[8,4096]{1,0:T(8,128)(2,1)S(1)}, u32[]{:S(2)}, u32[]{:S(2)}) collective-permute-start(bf16[8,4096]{1,0:T(8,128)(2,1)S(1)} %probe_sides.1.refs_0_), channel_id=1, source_target_pairs={{0,24},{4,28},{8,16},{12,20},{16,8},{20,12},{24,0},{28,4},{1,25},{... | collective-permute-start | bytes 196616 | tf_op jit(solution)/shard_map/ppermute | solution.py:303
  28.8 4.3 %collective-permute-start.12 = (bf16[8,4096]{1,0:T(8,128)(2,1)S(1)}, bf16[8,4096]{1,0:T(8,128)(2,1)S(1)}, u32[]{:S(2)}, u32[]{:S(2)}) collective-permute-start(bf16[8,4096]{1,0:T(8,128)(2,1)S(1)} %probe_sides.1.refs_0_), channel_id=1, source_target_pairs={{0,16},{1,9},{2,18},{3,11},{4,12},{5,21},{6,14},{7,23},{8,24},{9,1... | collective-permute-start | bytes 196616 | tf_op jit(solution)/shard_map/ppermute | solution.py:320
  29.3 4.3 %collective-permute-start.13 = (bf16[8,4096]{1,0:T(8,128)(2,1)S(1)}, bf16[8,4096]{1,0:T(8,128)(2,1)S(1)}, u32[]{:S(2)}, u32[]{:S(2)}) collective-permute-start(bf16[8,4096]{1,0:T(8,128)(2,1)S(1)} %probe_sides.1.refs_0_), channel_id=1, source_target_pairs={{0,8},{1,17},{2,10},{3,19},{4,20},{5,13},{6,22},{7,15},{8,0},{9,25... | collective-permute-start | bytes 196616 | tf_op jit(solution)/shard_map/ppermute | solution.py:320
  29.7 4.3 %collective-permute-start.15 = (f32[64,256]{1,0:T(8,128)S(1)}, f32[64,256]{1,0:T(8,128)S(1)}, u32[]{:S(2)}, u32[]{:S(2)}) collective-permute-start(f32[64,256]{1,0:T(8,128)S(1)} %get-tuple-element.59), channel_id=1, source_target_pairs={{0,4},{4,0},{8,12},{12,8},{16,20},{20,16},{24,28},{28,24},{1,5},{5... | collective-permute-start | bytes 196616 | tf_op jit(solution)/shard_map/ppermute | solution.py:303
  33.9 1.2 %collective-permute-start.14 = (f32[12,32]{1,0:T(8,128)S(1)}, f32[12,32]{1,0:T(8,128)S(1)}, u32[]{:S(2)}, u32[]{:S(2)}) collective-permute-start(f32[12,32]{1,0:T(8,128)S(1)} %get-tuple-element.57), channel_id=1, source_target_pairs={{0,4},{4,0},{8,12},{12,8},{16,20},{20,16},{24,28},{28,24},{1,5},{5... | collective-permute-start | bytes 4616 | tf_op jit(solution)/shard_map/ppermute | solution.py:303

commit v10 on v9

--- a/solution.py
+++ b/solution.py
@@ -387,7 +387,7 @@
 
     first, first_extra = along(sketch_in, False), along(extra, False)
     second = along(second, True)
-    c_xo, p_xo = sw(c_cols, 1), sw(p_cols, 1)
+    p_xo, c_xo = sw(p_cols, 1), sw(c_cols, 1)
 
     more = along(jnp.concatenate([first, first_extra]), True)
     rest = swap(first[:beside], 1, "dp", planes)

time: 35.9 us -> 35.9 us (level)
  no operation moved by 1% of the time
where the time goes in v10:
time: 35.9 us; the launch traced here: 35.7 us
  starting transfers between devices  14.1 us (39%)
  waiting for transfers between devices  10.5 us (29%)
  Pallas kernels  10.3 us (29%)
  between operations  0.77 us (2%)
    pallas_call x11, Pallas kernels, kernel(): pl.pallas_call(f, out_shape=outs, in_specs=in_specs or [VMEM] * len(opera...  10.3 us
    ppermute x6, starting transfers between devices, along(): return lax.ppermute(x, ('fsdp', 'dp'), pairs)  8.14 us
    ppermute x10, waiting for transfers between devices, swap(): return lax.ppermute(x, axis, [(i, i ^ k) for i in range(size)])  6.36 us
    ppermute x10, starting transfers between devices, swap(): return lax.ppermute(x, axis, [(i, i ^ k) for i in range(size)])  5.97 us
    ppermute x6, waiting for transfers between devices, along(): return lax.ppermute(x, ('fsdp', 'dp'), pairs)  4.13 us
  transfers between devices with their start and end apart: 16, of which 9 were waited for; matrix products, arithmetic and copies ran while one was open for 0% of the time, Pallas kernels for 25%

profile of v10, /device:TPU:0, one launch (start us, length us, event | category | flops | bytes accessed | tf_op | source)
XLA Modules:
  0.0 35.7 jit_solution(3108972252009237392)
XLA Ops:
  0.6 3.0 %collective-permute-start.2 = (bf16[1024,256]{1,0:T(8,128)(2,1)}, bf16[1024,256]{1,0:T(8,128)(2,1)S(1)}, u32[]{:S(2)}, u32[]{:S(2)}) collective-permute-start(bf16[1024,256]{1,0:T(8,128)(2,1)} %in_hbm.1), channel_id=1, source_target_pairs={{0,8},{1,17},{2,10},{3,19},{4,20},{5,13},{6,22},{7,15},{8,0},{9,25... | collective-permute-start | bytes 1572872 | tf_op jit(solution)/shard_map/ppermute | solution.py:320
  3.6 2.7 %prepare.1 = (bf16[208,256]{1,0:T(8,128)(2,1)S(1)}, bf16[256,8192]{1,0:T(8,128)(2,1)S(1)}, bf16[256,1024]{1,0:T(8,128)(2,1)S(1)}, bf16[2,16,128]{2,1,0:T(8,128)(...) custom-call(bf16[1024,128]{1,0:T(8,128)(2,1)} %down_hbm.1, bf16[128,128]{1,0:T(8,128)(2,1)} %up_hbm.1, ...), custom_call_target="tpu_custom_call" | custom-call | flops 1 | bytes 1 | tf_op jit(solution)/shard_map/prepare/pallas_call | solution.py:326
  6.4 0.1 collective-permute-start.3
  6.5 0.5 %collective-permute-start.1 = (bf16[128,3584]{1,0:T(8,128)(2,1)S(1)}, bf16[128,3584]{1,0:T(8,128)(2,1)S(1)}, u32[]{:S(2)}, u32[]{:S(2)}) collective-permute-start(bf16[128,3584]{1,0:T(8,128)(2,1)S(1)} %get-tuple-element.35), channel_id=1, source_target_pairs={{0,4},{4,0},{8,12},{12,8},{16,20},{20,16},{24,28},{28,24},{1,5},{5... | collective-permute-start | bytes 2752520 | tf_op jit(solution)/shard_map/ppermute | solution.py:303
  7.0 2.2 %own_products.1 = (bf16[1024,256]{1,0:T(8,128)(2,1)S(1)}, bf16[720,256]{1,0:T(8,128)(2,1)S(1)}, f32[2,2,128,256]{3,2,1,0:T(8,128)S(1)}, f32[2,2,128,16]{3,2,1,0:T(8,128)S(1)}) custom-call(bf16[1024,256]{1,0:T(8,128)(2,1)} %in_hbm.1, bf16[208,256]{1,0:T(8,128)(2,1)S(1)} %get-tuple-element.36.extra.refs_0_, bf16[256,8192]{1,0:T(8,128)(2,1)S(1)} %get-tuple-element.31.x, ...), custom_call_target="tpu_custom_call" | custom-call | flops 1 | bytes 1 | tf_op jit(solution)/shard_map/own_products/pallas_call | solution.py:326
  9.2 2.0 %collective-permute-start.4 = (bf16[720,256]{1,0:T(8,128)(2,1)S(1)}, bf16[720,256]{1,0:T(8,128)(2,1)S(1)}, u32[]{:S(2)}, u32[]{:S(2)}) collective-permute-start(bf16[720,256]{1,0:T(8,128)(2,1)S(1)} %get-tuple-element.39), channel_id=1, source_target_pairs={{0,16},{1,9},{2,18},{3,11},{4,12},{5,21},{6,14},{7,23},{8,24},{9,1... | collective-permute-start | bytes 1105928 | tf_op jit(solution)/shard_map/ppermute | solution.py:320
  11.3 0.9 %collective-permute-done.3.refs_2_ = bf16[208,256]{1,0:T(8,128)(2,1)S(1)} collective-permute-done((bf16[208,256]{1,0:T(8,128)(2,1)S(1)}, bf16[208,256]{1,0:T(8,128)(2,1)S(1)}, u32[]{:S(2)}, u32[]{:S(2)}) %collective-permute-start.3) | collective-permute-done | bytes 106528 | tf_op jit(solution)/shard_map/ppermute | solution.py:320
  12.2 2.4 %collective-permute-start.6 = (bf16[1232,256]{1,0:T(8,128)(2,1)S(1)}, bf16[1232,256]{1,0:T(8,128)(2,1)S(1)}, u32[]{:S(2)}, u32[]{:S(2)}) collective-permute-start(bf16[1232,256]{1,0:T(8,128)(2,1)S(1)} %pad_maximum_fusion), channel_id=1, source_target_pairs={{0,16},{1,9},{2,18},{3,11},{4,12},{5,21},{6,14},{7,23},{8,24},{9,1... | collective-permute-start | bytes 1892360 | tf_op jit(solution)/shard_map/ppermute | solution.py:320
  14.6 1.6 %collective-permute-start.7 = (bf16[512,256]{1,0:T(8,128)(2,1)S(1)}, bf16[512,256]{1,0:T(8,128)(2,1)S(1)}, u32[]{:S(2)}, u32[]{:S(2)}) collective-permute-start(bf16[512,256]{1,0:T(8,128)(2,1)S(1)} %slice.9), channel_id=1, source_target_pairs={{0,1},{1,0},{2,3},{3,2},{4,5},{5,4},{6,7},{7,6},{8,9},{9,8},{10,11... | collective-permute-start | bytes 786440 | tf_op jit(solution)/shard_map/ppermute | solution.py:303
  16.2 0.6 %collective-permute-done.4.refs_3_ = bf16[720,256]{1,0:T(8,128)(2,1)S(1)} collective-permute-done((bf16[720,256]{1,0:T(8,128)(2,1)S(1)}, bf16[720,256]{1,0:T(8,128)(2,1)S(1)}, u32[]{:S(2)}, u32[]{:S(2)}) %collective-permute-start.4) | collective-permute-done | bytes 368672 | tf_op jit(solution)/shard_map/ppermute | solution.py:320
  16.8 0.1 collective-permute-start.5
  16.9 4.4 %collective-permute-done.7.refs_1_ = bf16[512,256]{1,0:T(8,128)(2,1)S(1)} collective-permute-done((bf16[512,256]{1,0:T(8,128)(2,1)S(1)}, bf16[512,256]{1,0:T(8,128)(2,1)S(1)}, u32[]{:S(2)}, u32[]{:S(2)}) %collective-permute-start.7) | collective-permute-done | bytes 262176 | tf_op jit(solution)/shard_map/ppermute | solution.py:303
  21.3 1.6 %early_products.1 = (f32[2,2,2,128,256]{4,3,2,1,0:T(8,128)S(1)}, f32[2,2,2,128,16]{4,3,2,1,0:T(8,128)S(1)}) custom-call(bf16[256,8192]{1,0:T(8,128)(2,1)S(1)} %get-tuple-element.31.x, bf16[256,1024]{1,0:T(8,128)(2,1)S(1)} %get-tuple-element.32.m, bf16[128,3584]{1,0:T(8,128)(2,1)S(1)} %collective-permute-done.c_xo.xo, ...), custom_call_target="tpu_custom_call" | custom-call | flops 1 | bytes 1 | tf_op jit(solution)/shard_map/early_products/pallas_call | solution.py:326
  23.0 0.6 %collective-permute-done.6.refs_0_ = bf16[1232,256]{1,0:T(8,128)(2,1)S(1)} collective-permute-done((bf16[1232,256]{1,0:T(8,128)(2,1)S(1)}, bf16[1232,256]{1,0:T(8,128)(2,1)S(1)}, u32[]{:S(2)}, u32[]{:S(2)}) %collective-permute-start.6) | collective-permute-done | bytes 630816 | tf_op jit(solution)/shard_map/ppermute | solution.py:320
  23.6 0.6 %probe_products.1 = (f32[256,256]{1,0:T(8,128)S(1)}, f32[16,256]{1,0:T(8,128)S(1)}, bf16[304,256]{1,0:T(8,128)(2,1)S(1)}) custom-call(bf16[256,8192]{1,0:T(8,128)(2,1)S(1)} %get-tuple-element.31.x, bf16[256,1024]{1,0:T(8,128)(2,1)S(1)} %get-tuple-element.32.m, bf16[128,3584]{1,0:T(8,128)(2,1)S(1)} %collective-permute-done.1.p_xo.xo, ...), custom_call_target="tpu_custom_call" | custom-call | flops 1 | bytes 1 | tf_op jit(solution)/shard_map/probe_products/pallas_call | solution.py:326
  24.3 0.6 %candidate_products.1 = (f32[256,256]{1,0:T(8,128)S(1)}, f32[16,256]{1,0:T(8,128)S(1)}, bf16[304,256]{1,0:T(8,128)(2,1)S(1)}) custom-call(bf16[256,8192]{1,0:T(8,128)(2,1)S(1)} %get-tuple-element.31.x, bf16[256,1024]{1,0:T(8,128)(2,1)S(1)} %get-tuple-element.32.m, bf16[128,3584]{1,0:T(8,128)(2,1)S(1)} %collective-permute-done.c_xo.xo, ...), custom_call_target="tpu_custom_call" | custom-call | flops 1 | bytes 1 | tf_op jit(solution)/shard_map/candidate_products/pallas_call | solution.py:326
  24.9 0.6 %collective-permute-start.9 = (bf16[304,256]{1,0:T(8,128)(2,1)S(1)}, bf16[304,256]{1,0:T(8,128)(2,1)S(1)}, u32[]{:S(2)}, u32[]{:S(2)}) collective-permute-start(bf16[304,256]{1,0:T(8,128)(2,1)S(1)} %get-tuple-element.45), channel_id=1, source_target_pairs={{0,4},{4,0},{8,12},{12,8},{16,20},{20,16},{24,28},{28,24},{1,5},{5... | collective-permute-start | bytes 466952 | tf_op jit(solution)/shard_map/ppermute | solution.py:303
  25.4 0.2 collective-permute-done.10.got
  25.6 0.2 probe_sides.1.refs_0_
  25.9 3.0 %collective-permute-start.11 = (bf16[8,4096]{1,0:T(8,128)(2,1)S(1)}, bf16[8,4096]{1,0:T(8,128)(2,1)S(1)}, u32[]{:S(2)}, u32[]{:S(2)}) collective-permute-start(bf16[8,4096]{1,0:T(8,128)(2,1)S(1)} %probe_sides.1.refs_0_), channel_id=1, source_target_pairs={{0,24},{4,28},{8,16},{12,20},{16,8},{20,12},{24,0},{28,4},{1,25},{... | collective-permute-start | bytes 196616 | tf_op jit(solution)/shard_map/ppermute | solution.py:303
  28.8 0.5 %collective-permute-start.12 = (bf16[8,4096]{1,0:T(8,128)(2,1)S(1)}, bf16[8,4096]{1,0:T(8,128)(2,1)S(1)}, u32[]{:S(2)}, u32[]{:S(2)}) collective-permute-start(bf16[8,4096]{1,0:T(8,128)(2,1)S(1)} %probe_sides.1.refs_0_), channel_id=1, source_target_pairs={{0,16},{1,9},{2,18},{3,11},{4,12},{5,21},{6,14},{7,23},{8,24},{9,1... | collective-permute-start | bytes 196616 | tf_op jit(solution)/shard_map/ppermute | solution.py:320
  29.3 0.1 collective-permute-start.13
  29.5 0.2 candidate_sides.1
  29.7 0.1 collective-permute-start.15
  29.8 1.4 %collective-permute-done.11.refs_1_ = bf16[8,4096]{1,0:T(8,128)(2,1)S(1)} collective-permute-done((bf16[8,4096]{1,0:T(8,128)(2,1)S(1)}, bf16[8,4096]{1,0:T(8,128)(2,1)S(1)}, u32[]{:S(2)}, u32[]{:S(2)}) %collective-permute-start.11) | collective-permute-done | bytes 65568 | tf_op jit(solution)/shard_map/ppermute | solution.py:303
  31.2 0.4 first_shares.1
  31.6 1.5 %collective-permute-done.12.refs_0_ = bf16[8,4096]{1,0:T(8,128)(2,1)S(1)} collective-permute-done((bf16[8,4096]{1,0:T(8,128)(2,1)S(1)}, bf16[8,4096]{1,0:T(8,128)(2,1)S(1)}, u32[]{:S(2)}, u32[]{:S(2)}) %collective-permute-start.12) | collective-permute-done | bytes 65568 | tf_op jit(solution)/shard_map/ppermute | solution.py:320
  33.1 0.5 %collective-permute-done.13.refs_1_ = bf16[8,4096]{1,0:T(8,128)(2,1)S(1)} collective-permute-done((bf16[8,4096]{1,0:T(8,128)(2,1)S(1)}, bf16[8,4096]{1,0:T(8,128)(2,1)S(1)}, u32[]{:S(2)}, u32[]{:S(2)}) %collective-permute-start.13) | collective-permute-done | bytes 65568 | tf_op jit(solution)/shard_map/ppermute | solution.py:320
  33.6 0.3 score_shares.1
  34.0 0.8 %candidate_features.1 = bf16[4,8192]{1,0:T(4,128)(2,1)} custom-call(f32[64,256]{1,0:T(8,128)S(1)} %get-tuple-element.58.own, f32[64,256]{1,0:T(8,128)S(1)} %collective-permute-done.15.got), custom_call_target="tpu_custom_call" | custom-call | flops 1 | bytes 1 | tf_op jit(solution)/shard_map/candidate_features/pallas_call | solution.py:326
  34.8 0.3 collective-permute-done.14.got
  35.1 0.6 %scores.1 = f32[4,32]{1,0:T(4,128)} custom-call(f32[12,32]{1,0:T(8,128)S(1)} %get-tuple-element.56.own, f32[12,32]{1,0:T(8,128)S(1)} %collective-permute-done.14.got), custom_call_target="tpu_custom_call" | custom-call | flops 1 | bytes 1 | tf_op jit(solution)/shard_map/scores/pallas_call | solution.py:326
  (14 shorter events, 0.3 us)
Async XLA Ops:
  0.6 11.5 %collective-permute-start.2 = (bf16[1024,256]{1,0:T(8,128)(2,1)}, bf16[1024,256]{1,0:T(8,128)(2,1)S(1)}, u32[]{:S(2)}, u32[]{:S(2)}) collective-permute-start(bf16[1024,256]{1,0:T(8,128)(2,1)} %in_hbm.1), channel_id=1, source_target_pairs={{0,8},{1,17},{2,10},{3,19},{4,20},{5,13},{6,22},{7,15},{8,0},{9,25... | collective-permute-start | bytes 1572872 | tf_op jit(solution)/shard_map/ppermute | solution.py:320
  6.4 5.8 %collective-permute-start.3 = (bf16[208,256]{1,0:T(8,128)(2,1)S(1)}, bf16[208,256]{1,0:T(8,128)(2,1)S(1)}, u32[]{:S(2)}, u32[]{:S(2)}) collective-permute-start(bf16[208,256]{1,0:T(8,128)(2,1)S(1)} %get-tuple-element.36.extra.refs_0_), channel_id=1, source_target_pairs={{0,8},{1,17},{2,10},{3,19},{4,20},{5,13},{6,22},{7,15},{8,0},{9,25... | collective-permute-start | bytes 319496 | tf_op jit(solution)/shard_map/ppermute | solution.py:320
  6.5 14.8 %collective-permute-start = (bf16[128,3584]{1,0:T(8,128)(2,1)S(1)}, bf16[128,3584]{1,0:T(8,128)(2,1)S(1)}, u32[]{:S(2)}, u32[]{:S(2)}) collective-permute-start(bf16[128,3584]{1,0:T(8,128)(2,1)S(1)} %get-tuple-element.33), channel_id=1, source_target_pairs={{0,4},{4,0},{8,12},{12,8},{16,20},{20,16},{24,28},{28,24},{1,5},{5... | collective-permute-start | bytes 2752520 | tf_op jit(solution)/shard_map/ppermute | solution.py:303
  6.5 14.8 %collective-permute-start.1 = (bf16[128,3584]{1,0:T(8,128)(2,1)S(1)}, bf16[128,3584]{1,0:T(8,128)(2,1)S(1)}, u32[]{:S(2)}, u32[]{:S(2)}) collective-permute-start(bf16[128,3584]{1,0:T(8,128)(2,1)S(1)} %get-tuple-element.35), channel_id=1, source_target_pairs={{0,4},{4,0},{8,12},{12,8},{16,20},{20,16},{24,28},{28,24},{1,5},{5... | collective-permute-start | bytes 2752520 | tf_op jit(solution)/shard_map/ppermute | solution.py:303
  9.2 7.6 %collective-permute-start.4 = (bf16[720,256]{1,0:T(8,128)(2,1)S(1)}, bf16[720,256]{1,0:T(8,128)(2,1)S(1)}, u32[]{:S(2)}, u32[]{:S(2)}) collective-permute-start(bf16[720,256]{1,0:T(8,128)(2,1)S(1)} %get-tuple-element.39), channel_id=1, source_target_pairs={{0,16},{1,9},{2,18},{3,11},{4,12},{5,21},{6,14},{7,23},{8,24},{9,1... | collective-permute-start | bytes 1105928 | tf_op jit(solution)/shard_map/ppermute | solution.py:320
  12.2 11.4 %collective-permute-start.6 = (bf16[1232,256]{1,0:T(8,128)(2,1)S(1)}, bf16[1232,256]{1,0:T(8,128)(2,1)S(1)}, u32[]{:S(2)}, u32[]{:S(2)}) collective-permute-start(bf16[1232,256]{1,0:T(8,128)(2,1)S(1)} %pad_maximum_fusion), channel_id=1, source_target_pairs={{0,16},{1,9},{2,18},{3,11},{4,12},{5,21},{6,14},{7,23},{8,24},{9,1... | collective-permute-start | bytes 1892360 | tf_op jit(solution)/shard_map/ppermute | solution.py:320
  14.6 6.7 %collective-permute-start.7 = (bf16[512,256]{1,0:T(8,128)(2,1)S(1)}, bf16[512,256]{1,0:T(8,128)(2,1)S(1)}, u32[]{:S(2)}, u32[]{:S(2)}) collective-permute-start(bf16[512,256]{1,0:T(8,128)(2,1)S(1)} %slice.9), channel_id=1, source_target_pairs={{0,1},{1,0},{2,3},{3,2},{4,5},{5,4},{6,7},{7,6},{8,9},{9,8},{10,11... | collective-permute-start | bytes 786440 | tf_op jit(solution)/shard_map/ppermute | solution.py:303
  16.8 4.4 %collective-permute-start.5 = (bf16[592,256]{1,0:T(8,128)(2,1)S(1)}, bf16[592,256]{1,0:T(8,128)(2,1)S(1)}, u32[]{:S(2)}, u32[]{:S(2)}) collective-permute-start(bf16[592,256]{1,0:T(8,128)(2,1)S(1)} %slice.8), channel_id=1, source_target_pairs={{0,4},{4,0},{8,12},{12,8},{16,20},{20,16},{24,28},{28,24},{1,5},{5... | collective-permute-start | bytes 909320 | tf_op jit(solution)/shard_map/ppermute | solution.py:303
  21.3 1.7 %collective-permute-start.8 = (bf16[512,256]{1,0:T(8,128)(2,1)S(1)}, bf16[512,256]{1,0:T(8,128)(2,1)S(1)}, u32[]{:S(2)}, u32[]{:S(2)}) collective-permute-start(bf16[512,256]{1,0:T(8,128)(2,1)S(1)} %collective-permute-done.7.refs_1_), channel_id=1, source_target_pairs={{0,4},{4,0},{8,12},{12,8},{16,20},{20,16},{24,28},{28,24},{1,5},{5... | collective-permute-start | bytes 786440 | tf_op jit(solution)/shard_map/ppermute | solution.py:303
  24.2 1.4 %collective-permute-start.10 = (bf16[304,256]{1,0:T(8,128)(2,1)S(1)}, bf16[304,256]{1,0:T(8,128)(2,1)S(1)}, u32[]{:S(2)}, u32[]{:S(2)}) collective-permute-start(bf16[304,256]{1,0:T(8,128)(2,1)S(1)} %get-tuple-element.49), channel_id=1, source_target_pairs={{0,4},{4,0},{8,12},{12,8},{16,20},{20,16},{24,28},{28,24},{1,5},{5... | collective-permute-start | bytes 466952 | tf_op jit(solution)/shard_map/ppermute | solution.py:303
  24.9 4.6 %collective-permute-start.9 = (bf16[304,256]{1,0:T(8,128)(2,1)S(1)}, bf16[304,256]{1,0:T(8,128)(2,1)S(1)}, u32[]{:S(2)}, u32[]{:S(2)}) collective-permute-start(bf16[304,256]{1,0:T(8,128)(2,1)S(1)} %get-tuple-element.45), channel_id=1, source_target_pairs={{0,4},{4,0},{8,12},{12,8},{16,20},{20,16},{24,28},{28,24},{1,5},{5... | collective-permute-start | bytes 466952 | tf_op jit(solution)/shard_map/ppermute | solution.py:303
  25.9 5.4 %collective-permute-start.11 = (bf16[8,4096]{1,0:T(8,128)(2,1)S(1)}, bf16[8,4096]{1,0:T(8,128)(2,1)S(1)}, u32[]{:S(2)}, u32[]{:S(2)}) collective-permute-start(bf16[8,4096]{1,0:T(8,128)(2,1)S(1)} %probe_sides.1.refs_0_), channel_id=1, source_target_pairs={{0,24},{4,28},{8,16},{12,20},{16,8},{20,12},{24,0},{28,4},{1,25},{... | collective-permute-start | bytes 196616 | tf_op jit(solution)/shard_map/ppermute | solution.py:303
  28.8 4.3 %collective-permute-start.12 = (bf16[8,4096]{1,0:T(8,128)(2,1)S(1)}, bf16[8,4096]{1,0:T(8,128)(2,1)S(1)}, u32[]{:S(2)}, u32[]{:S(2)}) collective-permute-start(bf16[8,4096]{1,0:T(8,128)(2,1)S(1)} %probe_sides.1.refs_0_), channel_id=1, source_target_pairs={{0,16},{1,9},{2,18},{3,11},{4,12},{5,21},{6,14},{7,23},{8,24},{9,1... | collective-permute-start | bytes 196616 | tf_op jit(solution)/shard_map/ppermute | solution.py:320
  29.3 4.3 %collective-permute-start.13 = (bf16[8,4096]{1,0:T(8,128)(2,1)S(1)}, bf16[8,4096]{1,0:T(8,128)(2,1)S(1)}, u32[]{:S(2)}, u32[]{:S(2)}) collective-permute-start(bf16[8,4096]{1,0:T(8,128)(2,1)S(1)} %probe_sides.1.refs_0_), channel_id=1, source_target_pairs={{0,8},{1,17},{2,10},{3,19},{4,20},{5,13},{6,22},{7,15},{8,0},{9,25... | collective-permute-start | bytes 196616 | tf_op jit(solution)/shard_map/ppermute | solution.py:320
  29.7 4.3 %collective-permute-start.15 = (f32[64,256]{1,0:T(8,128)S(1)}, f32[64,256]{1,0:T(8,128)S(1)}, u32[]{:S(2)}, u32[]{:S(2)}) collective-permute-start(f32[64,256]{1,0:T(8,128)S(1)} %get-tuple-element.59), channel_id=1, source_target_pairs={{0,4},{4,0},{8,12},{12,8},{16,20},{20,16},{24,28},{28,24},{1,5},{5... | collective-permute-start | bytes 196616 | tf_op jit(solution)/shard_map/ppermute | solution.py:303
  33.9 1.2 %collective-permute-start.14 = (f32[12,32]{1,0:T(8,128)S(1)}, f32[12,32]{1,0:T(8,128)S(1)}, u32[]{:S(2)}, u32[]{:S(2)}) collective-permute-start(f32[12,32]{1,0:T(8,128)S(1)} %get-tuple-element.57), channel_id=1, source_target_pairs={{0,4},{4,0},{8,12},{12,8},{16,20},{20,16},{24,28},{28,24},{1,5},{5... | collective-permute-start | bytes 4616 | tf_op jit(solution)/shard_map/ppermute | solution.py:303
